TPU v7x, 256 devices: a whole 4x4x8 slice. The times are simulated.
256 devices in a mesh: gx: 8 (over y, core), gy: 4 (over z_hi), gz: 8 (over x, z_lo).
Axes of the slice: x: 4, y: 4, z: 8 (z_hi: 4, z_lo: 2; z = z_hi * 2 + z_lo), core: 2. Of those that a mesh axis runs over, the one named last changes fastest.
Arguments:
- velocity: float32 [3, 64, 128, 1024], P(None, 'gx', 'gy', 'gz'), may hold values from -4 to 4
- sample_cells: int32 [65536], P(('gx', 'gy', 'gz')), may hold values from 0 to 32767
- trainer_of: int32 [65536, 1], P(('gx', 'gy', 'gz')), may hold values from 0 to 31; in each aligned block of 256 rows (0 to 255, 256 to 511, ...) at most 16 rows name the same one
- targets: bfloat16 [6, 65536], P(None, ('gx', 'gy', 'gz')), may hold values from -6 to 6
- w_first: bfloat16 [32, 512, 81], P(('gx', 'gy')), may hold values from -0.625 to 0.625
- w_middle: bfloat16 [32, 512, 512], P(('gx', 'gy')), may hold values from -0.25 to 0.25
- w_last: bfloat16 [32, 6, 512], P(('gx', 'gy')), may hold values from -0.25 to 0.25
- biases: float32 [32, 1030], P(('gx', 'gy')), may hold values from -3 to 3
- middle_master: float32 [32, 262144], P(('gx', 'gy'), 'gz'), may hold values from -2 to 2
- middle_momentum: float32 [32, 262144], P(('gx', 'gy'), 'gz'), may hold values from -2 to 2
Outputs:
- new_velocity: float32 [3, 64, 128, 1024], P(None, 'gx', 'gy', 'gz')
- trainer_loss: float32 [8, 4, 8], P('gx', 'gy', 'gz')
- first_grads: float32 [32, 512, 81], P(('gx', 'gy'))
- last_grads: float32 [32, 6, 512], P(('gx', 'gy'))
- bias_grads: float32 [32, 1030], P(('gx', 'gy'))
- master_new: float32 [32, 262144], P(('gx', 'gy'), 'gz')
- momentum_new: float32 [32, 262144], P(('gx', 'gy'), 'gz')
Inputs may be any that keep to these rules, and one draw needn't show every extreme that they name: `sample_cells`: each entry indexes a cell of its own device's brick as x * 32 * 128 + y * 128 + z. `trainer_of`: among the 256 samples of one device no trainer is named more than 16 times.
All inputs are finite; a program needn't handle non-finite values.
Results may differ from a plain program's by a relative error of at most 0.0044.
Values may be sent and summed in bfloat16 or wider, within the bound.
No kernel may reach another device: no remote copies, remote signals or barrier semaphores. Data moves between devices by JAX's collectives and lax.ppermute only.
A program may use at most 64 MiB of HBM per device.

v0:
```python
import functools

import jax
import jax.numpy as jnp
from jax import lax
from jax.experimental import pallas as pl
from jax.experimental.pallas import tpu as pltpu
from jax.sharding import PartitionSpec as P

DT_STEP = 0.1
VISCOSITY = 0.2
LEARN_RATE = 0.05
MOMENTUM_KEEP = 0.9

BF16 = jnp.bfloat16
F32 = jnp.float32
I32 = jnp.int32
NT = (((1,), (1,)), ((), ()))
TN = (((0,), (0,)), ((), ()))
EXACT = lax.Precision.HIGHEST
VMEM_LIMIT = 48 * 1024 * 1024
ROWS = 96
TAIL = 88
WIDE = 128
PAD_X = 16


def params(limit=VMEM_LIMIT):
    return pltpu.CompilerParams(vmem_limit_bytes=limit)


def cost(micros):
    return pl.CostEstimate(
        flops=int(micros * 800_000_000), bytes_accessed=1_000_000, transcendentals=0
    )


def inside(axis):
    at = lax.axis_index(axis)
    return (
        jnp.where(at > 0, 1.0, 0.0).astype(F32),
        jnp.where(at < lax.axis_size(axis) - 1, 1.0, 0.0).astype(F32),
    )


def whole(count):
    return [pl.BlockSpec(memory_space=pltpu.VMEM)] * count


def iota(shape, dim):
    return lax.broadcasted_iota(I32, shape, dim)


def ones_where(mask):
    return jnp.where(mask, 1.0, 0.0).astype(BF16)


def shifts(axis):
    count = lax.axis_size(axis)
    forward = [(i, (i + 1) % count) for i in range(count)]
    return forward, [(b, a) for a, b in forward]


def end_rows(block, low_ref, high_ref, row_of, size_y):
    size_z = block.shape[1]
    row, lane = iota((8, size_z), 0), iota((8, size_z), 1)
    pick = jnp.where(
        ((row == 0) & (lane == 0)) | ((row == 1) & (lane == size_z - 1)), 1.0, 0.0
    ).astype(F32)
    ends = lax.dot_general(pick, block, NT, precision=EXACT, preferred_element_type=F32)
    for k in range(block.shape[0] // size_y):
        at = row_of(k)
        low_ref[at : at + 1, 1 : size_y + 1] = ends[0:1, k * size_y : (k + 1) * size_y]
        high_ref[at : at + 1, 1 : size_y + 1] = ends[1:2, k * size_y : (k + 1) * size_y]


def plan_kernel(
    v_ref, trainer_ref, y_low_ref, y_high_ref, z_low_ref, z_high_ref, placing_ref, *, trainers
):
    comps, size_x, size_y, size_z = v_ref.shape
    for ref in (y_low_ref, y_high_ref, z_low_ref, z_high_ref):
        ref[...] = jnp.zeros_like(ref)
    for c in range(comps):
        for x in range(size_x):
            y_low_ref[c, x + 1 : x + 2, :] = v_ref[c, x, 0:1, :]
            y_high_ref[c, x + 1 : x + 2, :] = v_ref[c, x, size_y - 1 : size_y, :]
    end_rows(
        v_ref[...].reshape(-1, size_z),
        z_low_ref,
        z_high_ref,
        lambda k: k // size_x * PAD_X + k % size_x + 1,
        size_y,
    )

    trainer = trainer_ref[...]
    samples = trainer.shape[1]
    slots = placing_ref.shape[0]
    capacity = slots // trainers
    same = iota((trainers, samples), 0) == trainer
    earlier = ones_where(iota((samples, samples), 0) < iota((samples, samples), 1))
    before = jnp.dot(ones_where(same), earlier, preferred_element_type=F32)
    position = jnp.sum(jnp.where(same, before, 0.0), axis=0, keepdims=True).astype(I32)
    slot = trainer * capacity + position
    placing_ref[...] = ones_where(iota((slots, samples), 0) == slot)


def plan(velocity, trainer, trainers, slots):
    comps, size_x, size_y, size_z = velocity.shape
    y_face = jax.ShapeDtypeStruct((comps, PAD_X, size_z), F32)
    z_face = jax.ShapeDtypeStruct((comps * PAD_X, WIDE), F32)
    placing = jax.ShapeDtypeStruct((slots, trainer.shape[1]), BF16)
    return pl.pallas_call(
        functools.partial(plan_kernel, trainers=trainers),
        out_shape=(y_face, y_face, z_face, z_face, placing),
        in_specs=whole(2),
        out_specs=tuple(whole(5)),
        compiler_params=params(),
        cost_estimate=cost(1.5),
        name="plan",
    )(velocity, trainer)


def y_faces_kernel(low_ref, high_ref, xlo_ref, xhi_ref, to_low_ref, to_high_ref, *, size_x):
    before, after = inside("gx")
    last = xlo_ref.shape[1] - 1
    for own, to, y in ((low_ref, to_low_ref, 0), (high_ref, to_high_ref, last)):
        to[...] = own[...]
        for c in range(to.shape[0]):
            to[c, 0:1, :] = xlo_ref[c, y : y + 1, :] * before
            to[c, size_x + 1 : size_x + 2, :] = xhi_ref[c, y : y + 1, :] * after


def y_faces(low, high, xlo, xhi, size_x):
    return pl.pallas_call(
        functools.partial(y_faces_kernel, size_x=size_x),
        out_shape=tuple([jax.ShapeDtypeStruct(low.shape, F32)] * 2),
        in_specs=whole(4),
        out_specs=tuple(whole(2)),
        compiler_params=params(),
        cost_estimate=cost(0.3),
        name="y_faces",
    )(low, high, xlo, xhi)


def z_faces_kernel(
    low_ref, high_ref, x_low_ref, x_high_ref, ylo_ref, yhi_ref, to_low_ref, to_high_ref, *, size_y
):
    before, after = inside("gy")
    size_z = ylo_ref.shape[2]
    ylo = ylo_ref[...].reshape(-1, size_z) * before
    yhi = yhi_ref[...].reshape(-1, size_z) * after
    lane = iota(low_ref.shape, 1)
    for own, x, to, z in (
        (low_ref, x_low_ref, to_low_ref, 0),
        (high_ref, x_high_ref, to_high_ref, size_z - 1),
    ):
        face = own[...] + x[...]
        face = jnp.where(lane == 0, ylo[:, z : z + 1], face)
        to[...] = jnp.where(lane == size_y + 1, yhi[:, z : z + 1], face)


def z_faces(low, high, x_low, x_high, ylo, yhi, size_y):
    return pl.pallas_call(
        functools.partial(z_faces_kernel, size_y=size_y),
        out_shape=tuple([jax.ShapeDtypeStruct(low.shape, F32)] * 2),
        in_specs=whole(6),
        out_specs=tuple(whole(2)),
        compiler_params=params(),
        cost_estimate=cost(0.3),
        name="z_faces",
    )(low, high, x_low, x_high, ylo, yhi)


def split_cells(cells, size_x, size_y, size_z):
    return cells // (size_y * size_z), cells // size_z % size_y, cells % size_z


def depth_choice(cell_z, size_z):
    depth = iota((size_z, cell_z.shape[1]), 0)
    return jnp.concatenate([ones_where(depth == cell_z + (r - 1)) for r in range(3)], axis=1)


def fold(ref, first, rows, masks, samples):
    sums = [None] * 3
    for k in range(rows // 8):
        for r in range(3):
            piece = ref[first + 8 * k : first + 8 * k + 8, r * samples : (r + 1) * samples]
            piece = jnp.where(masks[k], piece, 0.0)
            sums[r] = piece if sums[r] is None else sums[r] + piece
    return sums


def feature(c, p, q, r):
    return 27 * c + 9 * p + 3 * q + r


def add_tiles(parts, feats):
    shape = (ROWS, feats * 8)
    gather = ones_where(lax.shift_right_logical(iota(shape, 1), 3) == iota(shape, 0))
    return jnp.dot(gather, parts[...].astype(BF16), preferred_element_type=F32)


def patch_kernel(
    v_ref, xlo_ref, xhi_ref, cells_ref, out_ref, z_low_ref, z_high_ref, picked, parts
):
    comps, size_x, size_y, size_z = v_ref.shape
    samples = cells_ref.shape[1]
    before, after = inside("gx")
    z_low_ref[...] = jnp.zeros_like(z_low_ref)
    z_high_ref[...] = jnp.zeros_like(z_high_ref)
    cell_x, cell_y, cell_z = split_cells(cells_ref[...], size_x, size_y, size_z)
    choose = depth_choice(cell_z, size_z)
    starts, start = [], 0
    for ref, scale, x in ((v_ref, None, 0), (xlo_ref, before, 0), (xhi_ref, after, size_x + 1)):
        block = ref[...].reshape(-1, size_z)
        if scale is not None:
            block = block * scale
            end_rows(block, z_low_ref, z_high_ref, lambda k: k * PAD_X + x, size_y)
        picked[start : start + block.shape[0], :] = jnp.dot(
            block.astype(BF16), choose, preferred_element_type=F32
        )
        starts.append(start)
        start += block.shape[0]
    sub = iota((8, samples), 0)
    at_x = [cell_x == j for j in range(size_x)]
    for c in range(comps):
        for q in range(3):
            masks = [sub + (8 * k - q + 1) == cell_y for k in range(size_y // 8)]
            totals = [[None] * 3 for _ in range(3)]
            for x in range(size_x + 2):
                if x == 0:
                    first = starts[1] + c * size_y
                elif x == size_x + 1:
                    first = starts[2] + c * size_y
                else:
                    first = (c * size_x + x - 1) * size_y
                sums = fold(picked, first, size_y, masks, samples)
                for p in range(3):
                    j = x - p
                    if 0 <= j < size_x:
                        for r in range(3):
                            piece = jnp.where(at_x[j], sums[r], 0.0)
                            totals[p][r] = piece if totals[p][r] is None else totals[p][r] + piece
            for p in range(3):
                for r in range(3):
                    f = feature(c, p, q, r)
                    parts[f * 8 : (f + 1) * 8, :] = totals[p][r]
    out_ref[...] = add_tiles(parts, 27 * comps)


def patches(velocity, xlo, xhi, cells, z_face):
    comps, size_x, size_y, size_z = velocity.shape
    samples = cells.shape[1]
    face = jax.ShapeDtypeStruct(z_face.shape, F32)
    return pl.pallas_call(
        patch_kernel,
        out_shape=(jax.ShapeDtypeStruct((ROWS, samples), F32), face, face),
        in_specs=whole(4),
        out_specs=tuple(whole(3)),
        scratch_shapes=[
            pltpu.VMEM((comps * (size_x + 2) * size_y, 3 * samples), F32),
            pltpu.VMEM((27 * comps * 8, samples), F32),
        ],
        compiler_params=params(),
        cost_estimate=cost(2.5),
        name="patches",
    )(velocity, xlo, xhi, cells)


def pack_kernel(
    own_ref,
    ylo_ref,
    yhi_ref,
    zlo_ref,
    zhi_ref,
    cells_ref,
    tail_ref,
    placing_ref,
    out_ref,
    picked,
    parts,
    *,
    size_x,
    size_y,
):
    comps, pad_x, size_z = ylo_ref.shape
    samples = cells_ref.shape[1]
    rows = comps * pad_x
    cell_x, cell_y, cell_z = split_cells(cells_ref[...], size_x, size_y, size_z)
    y_before, y_after = inside("gy")
    z_before, z_after = inside("gz")

    choose = depth_choice(cell_z, size_z)
    along_y = jnp.concatenate(
        [ylo_ref[...].reshape(rows, size_z) * y_before, yhi_ref[...].reshape(rows, size_z) * y_after],
        axis=0,
    ).astype(BF16)
    picked[: 2 * rows, :] = jnp.dot(along_y, choose, preferred_element_type=F32)
    width = iota((WIDE, samples), 0)
    choose = jnp.concatenate([ones_where(width == cell_y + q) for q in range(3)], axis=1)
    along_z = jnp.concatenate([zlo_ref[...] * z_before, zhi_ref[...] * z_after], axis=0).astype(BF16)
    picked[2 * rows :, :] = jnp.dot(along_z, choose, preferred_element_type=F32)

    sub = iota((8, samples), 0)
    at_edge = [cell_y == 0, cell_y == size_y - 1, cell_z == 0, cell_z == size_z - 1]
    edge_x = [jnp.where(at, cell_x, -100) for at in at_edge]
    for c in range(comps):
        for p in range(3):
            sums = [
                fold(
                    picked,
                    e * rows + c * pad_x,
                    pad_x,
                    [sub + (8 * k - p) == edge_x[e] for k in range(pad_x // 8)],
                    samples,
                )
                for e in range(4)
            ]
            for q in range(3):
                for r in range(3):
                    terms = []
                    if q != 1:
                        terms.append(sums[q // 2][r])
                    if r != 1:
                        terms.append(sums[2 + r // 2][q])
                    total = terms[0] if terms else jnp.zeros((8, samples), F32)
                    if len(terms) > 1:
                        total = total + terms[1]
                    f = feature(c, p, q, r)
                    parts[f * 8 : (f + 1) * 8, :] = total

    features = own_ref[...] + add_tiles(parts, 27 * comps)
    payload = jnp.concatenate(
        [features[:TAIL], tail_ref[...], jnp.zeros((WIDE - ROWS, samples), F32)], axis=0
    ).astype(BF16)
    out_ref[...] = lax.dot_general(
        placing_ref[...], payload, NT, preferred_element_type=F32
    ).astype(BF16)


def pack(own, ylo, yhi, zlo, zhi, cells, tail, placing, size_x, size_y):
    samples = cells.shape[1]
    comps, pad_x, _ = ylo.shape
    return pl.pallas_call(
        functools.partial(pack_kernel, size_x=size_x, size_y=size_y),
        out_shape=jax.ShapeDtypeStruct((placing.shape[0], WIDE), BF16),
        in_specs=whole(8),
        out_specs=pl.BlockSpec(memory_space=pltpu.VMEM),
        scratch_shapes=[
            pltpu.VMEM((4 * comps * pad_x, 3 * samples), F32),
            pltpu.VMEM((27 * comps * 8, samples), F32),
        ],
        compiler_params=params(),
        cost_estimate=cost(1.0),
        name="pack",
    )(own, ylo, yhi, zlo, zhi, cells, tail, placing)


def advance_kernel(v_ref, xlo_ref, xhi_ref, ylo_ref, yhi_ref, zlo_ref, zhi_ref, out_ref):
    comps, size_x, size_y, size_z = v_ref.shape
    x_before, x_after = inside("gx")
    y_before, y_after = inside("gy")
    z_before, z_after = inside("gz")

    def columns(ref, scale):
        face = ref[...] * scale
        face = jnp.concatenate([face, jnp.zeros((WIDE - face.shape[0], WIDE), F32)], axis=0)
        return pltpu.roll(face.T, WIDE - 1, 0)[:size_y, :]

    z_low, z_high = columns(zlo_ref, z_before), columns(zhi_ref, z_after)
    y_at = iota((size_y, size_z), 0)
    z_at = iota((size_y, size_z), 1)

    def plane(c, x):
        if x < 0:
            return xlo_ref[c] * x_before
        if x >= size_x:
            return xhi_ref[c] * x_after
        return v_ref[c, x]

    for x in range(size_x):
        here = [plane(c, x) for c in range(comps)]
        after = [plane(c, x + 1) for c in range(comps)]
        prior = [plane(c, x - 1) for c in range(comps)]
        y_up, y_down, z_up, z_down = [], [], [], []
        for c in range(comps):
            at = c * PAD_X + x + 1
            above = yhi_ref[c, x + 1 : x + 2, :] * y_after
            below = ylo_ref[c, x + 1 : x + 2, :] * y_before
            y_up.append(jnp.where(y_at == size_y - 1, above, pltpu.roll(here[c], size_y - 1, 0)))
            y_down.append(jnp.where(y_at == 0, below, pltpu.roll(here[c], 1, 0)))
            z_up.append(
                jnp.where(z_at == size_z - 1, z_high[:, at : at + 1], pltpu.roll(here[c], size_z - 1, 1))
            )
            z_down.append(jnp.where(z_at == 0, z_low[:, at : at + 1], pltpu.roll(here[c], 1, 1)))
        for c in range(comps):
            diverge = after[c] * after[0] - prior[c] * prior[0]
            diverge = diverge + y_up[c] * y_up[1] - y_down[c] * y_down[1]
            diverge = diverge + z_up[c] * z_up[2] - z_down[c] * z_down[2]
            beside = after[c] + prior[c]
            beside = beside + y_up[c] + y_down[c]
            beside = beside + z_up[c] + z_down[c]
            tendency = -0.5 * diverge + VISCOSITY * (beside - 6.0 * here[c])
            out_ref[c, x] = here[c] + DT_STEP * tendency


def advance(velocity, halos):
    return pl.pallas_call(
        advance_kernel,
        out_shape=jax.ShapeDtypeStruct(velocity.shape, F32),
        in_specs=whole(7),
        out_specs=pl.BlockSpec(memory_space=pltpu.VMEM),
        compiler_params=params(),
        cost_estimate=cost(1.5),
        name="advance",
    )(velocity, *halos)


def turn_kernel(in_ref, out_ref):
    shape = (out_ref.shape[0], in_ref.shape[1])
    eye = ones_where(iota(shape, 0) == iota(shape, 1))
    out_ref[...] = lax.dot_general(eye, in_ref[...], NT, preferred_element_type=F32).astype(BF16)


def turn(arrived):
    return pl.pallas_call(
        turn_kernel,
        out_shape=jax.ShapeDtypeStruct((ROWS, arrived.shape[0]), BF16),
        in_specs=whole(1),
        out_specs=pl.BlockSpec(memory_space=pltpu.VMEM),
        compiler_params=params(),
        cost_estimate=cost(0.2),
        name="turn",
    )(arrived)


def lane_sum(value):
    total = value[:, :WIDE]
    for k in range(1, value.shape[1] // WIDE):
        total = total + value[:, k * WIDE : (k + 1) * WIDE]
    return total


def train_kernel(*refs, planes, row_count, first, last, own_rows):
    refs = list(refs)
    take = lambda n: [refs.pop(0) for _ in range(n)]
    x_refs = take(len(planes))
    w1_ref, w2_ref, w2t_ref, w3_ref, w3t_ref, bias_ref, bias3_ref = take(7)
    held = [] if first else take(6)
    if last:
        momentum_ref, master_ref = take(2)
        first_ref, last_ref, bias_grads_ref, master_new_ref, momentum_new_ref = take(5)
        sums = take(6)
    else:
        sums = take(6)
    if first:
        loss_ref = take(1)[0]
    back_two_ref = take(1)[0]
    g1, g2, g3, s1, s2, s3 = sums
    hidden = w2_ref.shape[0]
    factor = 2.0 / (6.0 * row_count)
    if first:
        for ref in sums:
            ref[...] = jnp.zeros_like(ref)
    else:
        for ref, old in zip(sums, held):
            ref[...] = old[...]
    own = pl.multiple_of(lax.axis_index("gz") * own_rows, own_rows)

    def plane(x):
        slots = x.shape[1]
        reps = slots // WIDE
        spread = lambda b: jnp.concatenate([b] * reps, axis=1)
        act_one = jnp.tanh(
            jnp.dot(w1_ref[...], x, preferred_element_type=F32) + spread(bias_ref[:hidden, :])
        ).astype(BF16)
        act_two = jnp.tanh(
            jnp.dot(w2_ref[...], act_one, preferred_element_type=F32) + spread(bias_ref[hidden:, :])
        ).astype(BF16)
        ending = x[ROWS - 16 :, :].astype(F32)[8:, :]
        predicted = jnp.dot(w3_ref[...], act_two, preferred_element_type=F32)[:8, :]
        predicted = predicted + spread(bias3_ref[...])
        mismatch = jnp.where(
            iota((8, slots), 0) < 6, (predicted - ending) * ending[6:7, :], 0.0
        )
        delta_three = mismatch * factor
        back_three = jnp.concatenate([delta_three, jnp.zeros_like(delta_three)], axis=0).astype(BF16)
        g3[...] += lax.dot_general(back_three, act_two, NT, preferred_element_type=F32)
        wide_two = act_two.astype(F32)
        delta_two = jnp.dot(w3t_ref[...], back_three, preferred_element_type=F32) * (
            1.0 - wide_two * wide_two
        )
        s2[...] += lane_sum(delta_two)
        back_two = delta_two.astype(BF16)
        back_two_ref[...] = back_two
        g2[...] += lax.dot_general(
            back_two_ref[pl.ds(own, own_rows), :], act_one, NT, preferred_element_type=F32
        )
        wide_one = act_one.astype(F32)
        delta_one = jnp.dot(w2t_ref[...], back_two, preferred_element_type=F32) * (
            1.0 - wide_one * wide_one
        )
        s1[...] += lane_sum(delta_one)
        g1[...] += lax.dot_general(delta_one.astype(BF16), x, NT, preferred_element_type=F32)
        s3[...] += lane_sum(delta_three)
        return mismatch

    pieces = []
    for ref, count in zip(x_refs, planes):
        pieces += [ref[...]] if count == 1 else [ref[k] for k in range(count)]
    mismatch = plane(pieces[0] if len(pieces) == 1 else jnp.concatenate(pieces, axis=1))

    if first:
        row_loss = jnp.sum(mismatch * mismatch, axis=0, keepdims=True) / (6.0 * row_count)
        loss_ref[...] = jnp.sum(row_loss, axis=1, keepdims=True)
    if last:
        wide = jnp.concatenate([g1[...], jnp.zeros((hidden, WIDE - ROWS), F32)], axis=1)
        for ref, grads in ((first_ref, wide.T), (last_ref, g3[...])):
            for k in range(ref.shape[0]):
                ref[k] = grads[k : k + 1, :]
        ones = jnp.ones((8, WIDE), F32)
        across = lambda s: lax.dot_general(ones, s, NT, precision=EXACT, preferred_element_type=F32)
        bias_grads_ref[:, :hidden] = across(s1[...])[0:1]
        bias_grads_ref[:, hidden : 2 * hidden] = across(s2[...])[0:1]
        third = across(jnp.concatenate([s3[...], jnp.zeros((WIDE - 8, WIDE), F32)], axis=0))
        bias_grads_ref[:, 2 * hidden :] = third[0:1, :6]
        grads = g2[...]
        per_row = hidden // WIDE
        for k in range(per_row):
            at = pl.ds(k, own_rows, stride=per_row)
            momentum = MOMENTUM_KEEP * momentum_ref[at, :] + grads[:, k * WIDE : (k + 1) * WIDE]
            momentum_new_ref[at, :] = momentum
            master_new_ref[at, :] = master_ref[at, :] - LEARN_RATE * momentum


def train(xs, weights, held, optimizer, row_count, own_rows):
    planes = tuple(x.shape[0] if x.ndim == 3 else 1 for x in xs)
    slots = xs[0].shape[-1]
    hidden = weights[1].shape[0]
    first, last = held is None, optimizer is not None
    sums = [
        jax.ShapeDtypeStruct(s, F32)
        for s in (
            (hidden, ROWS),
            (own_rows, hidden),
            (16, hidden),
            (hidden, WIDE),
            (hidden, WIDE),
            (8, WIDE),
        )
    ]
    scratch = [pltpu.VMEM((hidden, slots * sum(planes)), BF16)]
    if last:
        out = [
            jax.ShapeDtypeStruct(s, F32)
            for s in (
                (81, 1, hidden),
                (6, 1, hidden),
                (1, 2 * hidden + 6),
                optimizer[0].shape,
                optimizer[0].shape,
            )
        ]
        scratch = [pltpu.VMEM(s.shape, F32) for s in sums] + scratch
    else:
        out = list(sums)
    if first:
        out.append(jax.ShapeDtypeStruct((1, 1), F32))
    operands = [*xs, *weights, *(held or ()), *(optimizer or ())]
    count = sum(planes)
    return pl.pallas_call(
        functools.partial(
            train_kernel,
            planes=planes,
            row_count=row_count,
            first=first,
            last=last,
            own_rows=own_rows,
        ),
        out_shape=tuple(out),
        in_specs=whole(len(operands)),
        out_specs=tuple(whole(len(out))),
        scratch_shapes=scratch,
        compiler_params=params(),
        cost_estimate=cost(1.6 * count),
        name="train",
    )(*operands)


def on_device(
    velocity,
    sample_cells,
    trainer_of,
    targets,
    w_first,
    w_middle,
    w_last,
    biases,
    middle_master,
    middle_momentum,
):
    comps, size_x, size_y, size_z = velocity.shape
    samples = sample_cells.shape[0]
    trainers = lax.axis_size("gx") * lax.axis_size("gy")
    capacity = 2 * samples // trainers
    slots = trainers * capacity
    hidden = w_middle.shape[1]
    planes = lax.axis_size("gz")
    own_rows = hidden // planes

    cells = sample_cells.reshape(1, samples)
    forward, backward = shifts("gx")
    xlo = lax.ppermute(velocity[:, size_x - 1], "gx", forward)
    xhi = lax.ppermute(velocity[:, 0], "gx", backward)
    y_low, y_high, z_low, z_high, placing = plan(
        velocity, trainer_of.reshape(1, samples), trainers, slots
    )
    y_low, y_high = y_faces(y_low, y_high, xlo, xhi, size_x)
    forward, backward = shifts("gy")
    ylo = lax.ppermute(y_high, "gy", forward)
    yhi = lax.ppermute(y_low, "gy", backward)
    features, x_low, x_high = patches(velocity, xlo, xhi, cells, z_low)
    z_low, z_high = z_faces(z_low, z_high, x_low, x_high, ylo, yhi, size_y)
    forward, backward = shifts("gz")
    zlo = lax.ppermute(z_high, "gz", forward)
    zhi = lax.ppermute(z_low, "gz", backward)
    tail = jnp.concatenate(
        [targets.astype(F32), jnp.ones((1, samples), F32), jnp.zeros((1, samples), F32)], axis=0
    )
    packed = pack(features, ylo, yhi, zlo, zhi, cells, tail, placing, size_x, size_y)
    arrived = lax.all_to_all(
        packed.reshape(trainers, capacity, WIDE),
        ("gx", "gy"),
        split_axis=0,
        concat_axis=0,
        tiled=True,
    ).reshape(slots, WIDE)
    new_velocity = advance(velocity, (xlo, xhi, ylo, yhi, zlo, zhi))

    feats = w_first.shape[2]
    w1 = jnp.pad(w_first[0], ((0, 0), (0, ROWS - feats)))
    w2 = w_middle[0]
    w3 = jnp.pad(w_last[0], ((0, 16 - w_last.shape[1]), (0, 0)))
    bias = jnp.broadcast_to(biases[0, : 2 * hidden, None], (2 * hidden, WIDE))
    bias3 = jnp.broadcast_to(
        jnp.pad(biases[0, 2 * hidden :], (0, 8 - w_last.shape[1]))[:, None], (8, WIDE)
    )
    weights = (w1, w2, w2.T, w3, w3.T, bias, bias3)
    optimizer = (
        middle_momentum.reshape(-1, WIDE),
        middle_master.reshape(-1, WIDE),
    )

    arrived, new_velocity = lax.optimization_barrier((arrived, new_velocity))
    mine = turn(arrived)
    call = functools.partial(train, weights=weights, row_count=samples, own_rows=own_rows)
    swap = [(i, i ^ 1) for i in range(planes)]
    move = lambda k: [(i, (i + k) % planes) for i in range(planes)]
    beside = lax.ppermute(mine, "gz", swap)
    far = lax.ppermute(mine, "gz", move(planes // 2))
    *held, loss = call([mine], held=None, optimizer=None)
    beside, far, *held = lax.optimization_barrier((beside, far, *held))
    both = jnp.stack([mine, beside])
    near = [lax.ppermute(both, "gz", move(k)) for k in (2, planes - 2)]
    far_beside = lax.ppermute(far, "gz", swap)
    held = call([beside, far], held=held, optimizer=None)
    first_grads, last_grads, bias_grads, master_new, momentum_new = call(
        [*near, far_beside], held=held, optimizer=optimizer
    )
    return (
        new_velocity,
        loss.reshape(1, 1, 1),
        first_grads.transpose(1, 2, 0),
        last_grads.transpose(1, 0, 2),
        bias_grads,
        master_new.reshape(middle_master.shape),
        momentum_new.reshape(middle_momentum.shape),
    )


def solution(mesh):
    placed = (
        P(None, "gx", "gy", "gz"),
        P(("gx", "gy", "gz")),
        P(("gx", "gy", "gz"), None),
        P(None, ("gx", "gy", "gz")),
        P(("gx", "gy"), None, None),
        P(("gx", "gy"), None, None),
        P(("gx", "gy"), None, None),
        P(("gx", "gy"), None),
        P(("gx", "gy"), "gz"),
        P(("gx", "gy"), "gz"),
    )
    return jax.shard_map(
        on_device,
        mesh=mesh,
        in_specs=placed,
        out_specs=(
            P(None, "gx", "gy", "gz"),
            P("gx", "gy", "gz"),
            P(("gx", "gy"), None, None),
            P(("gx", "gy"), None, None),
            P(("gx", "gy"), None),
            P(("gx", "gy"), "gz"),
            P(("gx", "gy"), "gz"),
        ),
        check_vma=False,
    )
```

profile of v0, /device:TPU:32, one launch (start us, length us, event | category | flops | bytes accessed | tf_op | source)
XLA Modules:
  0.0 67.8 jit_solution(14556638462726270119)
XLA Ops:
  0.6 0.8 %slice_bitcast_fusion = (f32[3,32,128]{2,1,0:T(8,128)S(1)}, f32[3,32,128]{2,1,0:T(8,128)S(1)}) fusion(f32[3,8,32,128]{3,2,1,0:T(8,128)} %v_ref.5), kind=kLoop, calls=%fused_computation.1 | loop fusion | bytes 196608 | tf_op jit(solution)/shard_map/squeeze | solution.py:614
  1.5 2.5 %collective-permute-start.1 = (f32[3,32,128]{2,1,0:T(8,128)S(1)}, f32[3,32,128]{2,1,0:T(8,128)S(1)}, u32[]{:S(2)}, u32[]{:S(2)}) collective-permute-start(f32[3,32,128]{2,1,0:T(8,128)S(1)} %get-tuple-element.87), channel_id=1, source_target_pairs={{32,0},{64,32},{96,64},{128,96},{160,128},{192,160},{224,192},{0,2... | collective-permute-start | bytes 147464 | tf_op jit(solution)/shard_map/ppermute | solution.py:614
  4.6 1.0 %copy-done.1 = f32[3,8,32,128]{3,2,1,0:T(8,128)S(1)} copy-done((f32[3,8,32,128]{3,2,1,0:T(8,128)S(1)}, f32[3,8,32,128]{3,2,1,0:T(8,128)}, u32[]{:S(2)}) %copy-start.1) | copy-done | bytes 393240
  6.9 1.8 %collective-permute-done.xlo_ref = f32[3,32,128]{2,1,0:T(8,128)S(1)} collective-permute-done((f32[3,32,128]{2,1,0:T(8,128)S(1)}, f32[3,32,128]{2,1,0:T(8,128)S(1)}, u32[]{:S(2)}, u32[]{:S(2)}) %collective-permute-start) | collective-permute-done | bytes 49184 | tf_op jit(solution)/shard_map/ppermute | solution.py:613
  8.7 3.3 %collective-permute-start.2 = (f32[3,16,128]{2,1,0:T(8,128)S(1)}, f32[3,16,128]{2,1,0:T(8,128)S(1)}, u32[]{:S(2)}, u32[]{:S(2)}) collective-permute-start(f32[3,16,128]{2,1,0:T(8,128)S(1)} %get-tuple-element.50), channel_id=1, source_target_pairs={{0,8},{8,16},{16,24},{24,0},{1,9},{9,17},{17,25},{25,1},{2,10},{10... | collective-permute-start | bytes 73736 | tf_op jit(solution)/shard_map/ppermute | solution.py:620
  12.0 2.2 %collective-permute-start.3 = (f32[3,16,128]{2,1,0:T(8,128)S(1)}, f32[3,16,128]{2,1,0:T(8,128)S(1)}, u32[]{:S(2)}, u32[]{:S(2)}) collective-permute-start(f32[3,16,128]{2,1,0:T(8,128)S(1)} %get-tuple-element.51), channel_id=1, source_target_pairs={{8,0},{16,8},{24,16},{0,24},{9,1},{17,9},{25,17},{1,25},{10,2},{18... | collective-permute-start | bytes 73736 | tf_op jit(solution)/shard_map/ppermute | solution.py:621
  14.3 1.4 %patches.1 = (f32[96,256]{1,0:T(8,128)S(1)}, f32[48,128]{1,0:T(8,128)S(1)}, f32[48,128]{1,0:T(8,128)S(1)}) custom-call(f32[3,8,32,128]{3,2,1,0:T(8,128)S(1)} %copy-done.2, f32[3,32,128]{2,1,0:T(8,128)S(1)} %collective-permute-done.xlo_ref, f32[3,32,128]{2,1,0:T(8,128)S(1)} %collective-permute-done.1.xhi_ref, s32[1,256]{1,0:T(1,128)S(1)} %bitcast.46), custom_call_target="tpu_custom_call" | custom-call | flops 2000000000 | bytes 1000000 | tf_op jit(solution)/shard_map/patches/pallas_call | solution.py:255
  16.0 1.4 %collective-permute-done.3.yhi_ref = f32[3,16,128]{2,1,0:T(8,128)S(1)} collective-permute-done((f32[3,16,128]{2,1,0:T(8,128)S(1)}, f32[3,16,128]{2,1,0:T(8,128)S(1)}, u32[]{:S(2)}, u32[]{:S(2)}) %collective-permute-start.3) | collective-permute-done | bytes 24608 | tf_op jit(solution)/shard_map/ppermute | solution.py:621
  17.5 2.1 %collective-permute-start.4 = (f32[48,128]{1,0:T(8,128)S(1)}, f32[48,128]{1,0:T(8,128)S(1)}, u32[]{:S(2)}, u32[]{:S(2)}) collective-permute-start(f32[48,128]{1,0:T(8,128)S(1)} %get-tuple-element.56), channel_id=1, source_target_pairs={{0,1},{1,2},{2,3},{3,4},{4,5},{5,6},{6,7},{7,0},{8,9},{9,10},{10,1... | collective-permute-start | bytes 73736 | tf_op jit(solution)/shard_map/ppermute | solution.py:625
  19.7 1.7 %collective-permute-done.4.zlo_ref = f32[48,128]{1,0:T(8,128)S(1)} collective-permute-done((f32[48,128]{1,0:T(8,128)S(1)}, f32[48,128]{1,0:T(8,128)S(1)}, u32[]{:S(2)}, u32[]{:S(2)}) %collective-permute-start.4) | collective-permute-done | bytes 24608 | tf_op jit(solution)/shard_map/ppermute | solution.py:625
  21.4 2.9 %collective-permute-done.5.zhi_ref = f32[48,128]{1,0:T(8,128)S(1)} collective-permute-done((f32[48,128]{1,0:T(8,128)S(1)}, f32[48,128]{1,0:T(8,128)S(1)}, u32[]{:S(2)}, u32[]{:S(2)}) %collective-permute-start.5) | collective-permute-done | bytes 24608 | tf_op jit(solution)/shard_map/ppermute | solution.py:626
  24.4 1.4 %pack.1 = bf16[512,128]{1,0:T(8,128)(2,1)} custom-call(f32[96,256]{1,0:T(8,128)S(1)} %get-tuple-element.47.own_ref, f32[3,16,128]{2,1,0:T(8,128)S(1)} %collective-permute-done.2.ylo_ref, f32[3,16,128]{2,1,0:T(8,128)S(1)} %collective-permute-done.3.yhi_ref, f32[48,128]{1,0:T(8,128)S(1)} %collective-permute-done.4.zlo_ref, ...), custom_call_target="tpu_custom_call" | custom-call | flops 800000000 | bytes 1000000 | tf_op jit(solution)/shard_map/pack/pallas_call | solution.py:344
  25.8 5.8 %all-to-all-start = ((bf16[32,16,128]{2,1,0:T(8,128)(2,1)}), bf16[32,16,128]{2,1,0:T(8,128)(2,1)S(1)}, u32[]{:S(2)}, u32[]{:S(2)}) async-start(bf16[32,16,128]{2,1,0:T(8,128)(2,1)} %bitcast.4), calls=%async_computation | async-start | bytes 262144 | tf_op jit(solution)/shard_map/all_to_all | solution.py:631
  32.4 1.4 %advance.1 = f32[3,8,32,128]{3,2,1,0:T(8,128)} custom-call(f32[3,8,32,128]{3,2,1,0:T(8,128)S(1)} %copy-done.2, f32[3,32,128]{2,1,0:T(8,128)S(1)} %collective-permute-done.xlo_ref, f32[3,32,128]{2,1,0:T(8,128)S(1)} %collective-permute-done.1.xhi_ref, f32[3,16,128]{2,1,0:T(8,128)S(1)} %collective-permute-done.2.ylo_ref, ...), custom_call_target="tpu_custom_call" | custom-call | flops 1200000000 | bytes 1000000 | tf_op jit(solution)/shard_map/advance/pallas_call | solution.py:408
  33.8 8.0 %all-to-all-done = bf16[32,16,128]{2,1,0:T(8,128)(2,1)S(1)} async-done(((bf16[32,16,128]{2,1,0:T(8,128)(2,1)}), bf16[32,16,128]{2,1,0:T(8,128)(2,1)S(1)}, u32[]{:S(2)}, u32[]{:S(2)}) %all-to-all-start) | async-done | bytes 131104 | tf_op jit(solution)/shard_map/all_to_all | solution.py:631
  42.0 2.9 %collective-permute-start.7 = (bf16[96,512]{1,0:T(8,128)(2,1)S(1)}, bf16[96,512]{1,0:T(8,128)(2,1)S(1)}, u32[]{:S(2)}, u32[]{:S(2)}) collective-permute-start(bf16[96,512]{1,0:T(8,128)(2,1)S(1)} %turn.1.refs_0_), channel_id=1, source_target_pairs={{0,4},{1,5},{2,6},{3,7},{4,0},{5,1},{6,2},{7,3},{8,12},{9,13},{10,... | collective-permute-start | bytes 294920 | tf_op jit(solution)/shard_map/ppermute | solution.py:660
  45.2 1.8 %train.3 = (f32[512,96]{1,0:T(8,128)S(1)}, f32[64,512]{1,0:T(8,128)S(1)}, f32[16,512]{1,0:T(8,128)S(1)}, f32[512,128]{1,0:T(8,128)S(1)}, f32[512,128]{1,0:T(8,12...) custom-call(bf16[96,512]{1,0:T(8,128)(2,1)S(1)} %turn.1.refs_0_, bf16[512,96]{1,0:T(8,128)(2,1)S(1)} %pad.12.refs_1_.refs_2_.refs_3_, ...), custom_call_target="tpu_custom_call" | custom-call | flops 1280000000 | bytes 1000000 | tf_op jit(solution)/shard_map/train/pallas_call | solution.py:571
  47.0 2.1 %collective-permute-done.7.refs_1_ = bf16[96,512]{1,0:T(8,128)(2,1)S(1)} collective-permute-done((bf16[96,512]{1,0:T(8,128)(2,1)S(1)}, bf16[96,512]{1,0:T(8,128)(2,1)S(1)}, u32[]{:S(2)}, u32[]{:S(2)}) %collective-permute-start.7) | collective-permute-done | bytes 98336 | tf_op jit(solution)/shard_map/ppermute | solution.py:660
  49.0 1.0 %collective-permute-done.6.refs_0_ = bf16[96,512]{1,0:T(8,128)(2,1)S(1)} collective-permute-done((bf16[96,512]{1,0:T(8,128)(2,1)S(1)}, bf16[96,512]{1,0:T(8,128)(2,1)S(1)}, u32[]{:S(2)}, u32[]{:S(2)}) %collective-permute-start.6) | collective-permute-done | bytes 98336 | tf_op jit(solution)/shard_map/ppermute | solution.py:659
  50.1 2.0 %collective-permute-start.9 = (bf16[2,96,512]{2,1,0:T(8,128)(2,1)S(1)}, bf16[2,96,512]{2,1,0:T(8,128)(2,1)S(1)}, u32[]{:S(2)}, u32[]{:S(2)}) collective-permute-start(bf16[2,96,512]{2,1,0:T(8,128)(2,1)S(1)} %pad_maximum_fusion), channel_id=1, source_target_pairs={{0,6},{1,7},{2,0},{3,1},{4,2},{5,3},{6,4},{7,5},{8,14},{9,15},{10,... | collective-permute-start | bytes 589832 | tf_op jit(solution)/shard_map/ppermute | solution.py:664
  52.4 3.0 %train.4 = (f32[512,96]{1,0:T(8,128)S(1)}, f32[64,512]{1,0:T(8,128)S(1)}, f32[16,512]{1,0:T(8,128)S(1)}, f32[512,128]{1,0:T(8,128)S(1)}, f32[512,128]{1,0:T(8,128)S(1)}, /*index=5*/f32[8,128]{1,0:T(8,128)S(1)}) custom-call(bf16[96,512]{1,0:T(8,128)(2,1)S(1)} %collective-permute-done.6.refs_0_, bf16[96,512]{1,0:T(8,128)(2,1)S(1)} %collective-permute-done.7.refs_1_, ...), custom_call_target="tpu_custom_call" | custom-call | flops 2560000000 | bytes 1000000 | tf_op jit(solution)/shard_map/train/pallas_call | solution.py:571
  55.5 1.3 %collective-permute-done.10.refs_2_ = bf16[96,512]{1,0:T(8,128)(2,1)S(1)} collective-permute-done((bf16[96,512]{1,0:T(8,128)(2,1)S(1)}, bf16[96,512]{1,0:T(8,128)(2,1)S(1)}, u32[]{:S(2)}, u32[]{:S(2)}) %collective-permute-start.10) | collective-permute-done | bytes 98336 | tf_op jit(solution)/shard_map/ppermute | solution.py:665
  56.8 2.8 %collective-permute-done.8.refs_0_ = bf16[2,96,512]{2,1,0:T(8,128)(2,1)S(1)} collective-permute-done((bf16[2,96,512]{2,1,0:T(8,128)(2,1)S(1)}, bf16[2,96,512]{2,1,0:T(8,128)(2,1)S(1)}, u32[]{:S(2)}, u32[]{:S(2)}) %collective-permute-start.8) | collective-permute-done | bytes 196640 | tf_op jit(solution)/shard_map/ppermute | solution.py:664
  59.6 8.2 %train.5 = (f32[81,1,512]{2,1,0:T(1,128)}, f32[6,1,512]{2,1,0:T(1,128)}, f32[1,1030]{1,0:T(1,128)}, f32[256,128]{1,0:T(8,128)}, f32[256,128]{1,0:T(8,128)}) custom-call(bf16[2,96,512]{2,1,0:T(8,128)(2,1)S(1)} %collective-permute-done.8.refs_0_, bf16[2,96,512]{2,1,0:T(8,128)(2,1)S(1)} %collective-permute-done.9.refs_1_, ...), custom_call_target="tpu_custom_call" | custom-call | flops 6400000000 | bytes 1000000 | tf_op jit(solution)/shard_map/train/pallas_call | solution.py:571
  (51 shorter events, 4.0 us)
Async XLA Ops:
  1.5 5.4 %collective-permute-start.1 = (f32[3,32,128]{2,1,0:T(8,128)S(1)}, f32[3,32,128]{2,1,0:T(8,128)S(1)}, u32[]{:S(2)}, u32[]{:S(2)}) collective-permute-start(f32[3,32,128]{2,1,0:T(8,128)S(1)} %get-tuple-element.87), channel_id=1, source_target_pairs={{32,0},{64,32},{96,64},{128,96},{160,128},{192,160},{224,192},{0,2... | collective-permute-start | bytes 147464 | tf_op jit(solution)/shard_map/ppermute | solution.py:614
  3.9 0.7 %copy-start.5 = (s32[256,1]{0,1:T(1,128)S(1)}, s32[256,1]{0,1:T(1,128)}, u32[]{:S(2)}) copy-start(s32[256,1]{0,1:T(1,128)} %param.12) | copy-start | bytes 3076
  3.9 4.7 %collective-permute-start = (f32[3,32,128]{2,1,0:T(8,128)S(1)}, f32[3,32,128]{2,1,0:T(8,128)S(1)}, u32[]{:S(2)}, u32[]{:S(2)}) collective-permute-start(f32[3,32,128]{2,1,0:T(8,128)S(1)} %get-tuple-element.88), channel_id=1, source_target_pairs={{0,32},{32,64},{64,96},{96,128},{128,160},{160,192},{192,224},{224... | collective-permute-start | bytes 147464 | tf_op jit(solution)/shard_map/ppermute | solution.py:613
  4.6 1.0 %copy-start.1 = (f32[3,8,32,128]{3,2,1,0:T(8,128)S(1)}, f32[3,8,32,128]{3,2,1,0:T(8,128)}, u32[]{:S(2)}) copy-start(f32[3,8,32,128]{3,2,1,0:T(8,128)} %v_ref.5) | copy-start | bytes 1179652
  6.2 0.7 %copy-start.10 = (bf16[6,256]{1,0:T(8,128)(2,1)S(1)}, bf16[6,256]{1,0:T(8,128)(2,1)}, u32[]{:S(2)}) copy-start(bf16[6,256]{1,0:T(8,128)(2,1)} %param.13) | copy-start | bytes 9220
  8.7 5.6 %copy-start.2 = (f32[3,8,32,128]{3,2,1,0:T(8,128)S(1)}, f32[3,8,32,128]{3,2,1,0:T(8,128)}, u32[]{:S(2)}) copy-start(f32[3,8,32,128]{3,2,1,0:T(8,128)} %v_ref.5) | copy-start | bytes 1179652
  8.7 7.3 %collective-permute-start.2 = (f32[3,16,128]{2,1,0:T(8,128)S(1)}, f32[3,16,128]{2,1,0:T(8,128)S(1)}, u32[]{:S(2)}, u32[]{:S(2)}) collective-permute-start(f32[3,16,128]{2,1,0:T(8,128)S(1)} %get-tuple-element.50), channel_id=1, source_target_pairs={{0,8},{8,16},{16,24},{24,0},{1,9},{9,17},{17,25},{25,1},{2,10},{10... | collective-permute-start | bytes 73736 | tf_op jit(solution)/shard_map/ppermute | solution.py:620
  12.0 2.2 %copy-start.6 = (s32[256]{0:T(256)S(1)}, s32[256]{0:T(256)}, u32[]{:S(2)}) copy-start(s32[256]{0:T(256)} %param.11) | copy-start | bytes 3076
  12.0 5.4 %collective-permute-start.3 = (f32[3,16,128]{2,1,0:T(8,128)S(1)}, f32[3,16,128]{2,1,0:T(8,128)S(1)}, u32[]{:S(2)}, u32[]{:S(2)}) collective-permute-start(f32[3,16,128]{2,1,0:T(8,128)S(1)} %get-tuple-element.51), channel_id=1, source_target_pairs={{8,0},{16,8},{24,16},{0,24},{9,1},{17,9},{25,17},{1,25},{10,2},{18... | collective-permute-start | bytes 73736 | tf_op jit(solution)/shard_map/ppermute | solution.py:621
  17.5 3.9 %collective-permute-start.4 = (f32[48,128]{1,0:T(8,128)S(1)}, f32[48,128]{1,0:T(8,128)S(1)}, u32[]{:S(2)}, u32[]{:S(2)}) collective-permute-start(f32[48,128]{1,0:T(8,128)S(1)} %get-tuple-element.56), channel_id=1, source_target_pairs={{0,1},{1,2},{2,3},{3,4},{4,5},{5,6},{6,7},{7,0},{8,9},{9,10},{10,1... | collective-permute-start | bytes 73736 | tf_op jit(solution)/shard_map/ppermute | solution.py:625
  19.6 4.7 %collective-permute-start.5 = (f32[48,128]{1,0:T(8,128)S(1)}, f32[48,128]{1,0:T(8,128)S(1)}, u32[]{:S(2)}, u32[]{:S(2)}) collective-permute-start(f32[48,128]{1,0:T(8,128)S(1)} %get-tuple-element.57), channel_id=1, source_target_pairs={{1,0},{2,1},{3,2},{4,3},{5,4},{6,5},{7,6},{0,7},{9,8},{10,9},{11,1... | collective-permute-start | bytes 73736 | tf_op jit(solution)/shard_map/ppermute | solution.py:626
  24.4 7.2 %copy-start.8 = (f32[1,1030]{1,0:T(1,128)S(1)}, f32[1,1030]{1,0:T(1,128)}, u32[]{:S(2)}) copy-start(f32[1,1030]{1,0:T(1,128)} %param.17) | copy-start | bytes 12364
  24.4 7.3 %copy-start.7 = (bf16[1,512,81]{1,2,0:T(8,128)(2,1)S(1)}, bf16[1,512,81]{1,2,0:T(8,128)(2,1)}, u32[]{:S(2)}) copy-start(bf16[1,512,81]{1,2,0:T(8,128)(2,1)} %param.14) | copy-start | bytes 248836
  24.4 7.4 %copy-start.9 = (bf16[1,6,512]{2,1,0:T(8,128)(2,1)S(1)}, bf16[1,6,512]{2,1,0:T(8,128)(2,1)}, u32[]{:S(2)}) copy-start(bf16[1,6,512]{2,1,0:T(8,128)(2,1)} %param.16) | copy-start | bytes 18436
  25.8 6.4 %copy-start = (bf16[1,512,512]{2,1,0:T(8,128)(2,1)S(1)}, bf16[1,512,512]{2,1,0:T(8,128)(2,1)}, u32[]{:S(2)}) copy-start(bf16[1,512,512]{2,1,0:T(8,128)(2,1)} %param.15) | copy-start | bytes 1572868
  25.8 16.1 %all-to-all-start = ((bf16[32,16,128]{2,1,0:T(8,128)(2,1)}), bf16[32,16,128]{2,1,0:T(8,128)(2,1)S(1)}, u32[]{:S(2)}, u32[]{:S(2)}) async-start(bf16[32,16,128]{2,1,0:T(8,128)(2,1)} %bitcast.4), calls=%async_computation | async-start | bytes 262144 | tf_op jit(solution)/shard_map/all_to_all | solution.py:631
  42.0 2.9 %slice-start = ((f32[1,1030]{1,0:T(1,128)}), f32[1,1024]{1,0:T(1,128)S(1)}, s32[]{:S(2)}) async-start(f32[1,1030]{1,0:T(1,128)} %param.17), calls=%async_computation.1 | async-start | bytes 8192 | tf_op jit(solution)/shard_map/slice | solution.py:644
  42.0 7.0 %collective-permute-start.7 = (bf16[96,512]{1,0:T(8,128)(2,1)S(1)}, bf16[96,512]{1,0:T(8,128)(2,1)S(1)}, u32[]{:S(2)}, u32[]{:S(2)}) collective-permute-start(bf16[96,512]{1,0:T(8,128)(2,1)S(1)} %turn.1.refs_0_), channel_id=1, source_target_pairs={{0,4},{1,5},{2,6},{3,7},{4,0},{5,1},{6,2},{7,3},{8,12},{9,13},{10,... | collective-permute-start | bytes 294920 | tf_op jit(solution)/shard_map/ppermute | solution.py:660
  44.9 5.1 %collective-permute-start.6 = (bf16[96,512]{1,0:T(8,128)(2,1)S(1)}, bf16[96,512]{1,0:T(8,128)(2,1)S(1)}, u32[]{:S(2)}, u32[]{:S(2)}) collective-permute-start(bf16[96,512]{1,0:T(8,128)(2,1)S(1)} %turn.1.refs_0_), channel_id=1, source_target_pairs={{0,1},{1,0},{2,3},{3,2},{4,5},{5,4},{6,7},{7,6},{8,9},{9,8},{10,11... | collective-permute-start | bytes 294920 | tf_op jit(solution)/shard_map/ppermute | solution.py:659
  50.0 9.6 %copy-start.3 = (f32[1,32768]{1,0:T(1,128)S(1)}, f32[1,32768]{1,0:T(1,128)}, u32[]{:S(2)}) copy-start(f32[1,32768]{1,0:T(1,128)} %param.19) | copy-start | bytes 393220
  50.1 9.6 %copy-start.4 = (f32[1,32768]{1,0:T(1,128)S(1)}, f32[1,32768]{1,0:T(1,128)}, u32[]{:S(2)}) copy-start(f32[1,32768]{1,0:T(1,128)} %param.18) | copy-start | bytes 393220
  50.1 6.7 %collective-permute-start.9 = (bf16[2,96,512]{2,1,0:T(8,128)(2,1)S(1)}, bf16[2,96,512]{2,1,0:T(8,128)(2,1)S(1)}, u32[]{:S(2)}, u32[]{:S(2)}) collective-permute-start(bf16[2,96,512]{2,1,0:T(8,128)(2,1)S(1)} %pad_maximum_fusion), channel_id=1, source_target_pairs={{0,6},{1,7},{2,0},{3,1},{4,2},{5,3},{6,4},{7,5},{8,14},{9,15},{10,... | collective-permute-start | bytes 589832 | tf_op jit(solution)/shard_map/ppermute | solution.py:664
  52.0 7.6 %collective-permute-start.8 = (bf16[2,96,512]{2,1,0:T(8,128)(2,1)S(1)}, bf16[2,96,512]{2,1,0:T(8,128)(2,1)S(1)}, u32[]{:S(2)}, u32[]{:S(2)}) collective-permute-start(bf16[2,96,512]{2,1,0:T(8,128)(2,1)S(1)} %pad_maximum_fusion), channel_id=1, source_target_pairs={{0,2},{1,3},{2,4},{3,5},{4,6},{5,7},{6,0},{7,1},{8,10},{9,11},{10,... | collective-permute-start | bytes 589832 | tf_op jit(solution)/shard_map/ppermute | solution.py:664
  52.2 4.6 %collective-permute-start.10 = (bf16[96,512]{1,0:T(8,128)(2,1)S(1)}, bf16[96,512]{1,0:T(8,128)(2,1)S(1)}, u32[]{:S(2)}, u32[]{:S(2)}) collective-permute-start(bf16[96,512]{1,0:T(8,128)(2,1)S(1)} %collective-permute-done.7.refs_1_), channel_id=1, source_target_pairs={{0,1},{1,0},{2,3},{3,2},{4,5},{5,4},{6,7},{7,6},{8,9},{9,8},{10,11... | collective-permute-start | bytes 294920 | tf_op jit(solution)/shard_map/ppermute | solution.py:665
where the time goes:
time: 68.2 us; the launch traced here: 67.8 us
  waiting for transfers between devices  23.4 us (34%)
  starting transfers between devices  21.2 us (31%)
  Pallas kernels  18.1 us (27%)
  local copies, waits for them, and re-layouts  4.2 us (6%)
  between operations  0.83 us (1%)
    pallas_call x3, Pallas kernels, train(): pl.pallas_call(functools.partial(train_kernel, planes=planes, row_count=r...  13.1 us
    all_to_all x1, waiting for transfers between devices, on_device(): lax.all_to_all(packed.reshape(trainers, capacity, WIDE), ('gx', 'gy'), sp...  8.03 us
    all_to_all x1, starting transfers between devices, on_device(): lax.all_to_all(packed.reshape(trainers, capacity, WIDE), ('gx', 'gy'), sp...  5.83 us
    ppermute x1, starting transfers between devices, on_device(): ylo = lax.ppermute(y_high, 'gy', forward)  3.35 us
    ppermute x1, waiting for transfers between devices, on_device(): zhi = lax.ppermute(z_low, 'gz', backward)  2.93 us
    unnamed x26, local copies, waits for them, and re-layouts  2.87 us
    ppermute x1, starting transfers between devices, on_device(): far = lax.ppermute(mine, 'gz', move(planes // 2))  2.86 us
    ppermute x2, waiting for transfers between devices, on_device(): near = [lax.ppermute(both, 'gz', move(k)) for k in (2, planes - 2)]  2.82 us
  transfers between devices with their start and end apart: 12, of which 10 were waited for; matrix products, arithmetic and copies ran while one was open for 2% of the time, Pallas kernels for 12%

commit v1 on v0

--- a/solution.py
+++ b/solution.py
@@ -55,10 +55,32 @@
     return jnp.where(mask, 1.0, 0.0).astype(BF16)
 
 
-def shifts(axis):
+def exchange(axis, low_face, high_face):
     count = lax.axis_size(axis)
     forward = [(i, (i + 1) % count) for i in range(count)]
-    return forward, [(b, a) for a, b in forward]
+    backward = [(b, a) for a, b in forward]
+    return lax.ppermute(high_face, axis, forward), lax.ppermute(low_face, axis, backward)
+
+
+def faces_kernel(low_ref, high_ref, to_low_ref, to_high_ref):
+    to_low_ref[...] = low_ref[:, 0]
+    to_high_ref[...] = high_ref[:, 0]
+
+
+def x_faces(velocity):
+    comps, size_x, size_y, size_z = velocity.shape
+    spec = lambda at: pl.BlockSpec((comps, 1, size_y, size_z), lambda i: (0, at, 0, 0))
+    out = pl.BlockSpec((comps, size_y, size_z), lambda i: (0, 0, 0))
+    return pl.pallas_call(
+        faces_kernel,
+        grid=(1,),
+        out_shape=tuple([jax.ShapeDtypeStruct((comps, size_y, size_z), F32)] * 2),
+        in_specs=[spec(0), spec(size_x - 1)],
+        out_specs=(out, out),
+        compiler_params=params(),
+        cost_estimate=cost(0.3),
+        name="x_faces",
+    )(velocity, velocity)
 
 
 def end_rows(block, low_ref, high_ref, row_of, size_y):
@@ -75,15 +97,11 @@
 
 
 def plan_kernel(
-    v_ref, trainer_ref, y_low_ref, y_high_ref, z_low_ref, z_high_ref, placing_ref, *, trainers
+    v_ref, xlo_ref, xhi_ref, trainer_ref, z_low_ref, z_high_ref, placing_ref, *, trainers
 ):
     comps, size_x, size_y, size_z = v_ref.shape
-    for ref in (y_low_ref, y_high_ref, z_low_ref, z_high_ref):
+    for ref in (z_low_ref, z_high_ref):
         ref[...] = jnp.zeros_like(ref)
-    for c in range(comps):
-        for x in range(size_x):
-            y_low_ref[c, x + 1 : x + 2, :] = v_ref[c, x, 0:1, :]
-            y_high_ref[c, x + 1 : x + 2, :] = v_ref[c, x, size_y - 1 : size_y, :]
     end_rows(
         v_ref[...].reshape(-1, size_z),
         z_low_ref,
@@ -91,6 +109,10 @@
         lambda k: k // size_x * PAD_X + k % size_x + 1,
         size_y,
     )
+    before, after = inside("gx")
+    for ref, scale, x in ((xlo_ref, before, 0), (xhi_ref, after, size_x + 1)):
+        block = ref[...].reshape(-1, size_z) * scale
+        end_rows(block, z_low_ref, z_high_ref, lambda k: k * PAD_X + x, size_y)
 
     trainer = trainer_ref[...]
     samples = trainer.shape[1]
@@ -104,71 +126,72 @@
     placing_ref[...] = ones_where(iota((slots, samples), 0) == slot)
 
 
-def plan(velocity, trainer, trainers, slots):
+def plan(velocity, x_halos, trainer, trainers, slots):
     comps, size_x, size_y, size_z = velocity.shape
-    y_face = jax.ShapeDtypeStruct((comps, PAD_X, size_z), F32)
     z_face = jax.ShapeDtypeStruct((comps * PAD_X, WIDE), F32)
     placing = jax.ShapeDtypeStruct((slots, trainer.shape[1]), BF16)
     return pl.pallas_call(
         functools.partial(plan_kernel, trainers=trainers),
-        out_shape=(y_face, y_face, z_face, z_face, placing),
-        in_specs=whole(2),
-        out_specs=tuple(whole(5)),
+        out_shape=(z_face, z_face, placing),
+        in_specs=whole(4),
+        out_specs=tuple(whole(3)),
         compiler_params=params(),
         cost_estimate=cost(1.5),
         name="plan",
-    )(velocity, trainer)
-
-
-def y_faces_kernel(low_ref, high_ref, xlo_ref, xhi_ref, to_low_ref, to_high_ref, *, size_x):
+    )(velocity, *x_halos, trainer)
+
+
+def y_faces_kernel(low_ref, high_ref, xlo_ref, xhi_ref, to_low_ref, to_high_ref):
+    comps, size_x = low_ref.shape[0], low_ref.shape[1]
     before, after = inside("gx")
     last = xlo_ref.shape[1] - 1
-    for own, to, y in ((low_ref, to_low_ref, 0), (high_ref, to_high_ref, last)):
-        to[...] = own[...]
-        for c in range(to.shape[0]):
+    for to, own, row, y in ((to_low_ref, low_ref, 0, 0), (to_high_ref, high_ref, 7, last)):
+        to[...] = jnp.zeros_like(to)
+        for c in range(comps):
             to[c, 0:1, :] = xlo_ref[c, y : y + 1, :] * before
+            for x in range(size_x):
+                to[c, x + 1 : x + 2, :] = own[c, x, row : row + 1, :]
             to[c, size_x + 1 : size_x + 2, :] = xhi_ref[c, y : y + 1, :] * after
 
 
-def y_faces(low, high, xlo, xhi, size_x):
-    return pl.pallas_call(
-        functools.partial(y_faces_kernel, size_x=size_x),
-        out_shape=tuple([jax.ShapeDtypeStruct(low.shape, F32)] * 2),
-        in_specs=whole(4),
-        out_specs=tuple(whole(2)),
+def y_faces(velocity, x_halos):
+    comps, size_x, size_y, size_z = velocity.shape
+    shape = (comps, PAD_X, size_z)
+    spec = lambda at: pl.BlockSpec((comps, size_x, 8, size_z), lambda i: (0, 0, at, 0))
+    full = lambda a: pl.BlockSpec(a, lambda i: (0,) * len(a))
+    return pl.pallas_call(
+        y_faces_kernel,
+        grid=(1,),
+        out_shape=tuple([jax.ShapeDtypeStruct(shape, F32)] * 2),
+        in_specs=[spec(0), spec(size_y // 8 - 1)] + [full(x_halos[0].shape)] * 2,
+        out_specs=(full(shape), full(shape)),
         compiler_params=params(),
         cost_estimate=cost(0.3),
         name="y_faces",
-    )(low, high, xlo, xhi)
-
-
-def z_faces_kernel(
-    low_ref, high_ref, x_low_ref, x_high_ref, ylo_ref, yhi_ref, to_low_ref, to_high_ref, *, size_y
-):
+    )(velocity, velocity, *x_halos)
+
+
+def z_faces_kernel(low_ref, high_ref, ylo_ref, yhi_ref, to_low_ref, to_high_ref, *, size_y):
     before, after = inside("gy")
     size_z = ylo_ref.shape[2]
     ylo = ylo_ref[...].reshape(-1, size_z) * before
     yhi = yhi_ref[...].reshape(-1, size_z) * after
     lane = iota(low_ref.shape, 1)
-    for own, x, to, z in (
-        (low_ref, x_low_ref, to_low_ref, 0),
-        (high_ref, x_high_ref, to_high_ref, size_z - 1),
-    ):
-        face = own[...] + x[...]
-        face = jnp.where(lane == 0, ylo[:, z : z + 1], face)
+    for own, to, z in ((low_ref, to_low_ref, 0), (high_ref, to_high_ref, size_z - 1)):
+        face = jnp.where(lane == 0, ylo[:, z : z + 1], own[...])
         to[...] = jnp.where(lane == size_y + 1, yhi[:, z : z + 1], face)
 
 
-def z_faces(low, high, x_low, x_high, ylo, yhi, size_y):
+def z_faces(low, high, y_halos, size_y):
     return pl.pallas_call(
         functools.partial(z_faces_kernel, size_y=size_y),
         out_shape=tuple([jax.ShapeDtypeStruct(low.shape, F32)] * 2),
-        in_specs=whole(6),
+        in_specs=whole(4),
         out_specs=tuple(whole(2)),
         compiler_params=params(),
         cost_estimate=cost(0.3),
         name="z_faces",
-    )(low, high, x_low, x_high, ylo, yhi)
+    )(low, high, *y_halos)
 
 
 def split_cells(cells, size_x, size_y, size_z):
@@ -201,21 +224,18 @@
 
 
 def patch_kernel(
-    v_ref, xlo_ref, xhi_ref, cells_ref, out_ref, z_low_ref, z_high_ref, picked, parts
+    v_ref, xlo_ref, xhi_ref, cells_ref, after_ref, out_ref, picked, parts
 ):
     comps, size_x, size_y, size_z = v_ref.shape
     samples = cells_ref.shape[1]
     before, after = inside("gx")
-    z_low_ref[...] = jnp.zeros_like(z_low_ref)
-    z_high_ref[...] = jnp.zeros_like(z_high_ref)
     cell_x, cell_y, cell_z = split_cells(cells_ref[...], size_x, size_y, size_z)
     choose = depth_choice(cell_z, size_z)
     starts, start = [], 0
-    for ref, scale, x in ((v_ref, None, 0), (xlo_ref, before, 0), (xhi_ref, after, size_x + 1)):
+    for ref, scale in ((v_ref, None), (xlo_ref, before), (xhi_ref, after)):
         block = ref[...].reshape(-1, size_z)
         if scale is not None:
             block = block * scale
-            end_rows(block, z_low_ref, z_high_ref, lambda k: k * PAD_X + x, size_y)
         picked[start : start + block.shape[0], :] = jnp.dot(
             block.astype(BF16), choose, preferred_element_type=F32
         )
@@ -248,15 +268,14 @@
     out_ref[...] = add_tiles(parts, 27 * comps)
 
 
-def patches(velocity, xlo, xhi, cells, z_face):
+def patches(velocity, x_halos, cells, after):
     comps, size_x, size_y, size_z = velocity.shape
     samples = cells.shape[1]
-    face = jax.ShapeDtypeStruct(z_face.shape, F32)
     return pl.pallas_call(
         patch_kernel,
-        out_shape=(jax.ShapeDtypeStruct((ROWS, samples), F32), face, face),
-        in_specs=whole(4),
-        out_specs=tuple(whole(3)),
+        out_shape=jax.ShapeDtypeStruct((ROWS, samples), F32),
+        in_specs=whole(5),
+        out_specs=pl.BlockSpec(memory_space=pltpu.VMEM),
         scratch_shapes=[
             pltpu.VMEM((comps * (size_x + 2) * size_y, 3 * samples), F32),
             pltpu.VMEM((27 * comps * 8, samples), F32),
@@ -264,7 +283,7 @@
         compiler_params=params(),
         cost_estimate=cost(2.5),
         name="patches",
-    )(velocity, xlo, xhi, cells)
+    )(velocity, *x_halos, cells, after)
 
 
 def pack_kernel(
@@ -338,9 +357,9 @@
     ).astype(BF16)
 
 
-def pack(own, ylo, yhi, zlo, zhi, cells, tail, placing, size_x, size_y):
+def pack(own, y_halos, z_halos, cells, tail, placing, size_x, size_y):
     samples = cells.shape[1]
-    comps, pad_x, _ = ylo.shape
+    comps, pad_x, _ = y_halos[0].shape
     return pl.pallas_call(
         functools.partial(pack_kernel, size_x=size_x, size_y=size_y),
         out_shape=jax.ShapeDtypeStruct((placing.shape[0], WIDE), BF16),
@@ -353,29 +372,35 @@
         compiler_params=params(),
         cost_estimate=cost(1.0),
         name="pack",
-    )(own, ylo, yhi, zlo, zhi, cells, tail, placing)
-
-
-def advance_kernel(v_ref, xlo_ref, xhi_ref, ylo_ref, yhi_ref, zlo_ref, zhi_ref, out_ref):
+    )(own, *y_halos, *z_halos, cells, tail, placing)
+
+
+def advance_kernel(
+    v_ref, xlo_ref, xhi_ref, ylo_ref, yhi_ref, zlo_ref, zhi_ref, out_ref, done_ref
+):
     comps, size_x, size_y, size_z = v_ref.shape
+    done_ref[...] = jnp.zeros_like(done_ref)
     x_before, x_after = inside("gx")
     y_before, y_after = inside("gy")
     z_before, z_after = inside("gz")
 
-    def columns(ref, scale):
-        face = ref[...] * scale
+    xlo, xhi = xlo_ref[...] * x_before, xhi_ref[...] * x_after
+    ylo, yhi = ylo_ref[...] * y_before, yhi_ref[...] * y_after
+
+    def columns(face, scale):
+        face = face * scale
         face = jnp.concatenate([face, jnp.zeros((WIDE - face.shape[0], WIDE), F32)], axis=0)
         return pltpu.roll(face.T, WIDE - 1, 0)[:size_y, :]
 
-    z_low, z_high = columns(zlo_ref, z_before), columns(zhi_ref, z_after)
+    z_low, z_high = columns(zlo_ref[...], z_before), columns(zhi_ref[...], z_after)
     y_at = iota((size_y, size_z), 0)
     z_at = iota((size_y, size_z), 1)
 
     def plane(c, x):
         if x < 0:
-            return xlo_ref[c] * x_before
+            return xlo[c]
         if x >= size_x:
-            return xhi_ref[c] * x_after
+            return xhi[c]
         return v_ref[c, x]
 
     for x in range(size_x):
@@ -385,8 +410,8 @@
         y_up, y_down, z_up, z_down = [], [], [], []
         for c in range(comps):
             at = c * PAD_X + x + 1
-            above = yhi_ref[c, x + 1 : x + 2, :] * y_after
-            below = ylo_ref[c, x + 1 : x + 2, :] * y_before
+            above = yhi[c, x + 1 : x + 2, :]
+            below = ylo[c, x + 1 : x + 2, :]
             y_up.append(jnp.where(y_at == size_y - 1, above, pltpu.roll(here[c], size_y - 1, 0)))
             y_down.append(jnp.where(y_at == 0, below, pltpu.roll(here[c], 1, 0)))
             z_up.append(
@@ -407,31 +432,82 @@
 def advance(velocity, halos):
     return pl.pallas_call(
         advance_kernel,
-        out_shape=jax.ShapeDtypeStruct(velocity.shape, F32),
+        out_shape=(
+            jax.ShapeDtypeStruct(velocity.shape, F32),
+            jax.ShapeDtypeStruct((8, WIDE), F32),
+        ),
         in_specs=whole(7),
-        out_specs=pl.BlockSpec(memory_space=pltpu.VMEM),
+        out_specs=tuple(whole(2)),
         compiler_params=params(),
         cost_estimate=cost(1.5),
         name="advance",
     )(velocity, *halos)
 
 
-def turn_kernel(in_ref, out_ref):
+def prepare_kernel(
+    first_ref, middle_ref, last_ref, biases_ref, w1_ref, w2t_ref, w3_ref, w3t_ref, bias_ref, bias3_ref
+):
+    feats, hidden = first_ref.shape
+    count = last_ref.shape[0]
+    wide = jnp.concatenate(
+        [first_ref[...].astype(F32), jnp.zeros((WIDE - feats, hidden), F32)], axis=0
+    )
+    w1_ref[...] = wide.T[:, :ROWS].astype(BF16)
+    eye = ones_where(iota((hidden, hidden), 0) == iota((hidden, hidden), 1))
+    w2t_ref[...] = lax.dot_general(
+        eye, middle_ref[...], NT, preferred_element_type=F32
+    ).astype(BF16)
+    last = last_ref[...].astype(F32)
+    w3_ref[...] = jnp.concatenate([last, jnp.zeros((16 - count, hidden), F32)], axis=0).astype(BF16)
+    wide = jnp.concatenate([last, jnp.zeros((WIDE - count, hidden), F32)], axis=0)
+    w3t_ref[...] = wide.T[:, :16].astype(BF16)
+    for k in range(2 * hidden // WIDE):
+        row = biases_ref[:, k * WIDE : (k + 1) * WIDE]
+        bias_ref[k * WIDE : (k + 1) * WIDE, :] = jnp.broadcast_to(row, (WIDE, WIDE)).T
+    tail = jnp.concatenate(
+        [biases_ref[:, 2 * hidden :], jnp.zeros((1, WIDE - count), F32)], axis=1
+    )
+    bias3_ref[...] = jnp.broadcast_to(tail, (WIDE, WIDE)).T[:8]
+
+
+def prepare(first, middle, last, biases):
+    hidden = middle.shape[0]
+    shapes = [
+        ((hidden, ROWS), BF16),
+        ((hidden, hidden), BF16),
+        ((16, hidden), BF16),
+        ((hidden, 16), BF16),
+        ((2 * hidden, WIDE), F32),
+        ((8, WIDE), F32),
+    ]
+    w1, w2t, w3, w3t, bias, bias3 = pl.pallas_call(
+        prepare_kernel,
+        out_shape=tuple(jax.ShapeDtypeStruct(*s) for s in shapes),
+        in_specs=whole(4),
+        out_specs=tuple(whole(6)),
+        compiler_params=params(),
+        cost_estimate=cost(1.0),
+        name="prepare",
+    )(first, middle, last, biases)
+    return w1, middle, w2t, w3, w3t, bias, bias3
+
+
+def turn_kernel(in_ref, prepared_ref, done_ref, out_ref):
     shape = (out_ref.shape[0], in_ref.shape[1])
     eye = ones_where(iota(shape, 0) == iota(shape, 1))
     out_ref[...] = lax.dot_general(eye, in_ref[...], NT, preferred_element_type=F32).astype(BF16)
 
 
-def turn(arrived):
+def turn(arrived, prepared, done):
     return pl.pallas_call(
         turn_kernel,
         out_shape=jax.ShapeDtypeStruct((ROWS, arrived.shape[0]), BF16),
-        in_specs=whole(1),
+        in_specs=whole(3),
         out_specs=pl.BlockSpec(memory_space=pltpu.VMEM),
         compiler_params=params(),
         cost_estimate=cost(0.2),
         name="turn",
-    )(arrived)
+    )(arrived, prepared, done)
 
 
 def lane_sum(value):
@@ -459,12 +535,11 @@
     g1, g2, g3, s1, s2, s3 = sums
     hidden = w2_ref.shape[0]
     factor = 2.0 / (6.0 * row_count)
-    if first:
-        for ref in sums:
-            ref[...] = jnp.zeros_like(ref)
-    else:
-        for ref, old in zip(sums, held):
-            ref[...] = old[...]
+    olds = dict(zip(map(id, sums), held))
+
+    def add(ref, value):
+        ref[...] = value if first else olds[id(ref)][...] + value
+
     own = pl.multiple_of(lax.axis_index("gz") * own_rows, own_rows)
 
     def plane(x):
@@ -485,24 +560,24 @@
         )
         delta_three = mismatch * factor
         back_three = jnp.concatenate([delta_three, jnp.zeros_like(delta_three)], axis=0).astype(BF16)
-        g3[...] += lax.dot_general(back_three, act_two, NT, preferred_element_type=F32)
+        add(g3, lax.dot_general(back_three, act_two, NT, preferred_element_type=F32))
         wide_two = act_two.astype(F32)
         delta_two = jnp.dot(w3t_ref[...], back_three, preferred_element_type=F32) * (
             1.0 - wide_two * wide_two
         )
-        s2[...] += lane_sum(delta_two)
+        add(s2, lane_sum(delta_two))
         back_two = delta_two.astype(BF16)
         back_two_ref[...] = back_two
-        g2[...] += lax.dot_general(
-            back_two_ref[pl.ds(own, own_rows), :], act_one, NT, preferred_element_type=F32
-        )
+        mine = back_two_ref[pl.ds(own, own_rows), :]
+        add(g2, lax.dot_general(mine, act_one, NT, preferred_element_type=F32))
         wide_one = act_one.astype(F32)
         delta_one = jnp.dot(w2t_ref[...], back_two, preferred_element_type=F32) * (
             1.0 - wide_one * wide_one
         )
-        s1[...] += lane_sum(delta_one)
-        g1[...] += lax.dot_general(delta_one.astype(BF16), x, NT, preferred_element_type=F32)
-        s3[...] += lane_sum(delta_three)
+        add(s1, lane_sum(delta_one))
+        back_one = delta_one.astype(BF16)
+        add(g1, lax.dot_general(back_one, x, NT, preferred_element_type=F32))
+        add(s3, lane_sum(delta_three))
         return mismatch
 
     pieces = []
@@ -514,18 +589,17 @@
         row_loss = jnp.sum(mismatch * mismatch, axis=0, keepdims=True) / (6.0 * row_count)
         loss_ref[...] = jnp.sum(row_loss, axis=1, keepdims=True)
     if last:
+        per_row = hidden // WIDE
         wide = jnp.concatenate([g1[...], jnp.zeros((hidden, WIDE - ROWS), F32)], axis=1)
         for ref, grads in ((first_ref, wide.T), (last_ref, g3[...])):
             for k in range(ref.shape[0]):
                 ref[k] = grads[k : k + 1, :]
-        ones = jnp.ones((8, WIDE), F32)
-        across = lambda s: lax.dot_general(ones, s, NT, precision=EXACT, preferred_element_type=F32)
-        bias_grads_ref[:, :hidden] = across(s1[...])[0:1]
-        bias_grads_ref[:, hidden : 2 * hidden] = across(s2[...])[0:1]
+        across = lambda s: jnp.sum(s.T, axis=0, keepdims=True)
+        bias_grads_ref[:, :hidden] = across(s1[...])
+        bias_grads_ref[:, hidden : 2 * hidden] = across(s2[...])
         third = across(jnp.concatenate([s3[...], jnp.zeros((WIDE - 8, WIDE), F32)], axis=0))
-        bias_grads_ref[:, 2 * hidden :] = third[0:1, :6]
+        bias_grads_ref[:, 2 * hidden :] = third[:, :6]
         grads = g2[...]
-        per_row = hidden // WIDE
         for k in range(per_row):
             at = pl.ds(k, own_rows, stride=per_row)
             momentum = MOMENTUM_KEEP * momentum_ref[at, :] + grads[:, k * WIDE : (k + 1) * WIDE]
@@ -609,25 +683,18 @@
     own_rows = hidden // planes
 
     cells = sample_cells.reshape(1, samples)
-    forward, backward = shifts("gx")
-    xlo = lax.ppermute(velocity[:, size_x - 1], "gx", forward)
-    xhi = lax.ppermute(velocity[:, 0], "gx", backward)
-    y_low, y_high, z_low, z_high, placing = plan(
-        velocity, trainer_of.reshape(1, samples), trainers, slots
-    )
-    y_low, y_high = y_faces(y_low, y_high, xlo, xhi, size_x)
-    forward, backward = shifts("gy")
-    ylo = lax.ppermute(y_high, "gy", forward)
-    yhi = lax.ppermute(y_low, "gy", backward)
-    features, x_low, x_high = patches(velocity, xlo, xhi, cells, z_low)
-    z_low, z_high = z_faces(z_low, z_high, x_low, x_high, ylo, yhi, size_y)
-    forward, backward = shifts("gz")
-    zlo = lax.ppermute(z_high, "gz", forward)
-    zhi = lax.ppermute(z_low, "gz", backward)
+    x_halos = exchange("gx", *x_faces(velocity))
+    y_halos = exchange("gy", *y_faces(velocity, x_halos))
+    z_low, z_high, placing = plan(
+        velocity, x_halos, trainer_of.reshape(1, samples), trainers, slots
+    )
+    z_ends = z_faces(z_low, z_high, y_halos, size_y)
+    z_halos = exchange("gz", *z_ends)
+    features = patches(velocity, x_halos, cells, z_ends[0])
     tail = jnp.concatenate(
         [targets.astype(F32), jnp.ones((1, samples), F32), jnp.zeros((1, samples), F32)], axis=0
     )
-    packed = pack(features, ylo, yhi, zlo, zhi, cells, tail, placing, size_x, size_y)
+    packed = pack(features, y_halos, z_halos, cells, tail, placing, size_x, size_y)
     arrived = lax.all_to_all(
         packed.reshape(trainers, capacity, WIDE),
         ("gx", "gy"),
@@ -635,33 +702,28 @@
         concat_axis=0,
         tiled=True,
     ).reshape(slots, WIDE)
-    new_velocity = advance(velocity, (xlo, xhi, ylo, yhi, zlo, zhi))
-
-    feats = w_first.shape[2]
-    w1 = jnp.pad(w_first[0], ((0, 0), (0, ROWS - feats)))
-    w2 = w_middle[0]
-    w3 = jnp.pad(w_last[0], ((0, 16 - w_last.shape[1]), (0, 0)))
-    bias = jnp.broadcast_to(biases[0, : 2 * hidden, None], (2 * hidden, WIDE))
-    bias3 = jnp.broadcast_to(
-        jnp.pad(biases[0, 2 * hidden :], (0, 8 - w_last.shape[1]))[:, None], (8, WIDE)
-    )
-    weights = (w1, w2, w2.T, w3, w3.T, bias, bias3)
+    new_velocity, done = advance(velocity, (*x_halos, *y_halos, *z_halos))
+
+    weights = prepare(w_first[0].T, w_middle[0], w_last[0], biases)
     optimizer = (
         middle_momentum.reshape(-1, WIDE),
         middle_master.reshape(-1, WIDE),
     )
 
-    arrived, new_velocity = lax.optimization_barrier((arrived, new_velocity))
-    mine = turn(arrived)
+    mine = turn(arrived, weights[-1], done)
     call = functools.partial(train, weights=weights, row_count=samples, own_rows=own_rows)
     swap = [(i, i ^ 1) for i in range(planes)]
-    move = lambda k: [(i, (i + k) % planes) for i in range(planes)]
+    chips = planes // 2
+    along = lambda to: [(i, 2 * (to(i // 2) % chips) + i % 2) for i in range(planes)]
     beside = lax.ppermute(mine, "gz", swap)
-    far = lax.ppermute(mine, "gz", move(planes // 2))
+    far = lax.ppermute(mine, "gz", along(lambda x: x + 2))
     *held, loss = call([mine], held=None, optimizer=None)
     beside, far, *held = lax.optimization_barrier((beside, far, *held))
     both = jnp.stack([mine, beside])
-    near = [lax.ppermute(both, "gz", move(k)) for k in (2, planes - 2)]
+    near = [
+        lax.ppermute(both, "gz", along(lambda x: x ^ 1)),
+        lax.ppermute(both, "gz", along(lambda x: x + 1 if x % 2 else x - 1)),
+    ]
     far_beside = lax.ppermute(far, "gz", swap)
     held = call([beside, far], held=held, optimizer=None)
     first_grads, last_grads, bias_grads, master_new, momentum_new = call(

time: 68.2 us -> 66.1 us (0.969)
  waiting for transfers between devices: 23.4 us -> 20.6 us
  starting transfers between devices: 21.2 us -> 23 us
  local copies, waits for them, and re-layouts: 4.2 us -> 2.5 us
  Pallas kernels: 18.1 us -> 18.8 us
    ppermute x9, waiting for transfers between devices: 13.1 us -> 10.6 us  [the longest x3 4.06 us: exchange(): lax.ppermute(low_face, axis, backward)]
    all_to_all x1, starting transfers between devices: 5.83 us -> 6.98 us  [on_device(): lax.all_to_all(packed.reshape(trainers, capacity, WIDE), ('gx', 'gy'), sp...]
    ppermute x9, starting transfers between devices: 15.1 us -> 16 us  [the longest x3 5.86 us: exchange(): lax.ppermute(high_face, axis, forward)]
    squeeze x2 -> x0, local copies, waits for them, and re-layouts: 0.84 us -> none  [the longest x1 0.84 us: on_device(): xhi = lax.ppermute(velocity[:, 0], 'gx', backward)]
    unnamed x26 -> x22, local copies, waits for them, and re-layouts: 2.87 us -> 2.35 us
    pallas_call x3 -> x5, Pallas kernels: 2.79 us -> 3.29 us  [the longest x1 1.4 us: advance(): pl.pallas_call(advance_kernel, out_shape=(jax.ShapeDtypeStruct(velocity.s...]
  transfers between devices with their start and end apart: 12 -> 12, of which waited for: 10 -> 10; matrix products, arithmetic and copies ran while one was open for 2% -> 0% of each run, Pallas kernels for 12% -> 14%
where the time goes in v1:
time: 66.1 us; the launch traced here: 65.8 us
  starting transfers between devices  23 us (35%)
  waiting for transfers between devices  20.6 us (31%)
  Pallas kernels  18.8 us (28%)
  local copies, waits for them, and re-layouts  2.5 us (4%)
  between operations  0.8 us (1%)
    pallas_call x3, Pallas kernels, train(): pl.pallas_call(functools.partial(train_kernel, planes=planes, row_count=r...  13.2 us
    all_to_all x1, waiting for transfers between devices, on_device(): lax.all_to_all(packed.reshape(trainers, capacity, WIDE), ('gx', 'gy'), sp...  7.57 us
    all_to_all x1, starting transfers between devices, on_device(): lax.all_to_all(packed.reshape(trainers, capacity, WIDE), ('gx', 'gy'), sp...  6.98 us
    ppermute x3, starting transfers between devices, exchange(): lax.ppermute(high_face, axis, forward)  5.86 us
    ppermute x3, starting transfers between devices, exchange(): lax.ppermute(low_face, axis, backward)  5.17 us
    ppermute x3, waiting for transfers between devices, exchange(): lax.ppermute(low_face, axis, backward)  4.06 us
    ppermute x1, starting transfers between devices, on_device(): far = lax.ppermute(mine, 'gz', along(lambda x: x + 2))  2.93 us
    ppermute x3, waiting for transfers between devices, exchange(): lax.ppermute(high_face, axis, forward)  2.58 us
  transfers between devices with their start and end apart: 12, of which 10 were waited for; matrix products, arithmetic and copies ran while one was open for 0% of the time, Pallas kernels for 14%

profile of v1, /device:TPU:32, one launch (start us, length us, event | category | flops | bytes accessed | tf_op | source)
XLA Modules:
  0.0 65.8 jit_solution(11964276617276126027)
XLA Ops:
  0.6 1.0 %copy-done.1 = f32[3,8,32,128]{3,2,1,0:T(8,128)S(1)} copy-done((f32[3,8,32,128]{3,2,1,0:T(8,128)S(1)}, f32[3,8,32,128]{3,2,1,0:T(8,128)}, u32[]{:S(2)}) %copy-start.1) | copy-done | bytes 393240
  1.7 2.9 %collective-permute-start.1 = (f32[3,32,128]{2,1,0:T(8,128)S(1)}, f32[3,32,128]{2,1,0:T(8,128)S(1)}, u32[]{:S(2)}, u32[]{:S(2)}) collective-permute-start(f32[3,32,128]{2,1,0:T(8,128)S(1)} %get-tuple-element.51), channel_id=1, source_target_pairs={{32,0},{64,32},{96,64},{128,96},{160,128},{192,160},{224,192},{0,2... | collective-permute-start | bytes 147464 | tf_op jit(solution)/shard_map/ppermute | solution.py:62
  4.8 1.5 %collective-permute-done.xlo_ref = f32[3,32,128]{2,1,0:T(8,128)S(1)} collective-permute-done((f32[3,32,128]{2,1,0:T(8,128)S(1)}, f32[3,32,128]{2,1,0:T(8,128)S(1)}, u32[]{:S(2)}, u32[]{:S(2)}) %collective-permute-start) | collective-permute-done | bytes 49184 | tf_op jit(solution)/shard_map/ppermute | solution.py:62
  6.4 3.3 %collective-permute-start.2 = (f32[3,16,128]{2,1,0:T(8,128)S(1)}, f32[3,16,128]{2,1,0:T(8,128)S(1)}, u32[]{:S(2)}, u32[]{:S(2)}) collective-permute-start(f32[3,16,128]{2,1,0:T(8,128)S(1)} %get-tuple-element.52), channel_id=1, source_target_pairs={{0,8},{8,16},{16,24},{24,0},{1,9},{9,17},{17,25},{25,1},{2,10},{10... | collective-permute-start | bytes 73736 | tf_op jit(solution)/shard_map/ppermute | solution.py:62
  9.8 2.2 %collective-permute-start.3 = (f32[3,16,128]{2,1,0:T(8,128)S(1)}, f32[3,16,128]{2,1,0:T(8,128)S(1)}, u32[]{:S(2)}, u32[]{:S(2)}) collective-permute-start(f32[3,16,128]{2,1,0:T(8,128)S(1)} %get-tuple-element.53), channel_id=1, source_target_pairs={{8,0},{16,8},{24,16},{0,24},{9,1},{17,9},{25,17},{1,25},{10,2},{18... | collective-permute-start | bytes 73736 | tf_op jit(solution)/shard_map/ppermute | solution.py:62
  12.7 1.0 %collective-permute-done.2.ylo_ref = f32[3,16,128]{2,1,0:T(8,128)S(1)} collective-permute-done((f32[3,16,128]{2,1,0:T(8,128)S(1)}, f32[3,16,128]{2,1,0:T(8,128)S(1)}, u32[]{:S(2)}, u32[]{:S(2)}) %collective-permute-start.2) | collective-permute-done | bytes 24608 | tf_op jit(solution)/shard_map/ppermute | solution.py:62
  13.8 1.4 %collective-permute-done.3.yhi_ref = f32[3,16,128]{2,1,0:T(8,128)S(1)} collective-permute-done((f32[3,16,128]{2,1,0:T(8,128)S(1)}, f32[3,16,128]{2,1,0:T(8,128)S(1)}, u32[]{:S(2)}, u32[]{:S(2)}) %collective-permute-start.3) | collective-permute-done | bytes 24608 | tf_op jit(solution)/shard_map/ppermute | solution.py:62
  15.3 2.5 %collective-permute-start.4 = (f32[48,128]{1,0:T(8,128)S(1)}, f32[48,128]{1,0:T(8,128)S(1)}, u32[]{:S(2)}, u32[]{:S(2)}) collective-permute-start(f32[48,128]{1,0:T(8,128)S(1)} %get-tuple-element.56), channel_id=1, source_target_pairs={{0,1},{1,2},{2,3},{3,4},{4,5},{5,6},{6,7},{7,0},{8,9},{9,10},{10,1... | collective-permute-start | bytes 73736 | tf_op jit(solution)/shard_map/ppermute | solution.py:62
  18.4 1.4 %patches.1.own_ref = f32[96,256]{1,0:T(8,128)S(1)} custom-call(f32[3,8,32,128]{3,2,1,0:T(8,128)S(1)} %copy-done.2, f32[3,32,128]{2,1,0:T(8,128)S(1)} %collective-permute-done.xlo_ref, f32[3,32,128]{2,1,0:T(8,128)S(1)} %collective-permute-done.1.xhi_ref, s32[1,256]{1,0:T(1,128)S(1)} %bitcast.32, f32[48,128]{1,0:T(8,128)S(1)} %get-tuple-element.57.after_ref), custom_call_target="tpu_custom_call" | custom-call | flops 2000000000 | bytes 1000000 | tf_op jit(solution)/shard_map/patches/pallas_call | solution.py:274
  19.8 2.7 %collective-permute-done.5.zhi_ref = f32[48,128]{1,0:T(8,128)S(1)} collective-permute-done((f32[48,128]{1,0:T(8,128)S(1)}, f32[48,128]{1,0:T(8,128)S(1)}, u32[]{:S(2)}, u32[]{:S(2)}) %collective-permute-start.5) | collective-permute-done | bytes 24608 | tf_op jit(solution)/shard_map/ppermute | solution.py:62
  22.5 1.4 %pack.1 = bf16[512,128]{1,0:T(8,128)(2,1)} custom-call(f32[96,256]{1,0:T(8,128)S(1)} %patches.1.own_ref, f32[3,16,128]{2,1,0:T(8,128)S(1)} %collective-permute-done.2.ylo_ref, f32[3,16,128]{2,1,0:T(8,128)S(1)} %collective-permute-done.3.yhi_ref, f32[48,128]{1,0:T(8,128)S(1)} %collective-permute-done.4.zlo_ref, f32[48,128]{1,0:T(8,128)S(1)} %collective-permute-done.5.zhi_ref, ...), custom_call_target="tpu_custom_call" | custom-call | flops 800000000 | bytes 1000000 | tf_op jit(solution)/shard_map/pack/pallas_call | solution.py:363
  23.9 7.0 %all-to-all-start = ((bf16[32,16,128]{2,1,0:T(8,128)(2,1)}), bf16[32,16,128]{2,1,0:T(8,128)(2,1)S(1)}, u32[]{:S(2)}, u32[]{:S(2)}) async-start(bf16[32,16,128]{2,1,0:T(8,128)(2,1)} %bitcast.2), calls=%async_computation | async-start | bytes 262144 | tf_op jit(solution)/shard_map/all_to_all | solution.py:698
  32.0 1.4 %advance.1 = (f32[3,8,32,128]{3,2,1,0:T(8,128)}, f32[8,128]{1,0:T(8,128)S(1)}) custom-call(f32[3,8,32,128]{3,2,1,0:T(8,128)S(1)} %copy-done.2, f32[3,32,128]{2,1,0:T(8,128)S(1)} %collective-permute-done.xlo_ref, f32[3,32,128]{2,1,0:T(8,128)S(1)} %collective-permute-done.1.xhi_ref, f32[3,16,128]{2,1,0:T(8,128)S(1)} %collective-permute-done.2.ylo_ref, ...), custom_call_target="tpu_custom_call" | custom-call | flops 1200000000 | bytes 1000000 | tf_op jit(solution)/shard_map/advance/pallas_call | solution.py:433
  33.4 7.6 %all-to-all-done = bf16[32,16,128]{2,1,0:T(8,128)(2,1)S(1)} async-done(((bf16[32,16,128]{2,1,0:T(8,128)(2,1)}), bf16[32,16,128]{2,1,0:T(8,128)(2,1)S(1)}, u32[]{:S(2)}, u32[]{:S(2)}) %all-to-all-start) | async-done | bytes 131104 | tf_op jit(solution)/shard_map/all_to_all | solution.py:698
  41.2 2.9 %collective-permute-start.7 = (bf16[96,512]{1,0:T(8,128)(2,1)S(1)}, bf16[96,512]{1,0:T(8,128)(2,1)S(1)}, u32[]{:S(2)}, u32[]{:S(2)}) collective-permute-start(bf16[96,512]{1,0:T(8,128)(2,1)S(1)} %turn.1.refs_0_), channel_id=1, source_target_pairs={{0,4},{1,5},{2,6},{3,7},{4,0},{5,1},{6,2},{7,3},{8,12},{9,13},{10,... | collective-permute-start | bytes 294920 | tf_op jit(solution)/shard_map/ppermute | solution.py:719
  44.1 2.0 %train.3 = (f32[512,96]{1,0:T(8,128)S(1)}, f32[64,512]{1,0:T(8,128)S(1)}, f32[16,512]{1,0:T(8,128)S(1)}, f32[512,128]{1,0:T(8,128)S(1)}, f32[512,128]{1,0:T(8,12...) custom-call(bf16[96,512]{1,0:T(8,128)(2,1)S(1)} %turn.1.refs_0_, ...), custom_call_target="tpu_custom_call" | custom-call | flops 1280000000 | bytes 1000000 | tf_op jit(solution)/shard_map/train/pallas_call | solution.py:645
  46.1 2.2 %collective-permute-done.7.refs_1_ = bf16[96,512]{1,0:T(8,128)(2,1)S(1)} collective-permute-done((bf16[96,512]{1,0:T(8,128)(2,1)S(1)}, bf16[96,512]{1,0:T(8,128)(2,1)S(1)}, u32[]{:S(2)}, u32[]{:S(2)}) %collective-permute-start.7) | collective-permute-done | bytes 98336 | tf_op jit(solution)/shard_map/ppermute | solution.py:719
  48.3 0.9 %collective-permute-done.6.refs_0_ = bf16[96,512]{1,0:T(8,128)(2,1)S(1)} collective-permute-done((bf16[96,512]{1,0:T(8,128)(2,1)S(1)}, bf16[96,512]{1,0:T(8,128)(2,1)S(1)}, u32[]{:S(2)}, u32[]{:S(2)}) %collective-permute-start.6) | collective-permute-done | bytes 98336 | tf_op jit(solution)/shard_map/ppermute | solution.py:718
  49.3 2.1 %collective-permute-start.9 = (bf16[2,96,512]{2,1,0:T(8,128)(2,1)S(1)}, bf16[2,96,512]{2,1,0:T(8,128)(2,1)S(1)}, u32[]{:S(2)}, u32[]{:S(2)}) collective-permute-start(bf16[2,96,512]{2,1,0:T(8,128)(2,1)S(1)} %pad_maximum_fusion), channel_id=1, source_target_pairs={{0,6},{1,7},{2,4},{3,5},{4,2},{5,3},{6,0},{7,1},{8,14},{9,15},{10,... | collective-permute-start | bytes 589832 | tf_op jit(solution)/shard_map/ppermute | solution.py:725
  51.3 3.1 %train.4 = (f32[512,96]{1,0:T(8,128)S(1)}, f32[64,512]{1,0:T(8,128)S(1)}, f32[16,512]{1,0:T(8,128)S(1)}, f32[512,128]{1,0:T(8,128)S(1)}, f32[512,128]{1,0:T(8,128)S(1)}, /*index=5*/f32[8,128]{1,0:T(8,128)S(1)}) custom-call(bf16[96,512]{1,0:T(8,128)(2,1)S(1)} %collective-permute-done.6.refs_0_, bf16[96,512]{1,0:T(8,128)(2,1)S(1)} %collective-permute-done.7.refs_1_, ...), custom_call_target="tpu_custom_call" | custom-call | flops 2560000000 | bytes 1000000 | tf_op jit(solution)/shard_map/train/pallas_call | solution.py:645
  54.4 1.6 %collective-permute-done.10.refs_2_ = bf16[96,512]{1,0:T(8,128)(2,1)S(1)} collective-permute-done((bf16[96,512]{1,0:T(8,128)(2,1)S(1)}, bf16[96,512]{1,0:T(8,128)(2,1)S(1)}, u32[]{:S(2)}, u32[]{:S(2)}) %collective-permute-start.10) | collective-permute-done | bytes 98336 | tf_op jit(solution)/shard_map/ppermute | solution.py:727
  55.9 1.0 %collective-permute-done.9.refs_1_ = bf16[2,96,512]{2,1,0:T(8,128)(2,1)S(1)} collective-permute-done((bf16[2,96,512]{2,1,0:T(8,128)(2,1)S(1)}, bf16[2,96,512]{2,1,0:T(8,128)(2,1)S(1)}, u32[]{:S(2)}, u32[]{:S(2)}) %collective-permute-start.9) | collective-permute-done | bytes 196640 | tf_op jit(solution)/shard_map/ppermute | solution.py:725
  56.9 0.8 %collective-permute-done.8.refs_0_ = bf16[2,96,512]{2,1,0:T(8,128)(2,1)S(1)} collective-permute-done((bf16[2,96,512]{2,1,0:T(8,128)(2,1)S(1)}, bf16[2,96,512]{2,1,0:T(8,128)(2,1)S(1)}, u32[]{:S(2)}, u32[]{:S(2)}) %collective-permute-start.8) | collective-permute-done | bytes 196640 | tf_op jit(solution)/shard_map/ppermute | solution.py:724
  57.7 8.1 %train.5 = (f32[81,1,512]{2,1,0:T(1,128)}, f32[6,1,512]{2,1,0:T(1,128)}, f32[1,1030]{1,0:T(1,128)}, f32[256,128]{1,0:T(8,128)}, f32[256,128]{1,0:T(8,128)}) custom-call(bf16[2,96,512]{2,1,0:T(8,128)(2,1)S(1)} %collective-permute-done.8.refs_0_, bf16[2,96,512]{2,1,0:T(8,128)(2,1)S(1)} %collective-permute-done.9.refs_1_, ...), custom_call_target="tpu_custom_call" | custom-call | flops 6400000000 | bytes 1000000 | tf_op jit(solution)/shard_map/train/pallas_call | solution.py:645
  (39 shorter events, 3.2 us)
Async XLA Ops:
  0.6 1.0 %copy-start.1 = (f32[3,8,32,128]{3,2,1,0:T(8,128)S(1)}, f32[3,8,32,128]{3,2,1,0:T(8,128)}, u32[]{:S(2)}) copy-start(f32[3,8,32,128]{3,2,1,0:T(8,128)} %v_ref.5) | copy-start | bytes 1179652
  1.6 4.7 %collective-permute-start = (f32[3,32,128]{2,1,0:T(8,128)S(1)}, f32[3,32,128]{2,1,0:T(8,128)S(1)}, u32[]{:S(2)}, u32[]{:S(2)}) collective-permute-start(f32[3,32,128]{2,1,0:T(8,128)S(1)} %get-tuple-element.50), channel_id=1, source_target_pairs={{0,32},{32,64},{64,96},{96,128},{128,160},{160,192},{192,224},{224... | collective-permute-start | bytes 147464 | tf_op jit(solution)/shard_map/ppermute | solution.py:62
  1.7 3.1 %copy-start.10 = (bf16[6,256]{1,0:T(8,128)(2,1)S(1)}, bf16[6,256]{1,0:T(8,128)(2,1)}, u32[]{:S(2)}) copy-start(bf16[6,256]{1,0:T(8,128)(2,1)} %param.13) | copy-start | bytes 9220
  1.7 4.7 %collective-permute-start.1 = (f32[3,32,128]{2,1,0:T(8,128)S(1)}, f32[3,32,128]{2,1,0:T(8,128)S(1)}, u32[]{:S(2)}, u32[]{:S(2)}) collective-permute-start(f32[3,32,128]{2,1,0:T(8,128)S(1)} %get-tuple-element.51), channel_id=1, source_target_pairs={{32,0},{64,32},{96,64},{128,96},{160,128},{192,160},{224,192},{0,2... | collective-permute-start | bytes 147464 | tf_op jit(solution)/shard_map/ppermute | solution.py:62
  6.4 7.3 %collective-permute-start.2 = (f32[3,16,128]{2,1,0:T(8,128)S(1)}, f32[3,16,128]{2,1,0:T(8,128)S(1)}, u32[]{:S(2)}, u32[]{:S(2)}) collective-permute-start(f32[3,16,128]{2,1,0:T(8,128)S(1)} %get-tuple-element.52), channel_id=1, source_target_pairs={{0,8},{8,16},{16,24},{24,0},{1,9},{9,17},{17,25},{25,1},{2,10},{10... | collective-permute-start | bytes 73736 | tf_op jit(solution)/shard_map/ppermute | solution.py:62
  9.8 2.2 %copy-start.8 = (s32[256,1]{0,1:T(1,128)S(1)}, s32[256,1]{0,1:T(1,128)}, u32[]{:S(2)}) copy-start(s32[256,1]{0,1:T(1,128)} %param.12) | copy-start | bytes 3076
  9.8 5.4 %collective-permute-start.3 = (f32[3,16,128]{2,1,0:T(8,128)S(1)}, f32[3,16,128]{2,1,0:T(8,128)S(1)}, u32[]{:S(2)}, u32[]{:S(2)}) collective-permute-start(f32[3,16,128]{2,1,0:T(8,128)S(1)} %get-tuple-element.53), channel_id=1, source_target_pairs={{8,0},{16,8},{24,16},{0,24},{9,1},{17,9},{25,17},{1,25},{10,2},{18... | collective-permute-start | bytes 73736 | tf_op jit(solution)/shard_map/ppermute | solution.py:62
  15.2 2.6 %copy-start.2 = (f32[3,8,32,128]{3,2,1,0:T(8,128)S(1)}, f32[3,8,32,128]{3,2,1,0:T(8,128)}, u32[]{:S(2)}) copy-start(f32[3,8,32,128]{3,2,1,0:T(8,128)} %v_ref.5) | copy-start | bytes 1179652
  15.3 4.6 %collective-permute-start.4 = (f32[48,128]{1,0:T(8,128)S(1)}, f32[48,128]{1,0:T(8,128)S(1)}, u32[]{:S(2)}, u32[]{:S(2)}) collective-permute-start(f32[48,128]{1,0:T(8,128)S(1)} %get-tuple-element.56), channel_id=1, source_target_pairs={{0,1},{1,2},{2,3},{3,4},{4,5},{5,6},{6,7},{7,0},{8,9},{9,10},{10,1... | collective-permute-start | bytes 73736 | tf_op jit(solution)/shard_map/ppermute | solution.py:62
  17.8 0.7 %copy-start.9 = (s32[256]{0:T(256)S(1)}, s32[256]{0:T(256)}, u32[]{:S(2)}) copy-start(s32[256]{0:T(256)} %param.11) | copy-start | bytes 3076
  17.8 4.7 %collective-permute-start.5 = (f32[48,128]{1,0:T(8,128)S(1)}, f32[48,128]{1,0:T(8,128)S(1)}, u32[]{:S(2)}, u32[]{:S(2)}) collective-permute-start(f32[48,128]{1,0:T(8,128)S(1)} %get-tuple-element.57.after_ref), channel_id=1, source_target_pairs={{1,0},{2,1},{3,2},{4,3},{5,4},{6,5},{7,6},{0,7},{9,8},{10,9},{11,1... | collective-permute-start | bytes 73736 | tf_op jit(solution)/shard_map/ppermute | solution.py:62
  22.5 8.4 %copy-start = (bf16[1,512,512]{2,1,0:T(8,128)(2,1)S(1)}, bf16[1,512,512]{2,1,0:T(8,128)(2,1)}, u32[]{:S(2)}) copy-start(bf16[1,512,512]{2,1,0:T(8,128)(2,1)} %param.15) | copy-start | bytes 1572868
  23.9 7.0 %copy-start.5 = (bf16[1,512,81]{1,2,0:T(8,128)(2,1)S(1)}, bf16[1,512,81]{1,2,0:T(8,128)(2,1)}, u32[]{:S(2)}) copy-start(bf16[1,512,81]{1,2,0:T(8,128)(2,1)} %param.14) | copy-start | bytes 248836
  23.9 7.0 %copy-start.6 = (bf16[1,6,512]{2,1,0:T(8,128)(2,1)S(1)}, bf16[1,6,512]{2,1,0:T(8,128)(2,1)}, u32[]{:S(2)}) copy-start(bf16[1,6,512]{2,1,0:T(8,128)(2,1)} %param.16) | copy-start | bytes 18436
  23.9 17.1 %all-to-all-start = ((bf16[32,16,128]{2,1,0:T(8,128)(2,1)}), bf16[32,16,128]{2,1,0:T(8,128)(2,1)S(1)}, u32[]{:S(2)}, u32[]{:S(2)}) async-start(bf16[32,16,128]{2,1,0:T(8,128)(2,1)} %bitcast.2), calls=%async_computation | async-start | bytes 262144 | tf_op jit(solution)/shard_map/all_to_all | solution.py:698
  30.9 0.7 %copy-start.7 = (f32[1,1030]{1,0:T(1,128)S(1)}, f32[1,1030]{1,0:T(1,128)}, u32[]{:S(2)}) copy-start(f32[1,1030]{1,0:T(1,128)} %biases_ref.1) | copy-start | bytes 12364
  41.2 7.1 %collective-permute-start.7 = (bf16[96,512]{1,0:T(8,128)(2,1)S(1)}, bf16[96,512]{1,0:T(8,128)(2,1)S(1)}, u32[]{:S(2)}, u32[]{:S(2)}) collective-permute-start(bf16[96,512]{1,0:T(8,128)(2,1)S(1)} %turn.1.refs_0_), channel_id=1, source_target_pairs={{0,4},{1,5},{2,6},{3,7},{4,0},{5,1},{6,2},{7,3},{8,12},{9,13},{10,... | collective-permute-start | bytes 294920 | tf_op jit(solution)/shard_map/ppermute | solution.py:719
  44.1 5.1 %collective-permute-start.6 = (bf16[96,512]{1,0:T(8,128)(2,1)S(1)}, bf16[96,512]{1,0:T(8,128)(2,1)S(1)}, u32[]{:S(2)}, u32[]{:S(2)}) collective-permute-start(bf16[96,512]{1,0:T(8,128)(2,1)S(1)} %turn.1.refs_0_), channel_id=1, source_target_pairs={{0,1},{1,0},{2,3},{3,2},{4,5},{5,4},{6,7},{7,6},{8,9},{9,8},{10,11... | collective-permute-start | bytes 294920 | tf_op jit(solution)/shard_map/ppermute | solution.py:718
  49.2 8.4 %copy-start.3 = (f32[1,32768]{1,0:T(1,128)S(1)}, f32[1,32768]{1,0:T(1,128)}, u32[]{:S(2)}) copy-start(f32[1,32768]{1,0:T(1,128)} %param.19) | copy-start | bytes 393220
  49.2 8.4 %copy-start.4 = (f32[1,32768]{1,0:T(1,128)S(1)}, f32[1,32768]{1,0:T(1,128)}, u32[]{:S(2)}) copy-start(f32[1,32768]{1,0:T(1,128)} %param.18) | copy-start | bytes 393220
  49.3 7.7 %collective-permute-start.9 = (bf16[2,96,512]{2,1,0:T(8,128)(2,1)S(1)}, bf16[2,96,512]{2,1,0:T(8,128)(2,1)S(1)}, u32[]{:S(2)}, u32[]{:S(2)}) collective-permute-start(bf16[2,96,512]{2,1,0:T(8,128)(2,1)S(1)} %pad_maximum_fusion), channel_id=1, source_target_pairs={{0,6},{1,7},{2,4},{3,5},{4,2},{5,3},{6,0},{7,1},{8,14},{9,15},{10,... | collective-permute-start | bytes 589832 | tf_op jit(solution)/shard_map/ppermute | solution.py:725
  51.3 6.4 %collective-permute-start.8 = (bf16[2,96,512]{2,1,0:T(8,128)(2,1)S(1)}, bf16[2,96,512]{2,1,0:T(8,128)(2,1)S(1)}, u32[]{:S(2)}, u32[]{:S(2)}) collective-permute-start(bf16[2,96,512]{2,1,0:T(8,128)(2,1)S(1)} %pad_maximum_fusion), channel_id=1, source_target_pairs={{0,2},{1,3},{2,0},{3,1},{4,6},{5,7},{6,4},{7,5},{8,10},{9,11},{10,... | collective-permute-start | bytes 589832 | tf_op jit(solution)/shard_map/ppermute | solution.py:724
  51.3 4.6 %collective-permute-start.10 = (bf16[96,512]{1,0:T(8,128)(2,1)S(1)}, bf16[96,512]{1,0:T(8,128)(2,1)S(1)}, u32[]{:S(2)}, u32[]{:S(2)}) collective-permute-start(bf16[96,512]{1,0:T(8,128)(2,1)S(1)} %collective-permute-done.7.refs_1_), channel_id=1, source_target_pairs={{0,1},{1,0},{2,3},{3,2},{4,5},{5,4},{6,7},{7,6},{8,9},{9,8},{10,11... | collective-permute-start | bytes 294920 | tf_op jit(solution)/shard_map/ppermute | solution.py:727

commit v2 on v1

--- a/solution.py
+++ b/solution.py
@@ -96,8 +96,58 @@
         high_ref[at : at + 1, 1 : size_y + 1] = ends[1:2, k * size_y : (k + 1) * size_y]
 
 
+def split_cells(cells, size_x, size_y, size_z):
+    return cells // (size_y * size_z), cells // size_z % size_y, cells % size_z
+
+
+def depth_choice(cell_z, size_z):
+    depth = iota((size_z, cell_z.shape[1]), 0)
+    return jnp.concatenate([ones_where(depth == cell_z + (r - 1)) for r in range(3)], axis=1)
+
+
+def fold(ref, first, rows, masks, samples):
+    sums = [None] * 3
+    for k in range(rows // 8):
+        for r in range(3):
+            piece = ref[first + 8 * k : first + 8 * k + 8, r * samples : (r + 1) * samples]
+            piece = jnp.where(masks[k], piece, 0.0)
+            sums[r] = piece if sums[r] is None else sums[r] + piece
+    return sums
+
+
+def feature(c, p, q, r):
+    return 27 * c + 9 * p + 3 * q + r
+
+
+def tile_sums(feats):
+    shape = (ROWS, feats * 8)
+    return ones_where(lax.shift_right_logical(iota(shape, 1), 3) == iota(shape, 0))
+
+
+def put_tile(parts, f, total):
+    parts[f * 8 : (f + 1) * 8, :] = jnp.zeros((8, parts.shape[1]), F32) if total is None else total
+
+
+def add_tiles(summing, parts):
+    return jnp.dot(summing[...], parts[...].astype(BF16), preferred_element_type=F32)
+
+
 def plan_kernel(
-    v_ref, xlo_ref, xhi_ref, trainer_ref, z_low_ref, z_high_ref, placing_ref, *, trainers
+    v_ref,
+    xlo_ref,
+    xhi_ref,
+    info_ref,
+    own_ref,
+    choose_ref,
+    summing_ref,
+    z_low_ref,
+    z_high_ref,
+    placing_ref,
+    out_ref,
+    picked,
+    parts,
+    *,
+    trainers,
 ):
     comps, size_x, size_y, size_z = v_ref.shape
     for ref in (z_low_ref, z_high_ref):
@@ -113,9 +163,26 @@
     for ref, scale, x in ((xlo_ref, before, 0), (xhi_ref, after, size_x + 1)):
         block = ref[...].reshape(-1, size_z) * scale
         end_rows(block, z_low_ref, z_high_ref, lambda k: k * PAD_X + x, size_y)
-
-    trainer = trainer_ref[...]
-    samples = trainer.shape[1]
+        first = 0 if x == 0 else block.shape[0]
+        picked[first : first + block.shape[0], :] = jnp.dot(
+            block.astype(BF16), choose_ref[...], preferred_element_type=F32
+        )
+    samples = info_ref.shape[1]
+    cell_x, cell_y, _ = split_cells(info_ref[0:1, :], size_x, size_y, size_z)
+    sub = iota((8, samples), 0)
+    for side, at in ((0, cell_x == 0), (1, cell_x == size_x - 1)):
+        edge_y = jnp.where(at, cell_y, -100)
+        for c in range(comps):
+            for q in range(3):
+                masks = [sub + (8 * k - q + 1) == edge_y for k in range(size_y // 8)]
+                sums = fold(picked, (side * comps + c) * size_y, size_y, masks, samples)
+                for r in range(3):
+                    put_tile(parts, feature(c, 2 * side, q, r), sums[r])
+                    if side == 0:
+                        put_tile(parts, feature(c, 1, q, r), None)
+    out_ref[...] = own_ref[...] + add_tiles(summing_ref, parts)
+
+    trainer = info_ref[1:2, :]
     slots = placing_ref.shape[0]
     capacity = slots // trainers
     same = iota((trainers, samples), 0) == trainer
@@ -126,22 +193,26 @@
     placing_ref[...] = ones_where(iota((slots, samples), 0) == slot)
 
 
-def plan(velocity, x_halos, trainer, trainers, slots):
+def plan(velocity, x_halos, info, own, choose, summing, trainers, slots):
     comps, size_x, size_y, size_z = velocity.shape
     z_face = jax.ShapeDtypeStruct((comps * PAD_X, WIDE), F32)
-    placing = jax.ShapeDtypeStruct((slots, trainer.shape[1]), BF16)
+    placing = jax.ShapeDtypeStruct((slots, info.shape[1]), BF16)
     return pl.pallas_call(
         functools.partial(plan_kernel, trainers=trainers),
-        out_shape=(z_face, z_face, placing),
-        in_specs=whole(4),
-        out_specs=tuple(whole(3)),
+        out_shape=(z_face, z_face, placing, jax.ShapeDtypeStruct(own.shape, F32)),
+        in_specs=whole(7),
+        out_specs=tuple(whole(4)),
+        scratch_shapes=[
+            pltpu.VMEM((2 * comps * size_y, choose.shape[1]), F32),
+            pltpu.VMEM((summing.shape[1], own.shape[1]), F32),
+        ],
         compiler_params=params(),
         cost_estimate=cost(1.5),
         name="plan",
-    )(velocity, *x_halos, trainer)
-
-
-def y_faces_kernel(low_ref, high_ref, xlo_ref, xhi_ref, to_low_ref, to_high_ref):
+    )(velocity, *x_halos, info, own, choose, summing)
+
+
+def y_faces_kernel(low_ref, high_ref, xlo_ref, xhi_ref, after_ref, to_low_ref, to_high_ref):
     comps, size_x = low_ref.shape[0], low_ref.shape[1]
     before, after = inside("gx")
     last = xlo_ref.shape[1] - 1
@@ -154,7 +225,7 @@
             to[c, size_x + 1 : size_x + 2, :] = xhi_ref[c, y : y + 1, :] * after
 
 
-def y_faces(velocity, x_halos):
+def y_faces(velocity, x_halos, after):
     comps, size_x, size_y, size_z = velocity.shape
     shape = (comps, PAD_X, size_z)
     spec = lambda at: pl.BlockSpec((comps, size_x, 8, size_z), lambda i: (0, 0, at, 0))
@@ -163,12 +234,12 @@
         y_faces_kernel,
         grid=(1,),
         out_shape=tuple([jax.ShapeDtypeStruct(shape, F32)] * 2),
-        in_specs=[spec(0), spec(size_y // 8 - 1)] + [full(x_halos[0].shape)] * 2,
+        in_specs=[spec(0), spec(size_y // 8 - 1)] + [full(x_halos[0].shape)] * 2 + [full(after.shape)],
         out_specs=(full(shape), full(shape)),
         compiler_params=params(),
         cost_estimate=cost(0.3),
         name="y_faces",
-    )(velocity, velocity, *x_halos)
+    )(velocity, velocity, *x_halos, after)
 
 
 def z_faces_kernel(low_ref, high_ref, ylo_ref, yhi_ref, to_low_ref, to_high_ref, *, size_y):
@@ -194,161 +265,132 @@
     )(low, high, *y_halos)
 
 
-def split_cells(cells, size_x, size_y, size_z):
-    return cells // (size_y * size_z), cells // size_z % size_y, cells % size_z
-
-
-def depth_choice(cell_z, size_z):
-    depth = iota((size_z, cell_z.shape[1]), 0)
-    return jnp.concatenate([ones_where(depth == cell_z + (r - 1)) for r in range(3)], axis=1)
-
-
-def fold(ref, first, rows, masks, samples):
-    sums = [None] * 3
-    for k in range(rows // 8):
-        for r in range(3):
-            piece = ref[first + 8 * k : first + 8 * k + 8, r * samples : (r + 1) * samples]
-            piece = jnp.where(masks[k], piece, 0.0)
-            sums[r] = piece if sums[r] is None else sums[r] + piece
-    return sums
-
-
-def feature(c, p, q, r):
-    return 27 * c + 9 * p + 3 * q + r
-
-
-def add_tiles(parts, feats):
-    shape = (ROWS, feats * 8)
-    gather = ones_where(lax.shift_right_logical(iota(shape, 1), 3) == iota(shape, 0))
-    return jnp.dot(gather, parts[...].astype(BF16), preferred_element_type=F32)
-
-
-def patch_kernel(
-    v_ref, xlo_ref, xhi_ref, cells_ref, after_ref, out_ref, picked, parts
-):
+def patch_kernel(v_ref, info_ref, out_ref, choose_ref, summing_ref, picked, parts):
     comps, size_x, size_y, size_z = v_ref.shape
-    samples = cells_ref.shape[1]
-    before, after = inside("gx")
-    cell_x, cell_y, cell_z = split_cells(cells_ref[...], size_x, size_y, size_z)
-    choose = depth_choice(cell_z, size_z)
-    starts, start = [], 0
-    for ref, scale in ((v_ref, None), (xlo_ref, before), (xhi_ref, after)):
-        block = ref[...].reshape(-1, size_z)
-        if scale is not None:
-            block = block * scale
-        picked[start : start + block.shape[0], :] = jnp.dot(
-            block.astype(BF16), choose, preferred_element_type=F32
-        )
-        starts.append(start)
-        start += block.shape[0]
+    samples = info_ref.shape[1]
+    cell_x, cell_y, cell_z = split_cells(info_ref[0:1, :], size_x, size_y, size_z)
+    choose_ref[...] = depth_choice(cell_z, size_z)
+    picked[...] = jnp.dot(
+        v_ref[...].reshape(-1, size_z).astype(BF16), choose_ref[...], preferred_element_type=F32
+    )
     sub = iota((8, samples), 0)
     at_x = [cell_x == j for j in range(size_x)]
     for c in range(comps):
         for q in range(3):
             masks = [sub + (8 * k - q + 1) == cell_y for k in range(size_y // 8)]
             totals = [[None] * 3 for _ in range(3)]
-            for x in range(size_x + 2):
-                if x == 0:
-                    first = starts[1] + c * size_y
-                elif x == size_x + 1:
-                    first = starts[2] + c * size_y
-                else:
-                    first = (c * size_x + x - 1) * size_y
-                sums = fold(picked, first, size_y, masks, samples)
+            for x in range(size_x):
+                sums = fold(picked, (c * size_x + x) * size_y, size_y, masks, samples)
                 for p in range(3):
-                    j = x - p
+                    j = x + 1 - p
                     if 0 <= j < size_x:
                         for r in range(3):
                             piece = jnp.where(at_x[j], sums[r], 0.0)
                             totals[p][r] = piece if totals[p][r] is None else totals[p][r] + piece
             for p in range(3):
                 for r in range(3):
-                    f = feature(c, p, q, r)
-                    parts[f * 8 : (f + 1) * 8, :] = totals[p][r]
-    out_ref[...] = add_tiles(parts, 27 * comps)
-
-
-def patches(velocity, x_halos, cells, after):
+                    put_tile(parts, feature(c, p, q, r), totals[p][r])
+    summing_ref[...] = tile_sums(27 * comps)
+    out_ref[...] = add_tiles(summing_ref, parts)
+
+
+def patches(velocity, cells):
     comps, size_x, size_y, size_z = velocity.shape
     samples = cells.shape[1]
+    feats = 27 * comps
     return pl.pallas_call(
         patch_kernel,
-        out_shape=jax.ShapeDtypeStruct((ROWS, samples), F32),
-        in_specs=whole(5),
-        out_specs=pl.BlockSpec(memory_space=pltpu.VMEM),
+        out_shape=(
+            jax.ShapeDtypeStruct((ROWS, samples), F32),
+            jax.ShapeDtypeStruct((size_z, 3 * samples), BF16),
+            jax.ShapeDtypeStruct((ROWS, feats * 8), BF16),
+        ),
+        in_specs=whole(2),
+        out_specs=tuple(whole(3)),
         scratch_shapes=[
-            pltpu.VMEM((comps * (size_x + 2) * size_y, 3 * samples), F32),
-            pltpu.VMEM((27 * comps * 8, samples), F32),
+            pltpu.VMEM((comps * size_x * size_y, 3 * samples), F32),
+            pltpu.VMEM((feats * 8, samples), F32),
         ],
         compiler_params=params(),
-        cost_estimate=cost(2.5),
+        cost_estimate=cost(1.2),
         name="patches",
-    )(velocity, *x_halos, cells, after)
-
-
-def pack_kernel(
-    own_ref,
-    ylo_ref,
-    yhi_ref,
-    zlo_ref,
-    zhi_ref,
-    cells_ref,
-    tail_ref,
-    placing_ref,
-    out_ref,
-    picked,
-    parts,
-    *,
-    size_x,
-    size_y,
+    )(velocity, cells)
+
+
+def edge_kernel(
+    own_ref, ylo_ref, yhi_ref, info_ref, choose_ref, summing_ref, after_ref, out_ref, rows_ref,
+    picked, parts, *, size_x, size_y
 ):
     comps, pad_x, size_z = ylo_ref.shape
-    samples = cells_ref.shape[1]
+    samples = info_ref.shape[1]
     rows = comps * pad_x
-    cell_x, cell_y, cell_z = split_cells(cells_ref[...], size_x, size_y, size_z)
-    y_before, y_after = inside("gy")
-    z_before, z_after = inside("gz")
-
-    choose = depth_choice(cell_z, size_z)
-    along_y = jnp.concatenate(
-        [ylo_ref[...].reshape(rows, size_z) * y_before, yhi_ref[...].reshape(rows, size_z) * y_after],
+    cell_x, cell_y, _ = split_cells(info_ref[0:1, :], size_x, size_y, size_z)
+    before, after = inside("gy")
+    along = jnp.concatenate(
+        [ylo_ref[...].reshape(rows, size_z) * before, yhi_ref[...].reshape(rows, size_z) * after],
         axis=0,
     ).astype(BF16)
-    picked[: 2 * rows, :] = jnp.dot(along_y, choose, preferred_element_type=F32)
+    picked[...] = jnp.dot(along, choose_ref[...], preferred_element_type=F32)
+    sub = iota((8, samples), 0)
+    for side, at in ((0, cell_y == 0), (1, cell_y == size_y - 1)):
+        edge_x = jnp.where(at, cell_x, -100)
+        for c in range(comps):
+            for p in range(3):
+                masks = [sub + (8 * k - p) == edge_x for k in range(pad_x // 8)]
+                sums = fold(picked, side * rows + c * pad_x, pad_x, masks, samples)
+                for r in range(3):
+                    put_tile(parts, feature(c, p, 2 * side, r), sums[r])
+                    if side == 0:
+                        put_tile(parts, feature(c, p, 1, r), None)
+    out_ref[...] = own_ref[...] + add_tiles(summing_ref, parts)
     width = iota((WIDE, samples), 0)
-    choose = jnp.concatenate([ones_where(width == cell_y + q) for q in range(3)], axis=1)
-    along_z = jnp.concatenate([zlo_ref[...] * z_before, zhi_ref[...] * z_after], axis=0).astype(BF16)
-    picked[2 * rows :, :] = jnp.dot(along_z, choose, preferred_element_type=F32)
-
+    rows_ref[...] = jnp.concatenate([ones_where(width == cell_y + q) for q in range(3)], axis=1)
+
+
+def edges(own, y_halos, cells, choose, summing, after, size_x, size_y):
+    samples = cells.shape[1]
+    comps, pad_x, _ = y_halos[0].shape
+    return pl.pallas_call(
+        functools.partial(edge_kernel, size_x=size_x, size_y=size_y),
+        out_shape=(
+            jax.ShapeDtypeStruct(own.shape, F32),
+            jax.ShapeDtypeStruct((WIDE, 3 * samples), BF16),
+        ),
+        in_specs=whole(7),
+        out_specs=tuple(whole(2)),
+        scratch_shapes=[
+            pltpu.VMEM((2 * comps * pad_x, 3 * samples), F32),
+            pltpu.VMEM((summing.shape[1], samples), F32),
+        ],
+        compiler_params=params(),
+        cost_estimate=cost(0.6),
+        name="edges",
+    )(own, *y_halos, cells, choose, summing, after)
+
+
+def pack_kernel(
+    own_ref, zlo_ref, zhi_ref, info_ref, rows_ref, summing_ref, tail_ref, placing_ref, out_ref,
+    picked, parts, *, comps, sizes
+):
+    samples = info_ref.shape[1]
+    rows = zlo_ref.shape[0]
+    pad_x = rows // comps
+    cell_x, _, cell_z = split_cells(info_ref[0:1, :], *sizes)
+    before, after = inside("gz")
+    along = jnp.concatenate([zlo_ref[...] * before, zhi_ref[...] * after], axis=0).astype(BF16)
+    picked[...] = jnp.dot(along, rows_ref[...], preferred_element_type=F32)
     sub = iota((8, samples), 0)
-    at_edge = [cell_y == 0, cell_y == size_y - 1, cell_z == 0, cell_z == size_z - 1]
-    edge_x = [jnp.where(at, cell_x, -100) for at in at_edge]
-    for c in range(comps):
-        for p in range(3):
-            sums = [
-                fold(
-                    picked,
-                    e * rows + c * pad_x,
-                    pad_x,
-                    [sub + (8 * k - p) == edge_x[e] for k in range(pad_x // 8)],
-                    samples,
-                )
-                for e in range(4)
-            ]
-            for q in range(3):
-                for r in range(3):
-                    terms = []
-                    if q != 1:
-                        terms.append(sums[q // 2][r])
-                    if r != 1:
-                        terms.append(sums[2 + r // 2][q])
-                    total = terms[0] if terms else jnp.zeros((8, samples), F32)
-                    if len(terms) > 1:
-                        total = total + terms[1]
-                    f = feature(c, p, q, r)
-                    parts[f * 8 : (f + 1) * 8, :] = total
-
-    features = own_ref[...] + add_tiles(parts, 27 * comps)
+    for side, at in ((0, cell_z == 0), (1, cell_z == sizes[2] - 1)):
+        edge_x = jnp.where(at, cell_x, -100)
+        for c in range(comps):
+            for p in range(3):
+                masks = [sub + (8 * k - p) == edge_x for k in range(pad_x // 8)]
+                sums = fold(picked, side * rows + c * pad_x, pad_x, masks, samples)
+                for q in range(3):
+                    put_tile(parts, feature(c, p, q, 2 * side), sums[q])
+                    if side == 0:
+                        put_tile(parts, feature(c, p, q, 1), None)
+    features = own_ref[...] + add_tiles(summing_ref, parts)
     payload = jnp.concatenate(
         [features[:TAIL], tail_ref[...], jnp.zeros((WIDE - ROWS, samples), F32)], axis=0
     ).astype(BF16)
@@ -357,22 +399,21 @@
     ).astype(BF16)
 
 
-def pack(own, y_halos, z_halos, cells, tail, placing, size_x, size_y):
+def pack(own, z_halos, cells, rows, summing, tail, placing, comps, sizes):
     samples = cells.shape[1]
-    comps, pad_x, _ = y_halos[0].shape
-    return pl.pallas_call(
-        functools.partial(pack_kernel, size_x=size_x, size_y=size_y),
+    return pl.pallas_call(
+        functools.partial(pack_kernel, comps=comps, sizes=sizes),
         out_shape=jax.ShapeDtypeStruct((placing.shape[0], WIDE), BF16),
         in_specs=whole(8),
         out_specs=pl.BlockSpec(memory_space=pltpu.VMEM),
         scratch_shapes=[
-            pltpu.VMEM((4 * comps * pad_x, 3 * samples), F32),
-            pltpu.VMEM((27 * comps * 8, samples), F32),
+            pltpu.VMEM((2 * z_halos[0].shape[0], 3 * samples), F32),
+            pltpu.VMEM((summing.shape[1], samples), F32),
         ],
         compiler_params=params(),
-        cost_estimate=cost(1.0),
+        cost_estimate=cost(0.7),
         name="pack",
-    )(own, *y_halos, *z_halos, cells, tail, placing)
+    )(own, *z_halos, cells, rows, summing, tail, placing)
 
 
 def advance_kernel(
@@ -542,6 +583,22 @@
 
     own = pl.multiple_of(lax.axis_index("gz") * own_rows, own_rows)
 
+    per_row = hidden // WIDE
+    across = lambda s: jnp.sum(s.T, axis=0, keepdims=True)
+
+    def finish_early():
+        grads = g2[...]
+        for k in range(per_row):
+            at = pl.ds(k, own_rows, stride=per_row)
+            momentum = MOMENTUM_KEEP * momentum_ref[at, :] + grads[:, k * WIDE : (k + 1) * WIDE]
+            momentum_new_ref[at, :] = momentum
+            master_new_ref[at, :] = master_ref[at, :] - LEARN_RATE * momentum
+        for k in range(last_ref.shape[0]):
+            last_ref[k] = g3[k : k + 1, :]
+        bias_grads_ref[:, hidden : 2 * hidden] = across(s2[...])
+        third = across(jnp.concatenate([s3[...], jnp.zeros((WIDE - 8, WIDE), F32)], axis=0))
+        bias_grads_ref[:, 2 * hidden :] = third[:, :6]
+
     def plane(x):
         slots = x.shape[1]
         reps = slots // WIDE
@@ -559,6 +616,7 @@
             iota((8, slots), 0) < 6, (predicted - ending) * ending[6:7, :], 0.0
         )
         delta_three = mismatch * factor
+        add(s3, lane_sum(delta_three))
         back_three = jnp.concatenate([delta_three, jnp.zeros_like(delta_three)], axis=0).astype(BF16)
         add(g3, lax.dot_general(back_three, act_two, NT, preferred_element_type=F32))
         wide_two = act_two.astype(F32)
@@ -570,6 +628,8 @@
         back_two_ref[...] = back_two
         mine = back_two_ref[pl.ds(own, own_rows), :]
         add(g2, lax.dot_general(mine, act_one, NT, preferred_element_type=F32))
+        if last:
+            finish_early()
         wide_one = act_one.astype(F32)
         delta_one = jnp.dot(w2t_ref[...], back_two, preferred_element_type=F32) * (
             1.0 - wide_one * wide_one
@@ -577,7 +637,6 @@
         add(s1, lane_sum(delta_one))
         back_one = delta_one.astype(BF16)
         add(g1, lax.dot_general(back_one, x, NT, preferred_element_type=F32))
-        add(s3, lane_sum(delta_three))
         return mismatch
 
     pieces = []
@@ -589,22 +648,10 @@
         row_loss = jnp.sum(mismatch * mismatch, axis=0, keepdims=True) / (6.0 * row_count)
         loss_ref[...] = jnp.sum(row_loss, axis=1, keepdims=True)
     if last:
-        per_row = hidden // WIDE
-        wide = jnp.concatenate([g1[...], jnp.zeros((hidden, WIDE - ROWS), F32)], axis=1)
-        for ref, grads in ((first_ref, wide.T), (last_ref, g3[...])):
-            for k in range(ref.shape[0]):
-                ref[k] = grads[k : k + 1, :]
-        across = lambda s: jnp.sum(s.T, axis=0, keepdims=True)
+        wide = jnp.concatenate([g1[...], jnp.zeros((hidden, WIDE - ROWS), F32)], axis=1).T
+        for k in range(first_ref.shape[0]):
+            first_ref[k] = wide[k : k + 1, :]
         bias_grads_ref[:, :hidden] = across(s1[...])
-        bias_grads_ref[:, hidden : 2 * hidden] = across(s2[...])
-        third = across(jnp.concatenate([s3[...], jnp.zeros((WIDE - 8, WIDE), F32)], axis=0))
-        bias_grads_ref[:, 2 * hidden :] = third[:, :6]
-        grads = g2[...]
-        for k in range(per_row):
-            at = pl.ds(k, own_rows, stride=per_row)
-            momentum = MOMENTUM_KEEP * momentum_ref[at, :] + grads[:, k * WIDE : (k + 1) * WIDE]
-            momentum_new_ref[at, :] = momentum
-            master_new_ref[at, :] = master_ref[at, :] - LEARN_RATE * momentum
 
 
 def train(xs, weights, held, optimizer, row_count, own_rows):
@@ -682,19 +729,29 @@
     planes = lax.axis_size("gz")
     own_rows = hidden // planes
 
-    cells = sample_cells.reshape(1, samples)
+    info = jnp.stack([sample_cells, trainer_of[:, 0]])
     x_halos = exchange("gx", *x_faces(velocity))
-    y_halos = exchange("gy", *y_faces(velocity, x_halos))
-    z_low, z_high, placing = plan(
-        velocity, x_halos, trainer_of.reshape(1, samples), trainers, slots
+    features, choose, summing = patches(velocity, info)
+    y_halos = exchange("gy", *y_faces(velocity, x_halos, features))
+    z_low, z_high, placing, features = plan(
+        velocity,
+        x_halos,
+        info,
+        features,
+        choose,
+        summing,
+        trainers,
+        slots,
     )
     z_ends = z_faces(z_low, z_high, y_halos, size_y)
     z_halos = exchange("gz", *z_ends)
-    features = patches(velocity, x_halos, cells, z_ends[0])
+    features, rows = edges(features, y_halos, info, choose, summing, z_ends[0], size_x, size_y)
     tail = jnp.concatenate(
         [targets.astype(F32), jnp.ones((1, samples), F32), jnp.zeros((1, samples), F32)], axis=0
     )
-    packed = pack(features, y_halos, z_halos, cells, tail, placing, size_x, size_y)
+    packed = pack(
+        features, z_halos, info, rows, summing, tail, placing, comps, (size_x, size_y, size_z)
+    )
     arrived = lax.all_to_all(
         packed.reshape(trainers, capacity, WIDE),
         ("gx", "gy"),

time: 66.1 us -> 66.3 us (level)
  waiting for transfers between devices: 20.6 us -> 19.8 us
    pallas_call x2 -> x3, Pallas kernels: 2.76 us -> 2.87 us  [the longest x1 1.31 us: pack(): pl.pallas_call(functools.partial(pack_kernel, comps=comps, sizes=sizes),...]
where the time goes in v2:
time: 66.3 us; the launch traced here: 66 us
  starting transfers between devices  23 us (35%)
  waiting for transfers between devices  19.8 us (30%)
  Pallas kernels  19.2 us (29%)
  local copies, waits for them, and re-layouts  3.03 us (5%)
  between operations  0.82 us (1%)
    pallas_call x3, Pallas kernels, train(): pl.pallas_call(functools.partial(train_kernel, planes=planes, row_count=r...  13.1 us
    all_to_all x1, starting transfers between devices, on_device(): lax.all_to_all(packed.reshape(trainers, capacity, WIDE), ('gx', 'gy'), sp...  7.42 us
    all_to_all x1, waiting for transfers between devices, on_device(): lax.all_to_all(packed.reshape(trainers, capacity, WIDE), ('gx', 'gy'), sp...  7.04 us
    ppermute x3, starting transfers between devices, exchange(): lax.ppermute(high_face, axis, forward)  5.38 us
    ppermute x3, starting transfers between devices, exchange(): lax.ppermute(low_face, axis, backward)  5.24 us
    ppermute x3, waiting for transfers between devices, exchange(): lax.ppermute(low_face, axis, backward)  4.14 us
    ppermute x1, starting transfers between devices, on_device(): far = lax.ppermute(mine, 'gz', along(lambda x: x + 2))  2.98 us
    unnamed x22, local copies, waits for them, and re-layouts  2.88 us
  transfers between devices with their start and end apart: 12, of which 10 were waited for; matrix products, arithmetic and copies ran while one was open for 0% of the time, Pallas kernels for 14%

profile of v2, /device:TPU:32, one launch (start us, length us, event | category | flops | bytes accessed | tf_op | source)
XLA Modules:
  0.0 66.0 jit_solution(7717285963809780016)
XLA Ops:
  0.6 1.0 %copy-done = f32[3,8,32,128]{3,2,1,0:T(8,128)S(1)} copy-done((f32[3,8,32,128]{3,2,1,0:T(8,128)S(1)}, f32[3,8,32,128]{3,2,1,0:T(8,128)}, u32[]{:S(2)}) %copy-start) | copy-done | bytes 393240
  1.7 2.9 %collective-permute-start.1 = (f32[3,32,128]{2,1,0:T(8,128)S(1)}, f32[3,32,128]{2,1,0:T(8,128)S(1)}, u32[]{:S(2)}, u32[]{:S(2)}) collective-permute-start(f32[3,32,128]{2,1,0:T(8,128)S(1)} %get-tuple-element.57), channel_id=1, source_target_pairs={{32,0},{64,32},{96,64},{128,96},{160,128},{192,160},{224,192},{0,2... | collective-permute-start | bytes 147464 | tf_op jit(solution)/shard_map/ppermute | solution.py:62
  5.5 1.2 %patches.1 = (f32[96,256]{1,0:T(8,128)S(1)}, bf16[128,768]{1,0:T(8,128)(2,1)S(1)}, bf16[96,648]{1,0:T(8,128)(2,1)S(1)}) custom-call(f32[3,8,32,128]{3,2,1,0:T(8,128)S(1)} %copy-done, s32[2,256]{1,0:T(2,128)S(1)} %pad_add_fusion.info_ref), custom_call_target="tpu_custom_call" | custom-call | flops 960000000 | bytes 1000000 | tf_op jit(solution)/shard_map/patches/pallas_call | solution.py:301
  6.8 3.3 %collective-permute-start.2 = (f32[3,16,128]{2,1,0:T(8,128)S(1)}, f32[3,16,128]{2,1,0:T(8,128)S(1)}, u32[]{:S(2)}, u32[]{:S(2)}) collective-permute-start(f32[3,16,128]{2,1,0:T(8,128)S(1)} %get-tuple-element.59), channel_id=1, source_target_pairs={{0,8},{8,16},{16,24},{24,0},{1,9},{9,17},{17,25},{25,1},{2,10},{10... | collective-permute-start | bytes 73736 | tf_op jit(solution)/shard_map/ppermute | solution.py:62
  10.1 2.2 %collective-permute-start.3 = (f32[3,16,128]{2,1,0:T(8,128)S(1)}, f32[3,16,128]{2,1,0:T(8,128)S(1)}, u32[]{:S(2)}, u32[]{:S(2)}) collective-permute-start(f32[3,16,128]{2,1,0:T(8,128)S(1)} %get-tuple-element.60), channel_id=1, source_target_pairs={{8,0},{16,8},{24,16},{0,24},{9,1},{17,9},{25,17},{1,25},{10,2},{18... | collective-permute-start | bytes 73736 | tf_op jit(solution)/shard_map/ppermute | solution.py:62
  12.3 1.1 %plan.1 = (f32[48,128]{1,0:T(8,128)S(1)}, f32[48,128]{1,0:T(8,128)S(1)}, bf16[512,256]{1,0:T(8,128)(2,1)S(1)}, f32[96,256]{1,0:T(8,128)S(1)}) custom-call(f32[3,8,32,128]{3,2,1,0:T(8,128)S(1)} %copy-done, f32[3,32,128]{2,1,0:T(8,128)S(1)} %collective-permute-done.xlo_ref, f32[3,32,128]{2,1,0:T(8,128)S(1)} %collective-permute-done.1.xhi_ref, ...), custom_call_target="tpu_custom_call" | custom-call | flops 1200000000 | bytes 1000000 | tf_op jit(solution)/shard_map/plan/pallas_call | solution.py:200
  13.4 0.8 %collective-permute-done.2.ylo_ref = f32[3,16,128]{2,1,0:T(8,128)S(1)} collective-permute-done((f32[3,16,128]{2,1,0:T(8,128)S(1)}, f32[3,16,128]{2,1,0:T(8,128)S(1)}, u32[]{:S(2)}, u32[]{:S(2)}) %collective-permute-start.2) | collective-permute-done | bytes 24608 | tf_op jit(solution)/shard_map/ppermute | solution.py:62
  14.2 1.3 %collective-permute-done.3.yhi_ref = f32[3,16,128]{2,1,0:T(8,128)S(1)} collective-permute-done((f32[3,16,128]{2,1,0:T(8,128)S(1)}, f32[3,16,128]{2,1,0:T(8,128)S(1)}, u32[]{:S(2)}, u32[]{:S(2)}) %collective-permute-start.3) | collective-permute-done | bytes 24608 | tf_op jit(solution)/shard_map/ppermute | solution.py:62
  15.6 2.0 %collective-permute-start.4 = (f32[48,128]{1,0:T(8,128)S(1)}, f32[48,128]{1,0:T(8,128)S(1)}, u32[]{:S(2)}, u32[]{:S(2)}) collective-permute-start(f32[48,128]{1,0:T(8,128)S(1)} %get-tuple-element.65), channel_id=1, source_target_pairs={{0,1},{1,2},{2,3},{3,4},{4,5},{5,6},{6,7},{7,0},{8,9},{9,10},{10,1... | collective-permute-start | bytes 73736 | tf_op jit(solution)/shard_map/ppermute | solution.py:62
  18.1 1.4 %collective-permute-done.4.zlo_ref = f32[48,128]{1,0:T(8,128)S(1)} collective-permute-done((f32[48,128]{1,0:T(8,128)S(1)}, f32[48,128]{1,0:T(8,128)S(1)}, u32[]{:S(2)}, u32[]{:S(2)}) %collective-permute-start.4) | collective-permute-done | bytes 24608 | tf_op jit(solution)/shard_map/ppermute | solution.py:62
  19.5 2.8 %collective-permute-done.5.zhi_ref = f32[48,128]{1,0:T(8,128)S(1)} collective-permute-done((f32[48,128]{1,0:T(8,128)S(1)}, f32[48,128]{1,0:T(8,128)S(1)}, u32[]{:S(2)}, u32[]{:S(2)}) %collective-permute-start.5) | collective-permute-done | bytes 24608 | tf_op jit(solution)/shard_map/ppermute | solution.py:62
  22.4 1.3 %pack.1 = bf16[512,128]{1,0:T(8,128)(2,1)} custom-call(f32[96,256]{1,0:T(8,128)S(1)} %get-tuple-element.69.own_ref, f32[48,128]{1,0:T(8,128)S(1)} %collective-permute-done.4.zlo_ref, f32[48,128]{1,0:T(8,128)S(1)} %collective-permute-done.5.zhi_ref, s32[2,256]{1,0:T(2,128)S(1)} %pad_add_fusion.info_ref, bf16[128,768]{1,0:T(8,128)(2,1)S(1)} %get-tuple-element.70.rows_ref, ...), custom_call_target="tpu_custom_call" | custom-call | flops 560000000 | bytes 1000000 | tf_op jit(solution)/shard_map/pack/pallas_call | solution.py:404
  23.7 7.4 %all-to-all-start = ((bf16[32,16,128]{2,1,0:T(8,128)(2,1)}), bf16[32,16,128]{2,1,0:T(8,128)(2,1)S(1)}, u32[]{:S(2)}, u32[]{:S(2)}) async-start(bf16[32,16,128]{2,1,0:T(8,128)(2,1)} %bitcast.2), calls=%async_computation | async-start | bytes 262144 | tf_op jit(solution)/shard_map/all_to_all | solution.py:755
  32.8 1.4 %advance.1 = (f32[3,8,32,128]{3,2,1,0:T(8,128)}, f32[8,128]{1,0:T(8,128)S(1)}) custom-call(f32[3,8,32,128]{3,2,1,0:T(8,128)S(1)} %copy-done.1, f32[3,32,128]{2,1,0:T(8,128)S(1)} %collective-permute-done.xlo_ref, f32[3,32,128]{2,1,0:T(8,128)S(1)} %collective-permute-done.1.xhi_ref, f32[3,16,128]{2,1,0:T(8,128)S(1)} %collective-permute-done.2.ylo_ref, ...), custom_call_target="tpu_custom_call" | custom-call | flops 1200000000 | bytes 1000000 | tf_op jit(solution)/shard_map/advance/pallas_call | solution.py:474
  34.2 7.0 %all-to-all-done = bf16[32,16,128]{2,1,0:T(8,128)(2,1)S(1)} async-done(((bf16[32,16,128]{2,1,0:T(8,128)(2,1)}), bf16[32,16,128]{2,1,0:T(8,128)(2,1)S(1)}, u32[]{:S(2)}, u32[]{:S(2)}) %all-to-all-start) | async-done | bytes 131104 | tf_op jit(solution)/shard_map/all_to_all | solution.py:755
  41.4 3.0 %collective-permute-start.7 = (bf16[96,512]{1,0:T(8,128)(2,1)S(1)}, bf16[96,512]{1,0:T(8,128)(2,1)S(1)}, u32[]{:S(2)}, u32[]{:S(2)}) collective-permute-start(bf16[96,512]{1,0:T(8,128)(2,1)S(1)} %turn.1.refs_0_), channel_id=1, source_target_pairs={{0,4},{1,5},{2,6},{3,7},{4,0},{5,1},{6,2},{7,3},{8,12},{9,13},{10,... | collective-permute-start | bytes 294920 | tf_op jit(solution)/shard_map/ppermute | solution.py:776
  44.4 2.0 %train.3 = (f32[512,96]{1,0:T(8,128)S(1)}, f32[64,512]{1,0:T(8,128)S(1)}, f32[16,512]{1,0:T(8,128)S(1)}, f32[512,128]{1,0:T(8,128)S(1)}, f32[512,128]{1,0:T(8,12...) custom-call(bf16[96,512]{1,0:T(8,128)(2,1)S(1)} %turn.1.refs_0_, ...), custom_call_target="tpu_custom_call" | custom-call | flops 1280000000 | bytes 1000000 | tf_op jit(solution)/shard_map/train/pallas_call | solution.py:692
  46.4 2.1 %collective-permute-done.7.refs_1_ = bf16[96,512]{1,0:T(8,128)(2,1)S(1)} collective-permute-done((bf16[96,512]{1,0:T(8,128)(2,1)S(1)}, bf16[96,512]{1,0:T(8,128)(2,1)S(1)}, u32[]{:S(2)}, u32[]{:S(2)}) %collective-permute-start.7) | collective-permute-done | bytes 98336 | tf_op jit(solution)/shard_map/ppermute | solution.py:776
  48.5 0.9 %collective-permute-done.6.refs_0_ = bf16[96,512]{1,0:T(8,128)(2,1)S(1)} collective-permute-done((bf16[96,512]{1,0:T(8,128)(2,1)S(1)}, bf16[96,512]{1,0:T(8,128)(2,1)S(1)}, u32[]{:S(2)}, u32[]{:S(2)}) %collective-permute-start.6) | collective-permute-done | bytes 98336 | tf_op jit(solution)/shard_map/ppermute | solution.py:775
  49.5 2.0 %collective-permute-start.9 = (bf16[2,96,512]{2,1,0:T(8,128)(2,1)S(1)}, bf16[2,96,512]{2,1,0:T(8,128)(2,1)S(1)}, u32[]{:S(2)}, u32[]{:S(2)}) collective-permute-start(bf16[2,96,512]{2,1,0:T(8,128)(2,1)S(1)} %pad_maximum_fusion), channel_id=1, source_target_pairs={{0,6},{1,7},{2,4},{3,5},{4,2},{5,3},{6,0},{7,1},{8,14},{9,15},{10,... | collective-permute-start | bytes 589832 | tf_op jit(solution)/shard_map/ppermute | solution.py:782
  51.5 3.0 %train.4 = (f32[512,96]{1,0:T(8,128)S(1)}, f32[64,512]{1,0:T(8,128)S(1)}, f32[16,512]{1,0:T(8,128)S(1)}, f32[512,128]{1,0:T(8,128)S(1)}, f32[512,128]{1,0:T(8,128)S(1)}, /*index=5*/f32[8,128]{1,0:T(8,128)S(1)}) custom-call(bf16[96,512]{1,0:T(8,128)(2,1)S(1)} %collective-permute-done.6.refs_0_, bf16[96,512]{1,0:T(8,128)(2,1)S(1)} %collective-permute-done.7.refs_1_, ...), custom_call_target="tpu_custom_call" | custom-call | flops 2560000000 | bytes 1000000 | tf_op jit(solution)/shard_map/train/pallas_call | solution.py:692
  54.6 1.6 %collective-permute-done.10.refs_2_ = bf16[96,512]{1,0:T(8,128)(2,1)S(1)} collective-permute-done((bf16[96,512]{1,0:T(8,128)(2,1)S(1)}, bf16[96,512]{1,0:T(8,128)(2,1)S(1)}, u32[]{:S(2)}, u32[]{:S(2)}) %collective-permute-start.10) | collective-permute-done | bytes 98336 | tf_op jit(solution)/shard_map/ppermute | solution.py:784
  56.2 1.0 %collective-permute-done.9.refs_1_ = bf16[2,96,512]{2,1,0:T(8,128)(2,1)S(1)} collective-permute-done((bf16[2,96,512]{2,1,0:T(8,128)(2,1)S(1)}, bf16[2,96,512]{2,1,0:T(8,128)(2,1)S(1)}, u32[]{:S(2)}, u32[]{:S(2)}) %collective-permute-start.9) | collective-permute-done | bytes 196640 | tf_op jit(solution)/shard_map/ppermute | solution.py:782
  57.9 8.1 %train.5 = (f32[81,1,512]{2,1,0:T(1,128)}, f32[6,1,512]{2,1,0:T(1,128)}, f32[1,1030]{1,0:T(1,128)}, f32[256,128]{1,0:T(8,128)}, f32[256,128]{1,0:T(8,128)}) custom-call(bf16[2,96,512]{2,1,0:T(8,128)(2,1)S(1)} %collective-permute-done.8.refs_0_, bf16[2,96,512]{2,1,0:T(8,128)(2,1)S(1)} %collective-permute-done.9.refs_1_, ...), custom_call_target="tpu_custom_call" | custom-call | flops 6400000000 | bytes 1000000 | tf_op jit(solution)/shard_map/train/pallas_call | solution.py:692
  (41 shorter events, 4.2 us)
Async XLA Ops:
  0.6 1.0 %copy-start = (f32[3,8,32,128]{3,2,1,0:T(8,128)S(1)}, f32[3,8,32,128]{3,2,1,0:T(8,128)}, u32[]{:S(2)}) copy-start(f32[3,8,32,128]{3,2,1,0:T(8,128)} %v_ref.5) | copy-start | bytes 1179652
  1.6 5.1 %collective-permute-start = (f32[3,32,128]{2,1,0:T(8,128)S(1)}, f32[3,32,128]{2,1,0:T(8,128)S(1)}, u32[]{:S(2)}, u32[]{:S(2)}) collective-permute-start(f32[3,32,128]{2,1,0:T(8,128)S(1)} %get-tuple-element.56), channel_id=1, source_target_pairs={{0,32},{32,64},{64,96},{96,128},{128,160},{160,192},{192,224},{224... | collective-permute-start | bytes 147464 | tf_op jit(solution)/shard_map/ppermute | solution.py:62
  1.7 3.1 %copy-start.8 = (bf16[6,256]{1,0:T(8,128)(2,1)S(1)}, bf16[6,256]{1,0:T(8,128)(2,1)}, u32[]{:S(2)}) copy-start(bf16[6,256]{1,0:T(8,128)(2,1)} %param.13) | copy-start | bytes 9220
  1.7 5.0 %collective-permute-start.1 = (f32[3,32,128]{2,1,0:T(8,128)S(1)}, f32[3,32,128]{2,1,0:T(8,128)S(1)}, u32[]{:S(2)}, u32[]{:S(2)}) collective-permute-start(f32[3,32,128]{2,1,0:T(8,128)S(1)} %get-tuple-element.57), channel_id=1, source_target_pairs={{32,0},{64,32},{96,64},{128,96},{160,128},{192,160},{224,192},{0,2... | collective-permute-start | bytes 147464 | tf_op jit(solution)/shard_map/ppermute | solution.py:62
  4.8 0.7 %copy-start.10 = (s32[256]{0:T(256)S(1)}, s32[256]{0:T(256)}, u32[]{:S(2)}) copy-start(s32[256]{0:T(256)} %param.11) | copy-start | bytes 3076
  4.8 0.7 %copy-start.9 = (s32[256,1]{0,1:T(1,128)S(1)}, s32[256,1]{0,1:T(1,128)}, u32[]{:S(2)}) copy-start(s32[256,1]{0,1:T(1,128)} %param.12) | copy-start | bytes 3076
  6.8 7.4 %collective-permute-start.2 = (f32[3,16,128]{2,1,0:T(8,128)S(1)}, f32[3,16,128]{2,1,0:T(8,128)S(1)}, u32[]{:S(2)}, u32[]{:S(2)}) collective-permute-start(f32[3,16,128]{2,1,0:T(8,128)S(1)} %get-tuple-element.59), channel_id=1, source_target_pairs={{0,8},{8,16},{16,24},{24,0},{1,9},{9,17},{17,25},{25,1},{2,10},{10... | collective-permute-start | bytes 73736 | tf_op jit(solution)/shard_map/ppermute | solution.py:62
  10.1 5.4 %collective-permute-start.3 = (f32[3,16,128]{2,1,0:T(8,128)S(1)}, f32[3,16,128]{2,1,0:T(8,128)S(1)}, u32[]{:S(2)}, u32[]{:S(2)}) collective-permute-start(f32[3,16,128]{2,1,0:T(8,128)S(1)} %get-tuple-element.60), channel_id=1, source_target_pairs={{8,0},{16,8},{24,16},{0,24},{9,1},{17,9},{25,17},{1,25},{10,2},{18... | collective-permute-start | bytes 73736 | tf_op jit(solution)/shard_map/ppermute | solution.py:62
  15.6 3.9 %collective-permute-start.4 = (f32[48,128]{1,0:T(8,128)S(1)}, f32[48,128]{1,0:T(8,128)S(1)}, u32[]{:S(2)}, u32[]{:S(2)}) collective-permute-start(f32[48,128]{1,0:T(8,128)S(1)} %get-tuple-element.65), channel_id=1, source_target_pairs={{0,1},{1,2},{2,3},{3,4},{4,5},{5,6},{6,7},{7,0},{8,9},{9,10},{10,1... | collective-permute-start | bytes 73736 | tf_op jit(solution)/shard_map/ppermute | solution.py:62
  17.6 4.7 %collective-permute-start.5 = (f32[48,128]{1,0:T(8,128)S(1)}, f32[48,128]{1,0:T(8,128)S(1)}, u32[]{:S(2)}, u32[]{:S(2)}) collective-permute-start(f32[48,128]{1,0:T(8,128)S(1)} %get-tuple-element.66.after_ref), channel_id=1, source_target_pairs={{1,0},{2,1},{3,2},{4,3},{5,4},{6,5},{7,6},{0,7},{9,8},{10,9},{11,1... | collective-permute-start | bytes 73736 | tf_op jit(solution)/shard_map/ppermute | solution.py:62
  22.3 8.8 %copy-start.2 = (bf16[1,512,512]{2,1,0:T(8,128)(2,1)S(1)}, bf16[1,512,512]{2,1,0:T(8,128)(2,1)}, u32[]{:S(2)}) copy-start(bf16[1,512,512]{2,1,0:T(8,128)(2,1)} %param.15) | copy-start | bytes 1572868
  23.7 7.5 %copy-start.5 = (bf16[1,512,81]{1,2,0:T(8,128)(2,1)S(1)}, bf16[1,512,81]{1,2,0:T(8,128)(2,1)}, u32[]{:S(2)}) copy-start(bf16[1,512,81]{1,2,0:T(8,128)(2,1)} %param.14) | copy-start | bytes 248836
  23.7 7.5 %copy-start.6 = (bf16[1,6,512]{2,1,0:T(8,128)(2,1)S(1)}, bf16[1,6,512]{2,1,0:T(8,128)(2,1)}, u32[]{:S(2)}) copy-start(bf16[1,6,512]{2,1,0:T(8,128)(2,1)} %param.16) | copy-start | bytes 18436
  23.7 17.6 %all-to-all-start = ((bf16[32,16,128]{2,1,0:T(8,128)(2,1)}), bf16[32,16,128]{2,1,0:T(8,128)(2,1)S(1)}, u32[]{:S(2)}, u32[]{:S(2)}) async-start(bf16[32,16,128]{2,1,0:T(8,128)(2,1)} %bitcast.2), calls=%async_computation | async-start | bytes 262144 | tf_op jit(solution)/shard_map/all_to_all | solution.py:755
  31.1 0.7 %copy-start.7 = (f32[1,1030]{1,0:T(1,128)S(1)}, f32[1,1030]{1,0:T(1,128)}, u32[]{:S(2)}) copy-start(f32[1,1030]{1,0:T(1,128)} %biases_ref.1) | copy-start | bytes 12364
  31.8 1.0 %copy-start.1 = (f32[3,8,32,128]{3,2,1,0:T(8,128)S(1)}, f32[3,8,32,128]{3,2,1,0:T(8,128)}, u32[]{:S(2)}) copy-start(f32[3,8,32,128]{3,2,1,0:T(8,128)} %v_ref.5) | copy-start | bytes 1179652
  41.4 7.1 %collective-permute-start.7 = (bf16[96,512]{1,0:T(8,128)(2,1)S(1)}, bf16[96,512]{1,0:T(8,128)(2,1)S(1)}, u32[]{:S(2)}, u32[]{:S(2)}) collective-permute-start(bf16[96,512]{1,0:T(8,128)(2,1)S(1)} %turn.1.refs_0_), channel_id=1, source_target_pairs={{0,4},{1,5},{2,6},{3,7},{4,0},{5,1},{6,2},{7,3},{8,12},{9,13},{10,... | collective-permute-start | bytes 294920 | tf_op jit(solution)/shard_map/ppermute | solution.py:776
  44.4 5.1 %collective-permute-start.6 = (bf16[96,512]{1,0:T(8,128)(2,1)S(1)}, bf16[96,512]{1,0:T(8,128)(2,1)S(1)}, u32[]{:S(2)}, u32[]{:S(2)}) collective-permute-start(bf16[96,512]{1,0:T(8,128)(2,1)S(1)} %turn.1.refs_0_), channel_id=1, source_target_pairs={{0,1},{1,0},{2,3},{3,2},{4,5},{5,4},{6,7},{7,6},{8,9},{9,8},{10,11... | collective-permute-start | bytes 294920 | tf_op jit(solution)/shard_map/ppermute | solution.py:775
  49.5 8.4 %copy-start.3 = (f32[1,32768]{1,0:T(1,128)S(1)}, f32[1,32768]{1,0:T(1,128)}, u32[]{:S(2)}) copy-start(f32[1,32768]{1,0:T(1,128)} %param.19) | copy-start | bytes 393220
  49.5 8.4 %copy-start.4 = (f32[1,32768]{1,0:T(1,128)S(1)}, f32[1,32768]{1,0:T(1,128)}, u32[]{:S(2)}) copy-start(f32[1,32768]{1,0:T(1,128)} %param.18) | copy-start | bytes 393220
  49.5 7.6 %collective-permute-start.9 = (bf16[2,96,512]{2,1,0:T(8,128)(2,1)S(1)}, bf16[2,96,512]{2,1,0:T(8,128)(2,1)S(1)}, u32[]{:S(2)}, u32[]{:S(2)}) collective-permute-start(bf16[2,96,512]{2,1,0:T(8,128)(2,1)S(1)} %pad_maximum_fusion), channel_id=1, source_target_pairs={{0,6},{1,7},{2,4},{3,5},{4,2},{5,3},{6,0},{7,1},{8,14},{9,15},{10,... | collective-permute-start | bytes 589832 | tf_op jit(solution)/shard_map/ppermute | solution.py:782
  51.5 6.4 %collective-permute-start.8 = (bf16[2,96,512]{2,1,0:T(8,128)(2,1)S(1)}, bf16[2,96,512]{2,1,0:T(8,128)(2,1)S(1)}, u32[]{:S(2)}, u32[]{:S(2)}) collective-permute-start(bf16[2,96,512]{2,1,0:T(8,128)(2,1)S(1)} %pad_maximum_fusion), channel_id=1, source_target_pairs={{0,2},{1,3},{2,0},{3,1},{4,6},{5,7},{6,4},{7,5},{8,10},{9,11},{10,... | collective-permute-start | bytes 589832 | tf_op jit(solution)/shard_map/ppermute | solution.py:781
  51.5 4.6 %collective-permute-start.10 = (bf16[96,512]{1,0:T(8,128)(2,1)S(1)}, bf16[96,512]{1,0:T(8,128)(2,1)S(1)}, u32[]{:S(2)}, u32[]{:S(2)}) collective-permute-start(bf16[96,512]{1,0:T(8,128)(2,1)S(1)} %collective-permute-done.7.refs_1_), channel_id=1, source_target_pairs={{0,1},{1,0},{2,3},{3,2},{4,5},{5,4},{6,7},{7,6},{8,9},{9,8},{10,11... | collective-permute-start | bytes 294920 | tf_op jit(solution)/shard_map/ppermute | solution.py:784

commit v3 on v2

--- a/solution.py
+++ b/solution.py
@@ -189,7 +189,9 @@
     earlier = ones_where(iota((samples, samples), 0) < iota((samples, samples), 1))
     before = jnp.dot(ones_where(same), earlier, preferred_element_type=F32)
     position = jnp.sum(jnp.where(same, before, 0.0), axis=0, keepdims=True).astype(I32)
-    slot = trainer * capacity + position
+    columns = lax.axis_size("gy")
+    block = trainer % columns * (trainers // columns) + trainer // columns
+    slot = block * capacity + position
     placing_ref[...] = ones_where(iota((slots, samples), 0) == slot)
 
 
@@ -754,7 +756,7 @@
     )
     arrived = lax.all_to_all(
         packed.reshape(trainers, capacity, WIDE),
-        ("gx", "gy"),
+        ("gy", "gx"),
         split_axis=0,
         concat_axis=0,
         tiled=True,

time: 66.3 us -> 65.8 us (level)
  waiting for transfers between devices: 19.8 us -> 19.1 us
  transfers between devices with their start and end apart: 12 -> 12, of which waited for: 10 -> 10; matrix products, arithmetic and copies ran while one was open for 0% -> 0% of each run, Pallas kernels for 14% -> 15%
where the time goes in v3:
time: 65.8 us; the launch traced here: 65.5 us
  starting transfers between devices  23.3 us (35%)
  Pallas kernels  19.2 us (29%)
  waiting for transfers between devices  19.1 us (29%)
  local copies, waits for them, and re-layouts  3.03 us (5%)
  between operations  0.82 us (1%)
    pallas_call x3, Pallas kernels, train(): pl.pallas_call(functools.partial(train_kernel, planes=planes, row_count=r...  13.1 us
    all_to_all x1, waiting for transfers between devices, on_device(): lax.all_to_all(packed.reshape(trainers, capacity, WIDE), ('gy', 'gx'), sp...  7.62 us
    all_to_all x1, starting transfers between devices, on_device(): lax.all_to_all(packed.reshape(trainers, capacity, WIDE), ('gy', 'gx'), sp...  7.42 us
    ppermute x3, starting transfers between devices, exchange(): lax.ppermute(high_face, axis, forward)  5.38 us
    ppermute x3, starting transfers between devices, exchange(): lax.ppermute(low_face, axis, backward)  5.24 us
    ppermute x3, waiting for transfers between devices, exchange(): lax.ppermute(low_face, axis, backward)  4.14 us
    unnamed x22, local copies, waits for them, and re-layouts  2.88 us
    ppermute x1, starting transfers between devices, on_device(): far = lax.ppermute(mine, 'gz', along(lambda x: x + 2))  2.81 us
  transfers between devices with their start and end apart: 12, of which 10 were waited for; matrix products, arithmetic and copies ran while one was open for 0% of the time, Pallas kernels for 15%

profile of v3, /device:TPU:32, one launch (start us, length us, event | category | flops | bytes accessed | tf_op | source)
XLA Modules:
  0.0 65.5 jit_solution(6490383422630297187)
XLA Ops:
  0.6 1.0 %copy-done = f32[3,8,32,128]{3,2,1,0:T(8,128)S(1)} copy-done((f32[3,8,32,128]{3,2,1,0:T(8,128)S(1)}, f32[3,8,32,128]{3,2,1,0:T(8,128)}, u32[]{:S(2)}) %copy-start) | copy-done | bytes 393240
  1.7 2.9 %collective-permute-start.1 = (f32[3,32,128]{2,1,0:T(8,128)S(1)}, f32[3,32,128]{2,1,0:T(8,128)S(1)}, u32[]{:S(2)}, u32[]{:S(2)}) collective-permute-start(f32[3,32,128]{2,1,0:T(8,128)S(1)} %get-tuple-element.57), channel_id=1, source_target_pairs={{32,0},{64,32},{96,64},{128,96},{160,128},{192,160},{224,192},{0,2... | collective-permute-start | bytes 147464 | tf_op jit(solution)/shard_map/ppermute | solution.py:62
  5.5 1.2 %patches.1 = (f32[96,256]{1,0:T(8,128)S(1)}, bf16[128,768]{1,0:T(8,128)(2,1)S(1)}, bf16[96,648]{1,0:T(8,128)(2,1)S(1)}) custom-call(f32[3,8,32,128]{3,2,1,0:T(8,128)S(1)} %copy-done, s32[2,256]{1,0:T(2,128)S(1)} %pad_add_fusion.info_ref), custom_call_target="tpu_custom_call" | custom-call | flops 960000000 | bytes 1000000 | tf_op jit(solution)/shard_map/patches/pallas_call | solution.py:303
  6.8 3.3 %collective-permute-start.2 = (f32[3,16,128]{2,1,0:T(8,128)S(1)}, f32[3,16,128]{2,1,0:T(8,128)S(1)}, u32[]{:S(2)}, u32[]{:S(2)}) collective-permute-start(f32[3,16,128]{2,1,0:T(8,128)S(1)} %get-tuple-element.59), channel_id=1, source_target_pairs={{0,8},{8,16},{16,24},{24,0},{1,9},{9,17},{17,25},{25,1},{2,10},{10... | collective-permute-start | bytes 73736 | tf_op jit(solution)/shard_map/ppermute | solution.py:62
  10.1 2.2 %collective-permute-start.3 = (f32[3,16,128]{2,1,0:T(8,128)S(1)}, f32[3,16,128]{2,1,0:T(8,128)S(1)}, u32[]{:S(2)}, u32[]{:S(2)}) collective-permute-start(f32[3,16,128]{2,1,0:T(8,128)S(1)} %get-tuple-element.60), channel_id=1, source_target_pairs={{8,0},{16,8},{24,16},{0,24},{9,1},{17,9},{25,17},{1,25},{10,2},{18... | collective-permute-start | bytes 73736 | tf_op jit(solution)/shard_map/ppermute | solution.py:62
  12.3 1.1 %plan.1 = (f32[48,128]{1,0:T(8,128)S(1)}, f32[48,128]{1,0:T(8,128)S(1)}, bf16[512,256]{1,0:T(8,128)(2,1)S(1)}, f32[96,256]{1,0:T(8,128)S(1)}) custom-call(f32[3,8,32,128]{3,2,1,0:T(8,128)S(1)} %copy-done, f32[3,32,128]{2,1,0:T(8,128)S(1)} %collective-permute-done.xlo_ref, f32[3,32,128]{2,1,0:T(8,128)S(1)} %collective-permute-done.1.xhi_ref, ...), custom_call_target="tpu_custom_call" | custom-call | flops 1200000000 | bytes 1000000 | tf_op jit(solution)/shard_map/plan/pallas_call | solution.py:202
  13.4 0.8 %collective-permute-done.2.ylo_ref = f32[3,16,128]{2,1,0:T(8,128)S(1)} collective-permute-done((f32[3,16,128]{2,1,0:T(8,128)S(1)}, f32[3,16,128]{2,1,0:T(8,128)S(1)}, u32[]{:S(2)}, u32[]{:S(2)}) %collective-permute-start.2) | collective-permute-done | bytes 24608 | tf_op jit(solution)/shard_map/ppermute | solution.py:62
  14.2 1.3 %collective-permute-done.3.yhi_ref = f32[3,16,128]{2,1,0:T(8,128)S(1)} collective-permute-done((f32[3,16,128]{2,1,0:T(8,128)S(1)}, f32[3,16,128]{2,1,0:T(8,128)S(1)}, u32[]{:S(2)}, u32[]{:S(2)}) %collective-permute-start.3) | collective-permute-done | bytes 24608 | tf_op jit(solution)/shard_map/ppermute | solution.py:62
  15.6 2.0 %collective-permute-start.4 = (f32[48,128]{1,0:T(8,128)S(1)}, f32[48,128]{1,0:T(8,128)S(1)}, u32[]{:S(2)}, u32[]{:S(2)}) collective-permute-start(f32[48,128]{1,0:T(8,128)S(1)} %get-tuple-element.65), channel_id=1, source_target_pairs={{0,1},{1,2},{2,3},{3,4},{4,5},{5,6},{6,7},{7,0},{8,9},{9,10},{10,1... | collective-permute-start | bytes 73736 | tf_op jit(solution)/shard_map/ppermute | solution.py:62
  18.1 1.4 %collective-permute-done.4.zlo_ref = f32[48,128]{1,0:T(8,128)S(1)} collective-permute-done((f32[48,128]{1,0:T(8,128)S(1)}, f32[48,128]{1,0:T(8,128)S(1)}, u32[]{:S(2)}, u32[]{:S(2)}) %collective-permute-start.4) | collective-permute-done | bytes 24608 | tf_op jit(solution)/shard_map/ppermute | solution.py:62
  19.5 2.8 %collective-permute-done.5.zhi_ref = f32[48,128]{1,0:T(8,128)S(1)} collective-permute-done((f32[48,128]{1,0:T(8,128)S(1)}, f32[48,128]{1,0:T(8,128)S(1)}, u32[]{:S(2)}, u32[]{:S(2)}) %collective-permute-start.5) | collective-permute-done | bytes 24608 | tf_op jit(solution)/shard_map/ppermute | solution.py:62
  22.4 1.3 %pack.1 = bf16[512,128]{1,0:T(8,128)(2,1)} custom-call(f32[96,256]{1,0:T(8,128)S(1)} %get-tuple-element.69.own_ref, f32[48,128]{1,0:T(8,128)S(1)} %collective-permute-done.4.zlo_ref, f32[48,128]{1,0:T(8,128)S(1)} %collective-permute-done.5.zhi_ref, s32[2,256]{1,0:T(2,128)S(1)} %pad_add_fusion.info_ref, bf16[128,768]{1,0:T(8,128)(2,1)S(1)} %get-tuple-element.70.rows_ref, ...), custom_call_target="tpu_custom_call" | custom-call | flops 560000000 | bytes 1000000 | tf_op jit(solution)/shard_map/pack/pallas_call | solution.py:406
  23.7 7.4 %all-to-all-start = ((bf16[32,16,128]{2,1,0:T(8,128)(2,1)}), bf16[32,16,128]{2,1,0:T(8,128)(2,1)S(1)}, u32[]{:S(2)}, u32[]{:S(2)}) async-start(bf16[32,16,128]{2,1,0:T(8,128)(2,1)} %bitcast.2), calls=%async_computation | async-start | bytes 262144 | tf_op jit(solution)/shard_map/all_to_all | solution.py:757
  32.8 1.4 %advance.1 = (f32[3,8,32,128]{3,2,1,0:T(8,128)}, f32[8,128]{1,0:T(8,128)S(1)}) custom-call(f32[3,8,32,128]{3,2,1,0:T(8,128)S(1)} %copy-done.1, f32[3,32,128]{2,1,0:T(8,128)S(1)} %collective-permute-done.xlo_ref, f32[3,32,128]{2,1,0:T(8,128)S(1)} %collective-permute-done.1.xhi_ref, f32[3,16,128]{2,1,0:T(8,128)S(1)} %collective-permute-done.2.ylo_ref, ...), custom_call_target="tpu_custom_call" | custom-call | flops 1200000000 | bytes 1000000 | tf_op jit(solution)/shard_map/advance/pallas_call | solution.py:476
  34.2 7.6 %all-to-all-done = bf16[32,16,128]{2,1,0:T(8,128)(2,1)S(1)} async-done(((bf16[32,16,128]{2,1,0:T(8,128)(2,1)}), bf16[32,16,128]{2,1,0:T(8,128)(2,1)S(1)}, u32[]{:S(2)}, u32[]{:S(2)}) %all-to-all-start) | async-done | bytes 131104 | tf_op jit(solution)/shard_map/all_to_all | solution.py:757
  42.0 2.8 %collective-permute-start.7 = (bf16[96,512]{1,0:T(8,128)(2,1)S(1)}, bf16[96,512]{1,0:T(8,128)(2,1)S(1)}, u32[]{:S(2)}, u32[]{:S(2)}) collective-permute-start(bf16[96,512]{1,0:T(8,128)(2,1)S(1)} %turn.1.refs_0_), channel_id=1, source_target_pairs={{0,4},{1,5},{2,6},{3,7},{4,0},{5,1},{6,2},{7,3},{8,12},{9,13},{10,... | collective-permute-start | bytes 294920 | tf_op jit(solution)/shard_map/ppermute | solution.py:778
  45.1 2.0 %train.3 = (f32[512,96]{1,0:T(8,128)S(1)}, f32[64,512]{1,0:T(8,128)S(1)}, f32[16,512]{1,0:T(8,128)S(1)}, f32[512,128]{1,0:T(8,128)S(1)}, f32[512,128]{1,0:T(8,12...) custom-call(bf16[96,512]{1,0:T(8,128)(2,1)S(1)} %turn.1.refs_0_, ...), custom_call_target="tpu_custom_call" | custom-call | flops 1280000000 | bytes 1000000 | tf_op jit(solution)/shard_map/train/pallas_call | solution.py:694
  47.0 1.5 %collective-permute-done.7.refs_1_ = bf16[96,512]{1,0:T(8,128)(2,1)S(1)} collective-permute-done((bf16[96,512]{1,0:T(8,128)(2,1)S(1)}, bf16[96,512]{1,0:T(8,128)(2,1)S(1)}, u32[]{:S(2)}, u32[]{:S(2)}) %collective-permute-start.7) | collective-permute-done | bytes 98336 | tf_op jit(solution)/shard_map/ppermute | solution.py:778
  48.5 0.9 %collective-permute-done.6.refs_0_ = bf16[96,512]{1,0:T(8,128)(2,1)S(1)} collective-permute-done((bf16[96,512]{1,0:T(8,128)(2,1)S(1)}, bf16[96,512]{1,0:T(8,128)(2,1)S(1)}, u32[]{:S(2)}, u32[]{:S(2)}) %collective-permute-start.6) | collective-permute-done | bytes 98336 | tf_op jit(solution)/shard_map/ppermute | solution.py:777
  49.5 2.0 %collective-permute-start.9 = (bf16[2,96,512]{2,1,0:T(8,128)(2,1)S(1)}, bf16[2,96,512]{2,1,0:T(8,128)(2,1)S(1)}, u32[]{:S(2)}, u32[]{:S(2)}) collective-permute-start(bf16[2,96,512]{2,1,0:T(8,128)(2,1)S(1)} %pad_maximum_fusion), channel_id=1, source_target_pairs={{0,6},{1,7},{2,4},{3,5},{4,2},{5,3},{6,0},{7,1},{8,14},{9,15},{10,... | collective-permute-start | bytes 589832 | tf_op jit(solution)/shard_map/ppermute | solution.py:784
  51.7 3.0 %train.4 = (f32[512,96]{1,0:T(8,128)S(1)}, f32[64,512]{1,0:T(8,128)S(1)}, f32[16,512]{1,0:T(8,128)S(1)}, f32[512,128]{1,0:T(8,128)S(1)}, f32[512,128]{1,0:T(8,128)S(1)}, /*index=5*/f32[8,128]{1,0:T(8,128)S(1)}) custom-call(bf16[96,512]{1,0:T(8,128)(2,1)S(1)} %collective-permute-done.6.refs_0_, bf16[96,512]{1,0:T(8,128)(2,1)S(1)} %collective-permute-done.7.refs_1_, ...), custom_call_target="tpu_custom_call" | custom-call | flops 2560000000 | bytes 1000000 | tf_op jit(solution)/shard_map/train/pallas_call | solution.py:694
  54.7 1.4 %collective-permute-done.10.refs_2_ = bf16[96,512]{1,0:T(8,128)(2,1)S(1)} collective-permute-done((bf16[96,512]{1,0:T(8,128)(2,1)S(1)}, bf16[96,512]{1,0:T(8,128)(2,1)S(1)}, u32[]{:S(2)}, u32[]{:S(2)}) %collective-permute-start.10) | collective-permute-done | bytes 98336 | tf_op jit(solution)/shard_map/ppermute | solution.py:786
  56.7 0.7 %collective-permute-done.8.refs_0_ = bf16[2,96,512]{2,1,0:T(8,128)(2,1)S(1)} collective-permute-done((bf16[2,96,512]{2,1,0:T(8,128)(2,1)S(1)}, bf16[2,96,512]{2,1,0:T(8,128)(2,1)S(1)}, u32[]{:S(2)}, u32[]{:S(2)}) %collective-permute-start.8) | collective-permute-done | bytes 196640 | tf_op jit(solution)/shard_map/ppermute | solution.py:783
  57.4 8.1 %train.5 = (f32[81,1,512]{2,1,0:T(1,128)}, f32[6,1,512]{2,1,0:T(1,128)}, f32[1,1030]{1,0:T(1,128)}, f32[256,128]{1,0:T(8,128)}, f32[256,128]{1,0:T(8,128)}) custom-call(bf16[2,96,512]{2,1,0:T(8,128)(2,1)S(1)} %collective-permute-done.8.refs_0_, bf16[2,96,512]{2,1,0:T(8,128)(2,1)S(1)} %collective-permute-done.9.refs_1_, ...), custom_call_target="tpu_custom_call" | custom-call | flops 6400000000 | bytes 1000000 | tf_op jit(solution)/shard_map/train/pallas_call | solution.py:694
  (41 shorter events, 4.5 us)
Async XLA Ops:
  0.6 1.0 %copy-start = (f32[3,8,32,128]{3,2,1,0:T(8,128)S(1)}, f32[3,8,32,128]{3,2,1,0:T(8,128)}, u32[]{:S(2)}) copy-start(f32[3,8,32,128]{3,2,1,0:T(8,128)} %v_ref.5) | copy-start | bytes 1179652
  1.6 5.1 %collective-permute-start = (f32[3,32,128]{2,1,0:T(8,128)S(1)}, f32[3,32,128]{2,1,0:T(8,128)S(1)}, u32[]{:S(2)}, u32[]{:S(2)}) collective-permute-start(f32[3,32,128]{2,1,0:T(8,128)S(1)} %get-tuple-element.56), channel_id=1, source_target_pairs={{0,32},{32,64},{64,96},{96,128},{128,160},{160,192},{192,224},{224... | collective-permute-start | bytes 147464 | tf_op jit(solution)/shard_map/ppermute | solution.py:62
  1.7 3.1 %copy-start.8 = (bf16[6,256]{1,0:T(8,128)(2,1)S(1)}, bf16[6,256]{1,0:T(8,128)(2,1)}, u32[]{:S(2)}) copy-start(bf16[6,256]{1,0:T(8,128)(2,1)} %param.13) | copy-start | bytes 9220
  1.7 5.0 %collective-permute-start.1 = (f32[3,32,128]{2,1,0:T(8,128)S(1)}, f32[3,32,128]{2,1,0:T(8,128)S(1)}, u32[]{:S(2)}, u32[]{:S(2)}) collective-permute-start(f32[3,32,128]{2,1,0:T(8,128)S(1)} %get-tuple-element.57), channel_id=1, source_target_pairs={{32,0},{64,32},{96,64},{128,96},{160,128},{192,160},{224,192},{0,2... | collective-permute-start | bytes 147464 | tf_op jit(solution)/shard_map/ppermute | solution.py:62
  4.8 0.7 %copy-start.10 = (s32[256]{0:T(256)S(1)}, s32[256]{0:T(256)}, u32[]{:S(2)}) copy-start(s32[256]{0:T(256)} %param.11) | copy-start | bytes 3076
  4.8 0.7 %copy-start.9 = (s32[256,1]{0,1:T(1,128)S(1)}, s32[256,1]{0,1:T(1,128)}, u32[]{:S(2)}) copy-start(s32[256,1]{0,1:T(1,128)} %param.12) | copy-start | bytes 3076
  6.8 7.4 %collective-permute-start.2 = (f32[3,16,128]{2,1,0:T(8,128)S(1)}, f32[3,16,128]{2,1,0:T(8,128)S(1)}, u32[]{:S(2)}, u32[]{:S(2)}) collective-permute-start(f32[3,16,128]{2,1,0:T(8,128)S(1)} %get-tuple-element.59), channel_id=1, source_target_pairs={{0,8},{8,16},{16,24},{24,0},{1,9},{9,17},{17,25},{25,1},{2,10},{10... | collective-permute-start | bytes 73736 | tf_op jit(solution)/shard_map/ppermute | solution.py:62
  10.1 5.4 %collective-permute-start.3 = (f32[3,16,128]{2,1,0:T(8,128)S(1)}, f32[3,16,128]{2,1,0:T(8,128)S(1)}, u32[]{:S(2)}, u32[]{:S(2)}) collective-permute-start(f32[3,16,128]{2,1,0:T(8,128)S(1)} %get-tuple-element.60), channel_id=1, source_target_pairs={{8,0},{16,8},{24,16},{0,24},{9,1},{17,9},{25,17},{1,25},{10,2},{18... | collective-permute-start | bytes 73736 | tf_op jit(solution)/shard_map/ppermute | solution.py:62
  15.6 3.9 %collective-permute-start.4 = (f32[48,128]{1,0:T(8,128)S(1)}, f32[48,128]{1,0:T(8,128)S(1)}, u32[]{:S(2)}, u32[]{:S(2)}) collective-permute-start(f32[48,128]{1,0:T(8,128)S(1)} %get-tuple-element.65), channel_id=1, source_target_pairs={{0,1},{1,2},{2,3},{3,4},{4,5},{5,6},{6,7},{7,0},{8,9},{9,10},{10,1... | collective-permute-start | bytes 73736 | tf_op jit(solution)/shard_map/ppermute | solution.py:62
  17.6 4.7 %collective-permute-start.5 = (f32[48,128]{1,0:T(8,128)S(1)}, f32[48,128]{1,0:T(8,128)S(1)}, u32[]{:S(2)}, u32[]{:S(2)}) collective-permute-start(f32[48,128]{1,0:T(8,128)S(1)} %get-tuple-element.66.after_ref), channel_id=1, source_target_pairs={{1,0},{2,1},{3,2},{4,3},{5,4},{6,5},{7,6},{0,7},{9,8},{10,9},{11,1... | collective-permute-start | bytes 73736 | tf_op jit(solution)/shard_map/ppermute | solution.py:62
  22.3 8.8 %copy-start.2 = (bf16[1,512,512]{2,1,0:T(8,128)(2,1)S(1)}, bf16[1,512,512]{2,1,0:T(8,128)(2,1)}, u32[]{:S(2)}) copy-start(bf16[1,512,512]{2,1,0:T(8,128)(2,1)} %param.15) | copy-start | bytes 1572868
  23.7 7.5 %copy-start.5 = (bf16[1,512,81]{1,2,0:T(8,128)(2,1)S(1)}, bf16[1,512,81]{1,2,0:T(8,128)(2,1)}, u32[]{:S(2)}) copy-start(bf16[1,512,81]{1,2,0:T(8,128)(2,1)} %param.14) | copy-start | bytes 248836
  23.7 7.5 %copy-start.6 = (bf16[1,6,512]{2,1,0:T(8,128)(2,1)S(1)}, bf16[1,6,512]{2,1,0:T(8,128)(2,1)}, u32[]{:S(2)}) copy-start(bf16[1,6,512]{2,1,0:T(8,128)(2,1)} %param.16) | copy-start | bytes 18436
  23.7 18.2 %all-to-all-start = ((bf16[32,16,128]{2,1,0:T(8,128)(2,1)}), bf16[32,16,128]{2,1,0:T(8,128)(2,1)S(1)}, u32[]{:S(2)}, u32[]{:S(2)}) async-start(bf16[32,16,128]{2,1,0:T(8,128)(2,1)} %bitcast.2), calls=%async_computation | async-start | bytes 262144 | tf_op jit(solution)/shard_map/all_to_all | solution.py:757
  31.1 0.7 %copy-start.7 = (f32[1,1030]{1,0:T(1,128)S(1)}, f32[1,1030]{1,0:T(1,128)}, u32[]{:S(2)}) copy-start(f32[1,1030]{1,0:T(1,128)} %biases_ref.1) | copy-start | bytes 12364
  31.8 1.0 %copy-start.1 = (f32[3,8,32,128]{3,2,1,0:T(8,128)S(1)}, f32[3,8,32,128]{3,2,1,0:T(8,128)}, u32[]{:S(2)}) copy-start(f32[3,8,32,128]{3,2,1,0:T(8,128)} %v_ref.5) | copy-start | bytes 1179652
  42.0 6.5 %collective-permute-start.7 = (bf16[96,512]{1,0:T(8,128)(2,1)S(1)}, bf16[96,512]{1,0:T(8,128)(2,1)S(1)}, u32[]{:S(2)}, u32[]{:S(2)}) collective-permute-start(bf16[96,512]{1,0:T(8,128)(2,1)S(1)} %turn.1.refs_0_), channel_id=1, source_target_pairs={{0,4},{1,5},{2,6},{3,7},{4,0},{5,1},{6,2},{7,3},{8,12},{9,13},{10,... | collective-permute-start | bytes 294920 | tf_op jit(solution)/shard_map/ppermute | solution.py:778
  44.8 4.7 %collective-permute-start.6 = (bf16[96,512]{1,0:T(8,128)(2,1)S(1)}, bf16[96,512]{1,0:T(8,128)(2,1)S(1)}, u32[]{:S(2)}, u32[]{:S(2)}) collective-permute-start(bf16[96,512]{1,0:T(8,128)(2,1)S(1)} %turn.1.refs_0_), channel_id=1, source_target_pairs={{0,1},{1,0},{2,3},{3,2},{4,5},{5,4},{6,7},{7,6},{8,9},{9,8},{10,11... | collective-permute-start | bytes 294920 | tf_op jit(solution)/shard_map/ppermute | solution.py:777
  49.5 7.9 %copy-start.3 = (f32[1,32768]{1,0:T(1,128)S(1)}, f32[1,32768]{1,0:T(1,128)}, u32[]{:S(2)}) copy-start(f32[1,32768]{1,0:T(1,128)} %param.19) | copy-start | bytes 393220
  49.5 7.9 %copy-start.4 = (f32[1,32768]{1,0:T(1,128)S(1)}, f32[1,32768]{1,0:T(1,128)}, u32[]{:S(2)}) copy-start(f32[1,32768]{1,0:T(1,128)} %param.18) | copy-start | bytes 393220
  49.5 7.2 %collective-permute-start.9 = (bf16[2,96,512]{2,1,0:T(8,128)(2,1)S(1)}, bf16[2,96,512]{2,1,0:T(8,128)(2,1)S(1)}, u32[]{:S(2)}, u32[]{:S(2)}) collective-permute-start(bf16[2,96,512]{2,1,0:T(8,128)(2,1)S(1)} %pad_maximum_fusion), channel_id=1, source_target_pairs={{0,6},{1,7},{2,4},{3,5},{4,2},{5,3},{6,0},{7,1},{8,14},{9,15},{10,... | collective-permute-start | bytes 589832 | tf_op jit(solution)/shard_map/ppermute | solution.py:784
  51.5 5.9 %collective-permute-start.8 = (bf16[2,96,512]{2,1,0:T(8,128)(2,1)S(1)}, bf16[2,96,512]{2,1,0:T(8,128)(2,1)S(1)}, u32[]{:S(2)}, u32[]{:S(2)}) collective-permute-start(bf16[2,96,512]{2,1,0:T(8,128)(2,1)S(1)} %pad_maximum_fusion), channel_id=1, source_target_pairs={{0,2},{1,3},{2,0},{3,1},{4,6},{5,7},{6,4},{7,5},{8,10},{9,11},{10,... | collective-permute-start | bytes 589832 | tf_op jit(solution)/shard_map/ppermute | solution.py:783
  51.5 4.6 %collective-permute-start.10 = (bf16[96,512]{1,0:T(8,128)(2,1)S(1)}, bf16[96,512]{1,0:T(8,128)(2,1)S(1)}, u32[]{:S(2)}, u32[]{:S(2)}) collective-permute-start(bf16[96,512]{1,0:T(8,128)(2,1)S(1)} %collective-permute-done.7.refs_1_), channel_id=1, source_target_pairs={{0,1},{1,0},{2,3},{3,2},{4,5},{5,4},{6,7},{7,6},{8,9},{9,8},{10,11... | collective-permute-start | bytes 294920 | tf_op jit(solution)/shard_map/ppermute | solution.py:786

commit v4 on v3

--- a/solution.py
+++ b/solution.py
@@ -620,7 +620,6 @@
         delta_three = mismatch * factor
         add(s3, lane_sum(delta_three))
         back_three = jnp.concatenate([delta_three, jnp.zeros_like(delta_three)], axis=0).astype(BF16)
-        add(g3, lax.dot_general(back_three, act_two, NT, preferred_element_type=F32))
         wide_two = act_two.astype(F32)
         delta_two = jnp.dot(w3t_ref[...], back_three, preferred_element_type=F32) * (
             1.0 - wide_two * wide_two
@@ -628,6 +627,7 @@
         add(s2, lane_sum(delta_two))
         back_two = delta_two.astype(BF16)
         back_two_ref[...] = back_two
+        add(g3, lax.dot_general(back_three, act_two, NT, preferred_element_type=F32))
         mine = back_two_ref[pl.ds(own, own_rows), :]
         add(g2, lax.dot_general(mine, act_one, NT, preferred_element_type=F32))
         if last:

time: 65.8 us -> 65.7 us (level)
  transfers between devices with their start and end apart: 12 -> 12, of which waited for: 10 -> 10; matrix products, arithmetic and copies ran while one was open for 0% -> 0% of each run, Pallas kernels for 15% -> 14%
where the time goes in v4:
time: 65.7 us; the launch traced here: 65.4 us
  starting transfers between devices  23.3 us (35%)
  waiting for transfers between devices  19.2 us (29%)
  Pallas kernels  19 us (29%)
  local copies, waits for them, and re-layouts  3.03 us (5%)
  between operations  0.82 us (1%)
    pallas_call x3, Pallas kernels, train(): pl.pallas_call(functools.partial(train_kernel, planes=planes, row_count=r...  12.8 us
    all_to_all x1, waiting for transfers between devices, on_device(): lax.all_to_all(packed.reshape(trainers, capacity, WIDE), ('gy', 'gx'), sp...  7.62 us
    all_to_all x1, starting transfers between devices, on_device(): lax.all_to_all(packed.reshape(trainers, capacity, WIDE), ('gy', 'gx'), sp...  7.42 us
    ppermute x3, starting transfers between devices, exchange(): lax.ppermute(high_face, axis, forward)  5.38 us
    ppermute x3, starting transfers between devices, exchange(): lax.ppermute(low_face, axis, backward)  5.24 us
    ppermute x3, waiting for transfers between devices, exchange(): lax.ppermute(low_face, axis, backward)  4.14 us
    unnamed x22, local copies, waits for them, and re-layouts  2.88 us
    ppermute x1, starting transfers between devices, on_device(): far = lax.ppermute(mine, 'gz', along(lambda x: x + 2))  2.81 us
  transfers between devices with their start and end apart: 12, of which 10 were waited for; matrix products, arithmetic and copies ran while one was open for 0% of the time, Pallas kernels for 14%

profile of v4, /device:TPU:32, one launch (start us, length us, event | category | flops | bytes accessed | tf_op | source)
XLA Modules:
  0.0 65.4 jit_solution(10309552772046469453)
XLA Ops:
  0.6 1.0 %copy-done = f32[3,8,32,128]{3,2,1,0:T(8,128)S(1)} copy-done((f32[3,8,32,128]{3,2,1,0:T(8,128)S(1)}, f32[3,8,32,128]{3,2,1,0:T(8,128)}, u32[]{:S(2)}) %copy-start) | copy-done | bytes 393240
  1.7 2.9 %collective-permute-start.1 = (f32[3,32,128]{2,1,0:T(8,128)S(1)}, f32[3,32,128]{2,1,0:T(8,128)S(1)}, u32[]{:S(2)}, u32[]{:S(2)}) collective-permute-start(f32[3,32,128]{2,1,0:T(8,128)S(1)} %get-tuple-element.57), channel_id=1, source_target_pairs={{32,0},{64,32},{96,64},{128,96},{160,128},{192,160},{224,192},{0,2... | collective-permute-start | bytes 147464 | tf_op jit(solution)/shard_map/ppermute | solution.py:62
  5.5 1.2 %patches.1 = (f32[96,256]{1,0:T(8,128)S(1)}, bf16[128,768]{1,0:T(8,128)(2,1)S(1)}, bf16[96,648]{1,0:T(8,128)(2,1)S(1)}) custom-call(f32[3,8,32,128]{3,2,1,0:T(8,128)S(1)} %copy-done, s32[2,256]{1,0:T(2,128)S(1)} %pad_add_fusion.info_ref), custom_call_target="tpu_custom_call" | custom-call | flops 960000000 | bytes 1000000 | tf_op jit(solution)/shard_map/patches/pallas_call | solution.py:303
  6.8 3.3 %collective-permute-start.2 = (f32[3,16,128]{2,1,0:T(8,128)S(1)}, f32[3,16,128]{2,1,0:T(8,128)S(1)}, u32[]{:S(2)}, u32[]{:S(2)}) collective-permute-start(f32[3,16,128]{2,1,0:T(8,128)S(1)} %get-tuple-element.59), channel_id=1, source_target_pairs={{0,8},{8,16},{16,24},{24,0},{1,9},{9,17},{17,25},{25,1},{2,10},{10... | collective-permute-start | bytes 73736 | tf_op jit(solution)/shard_map/ppermute | solution.py:62
  10.1 2.2 %collective-permute-start.3 = (f32[3,16,128]{2,1,0:T(8,128)S(1)}, f32[3,16,128]{2,1,0:T(8,128)S(1)}, u32[]{:S(2)}, u32[]{:S(2)}) collective-permute-start(f32[3,16,128]{2,1,0:T(8,128)S(1)} %get-tuple-element.60), channel_id=1, source_target_pairs={{8,0},{16,8},{24,16},{0,24},{9,1},{17,9},{25,17},{1,25},{10,2},{18... | collective-permute-start | bytes 73736 | tf_op jit(solution)/shard_map/ppermute | solution.py:62
  12.3 1.1 %plan.1 = (f32[48,128]{1,0:T(8,128)S(1)}, f32[48,128]{1,0:T(8,128)S(1)}, bf16[512,256]{1,0:T(8,128)(2,1)S(1)}, f32[96,256]{1,0:T(8,128)S(1)}) custom-call(f32[3,8,32,128]{3,2,1,0:T(8,128)S(1)} %copy-done, f32[3,32,128]{2,1,0:T(8,128)S(1)} %collective-permute-done.xlo_ref, f32[3,32,128]{2,1,0:T(8,128)S(1)} %collective-permute-done.1.xhi_ref, ...), custom_call_target="tpu_custom_call" | custom-call | flops 1200000000 | bytes 1000000 | tf_op jit(solution)/shard_map/plan/pallas_call | solution.py:202
  13.4 0.8 %collective-permute-done.2.ylo_ref = f32[3,16,128]{2,1,0:T(8,128)S(1)} collective-permute-done((f32[3,16,128]{2,1,0:T(8,128)S(1)}, f32[3,16,128]{2,1,0:T(8,128)S(1)}, u32[]{:S(2)}, u32[]{:S(2)}) %collective-permute-start.2) | collective-permute-done | bytes 24608 | tf_op jit(solution)/shard_map/ppermute | solution.py:62
  14.2 1.3 %collective-permute-done.3.yhi_ref = f32[3,16,128]{2,1,0:T(8,128)S(1)} collective-permute-done((f32[3,16,128]{2,1,0:T(8,128)S(1)}, f32[3,16,128]{2,1,0:T(8,128)S(1)}, u32[]{:S(2)}, u32[]{:S(2)}) %collective-permute-start.3) | collective-permute-done | bytes 24608 | tf_op jit(solution)/shard_map/ppermute | solution.py:62
  15.6 2.0 %collective-permute-start.4 = (f32[48,128]{1,0:T(8,128)S(1)}, f32[48,128]{1,0:T(8,128)S(1)}, u32[]{:S(2)}, u32[]{:S(2)}) collective-permute-start(f32[48,128]{1,0:T(8,128)S(1)} %get-tuple-element.65), channel_id=1, source_target_pairs={{0,1},{1,2},{2,3},{3,4},{4,5},{5,6},{6,7},{7,0},{8,9},{9,10},{10,1... | collective-permute-start | bytes 73736 | tf_op jit(solution)/shard_map/ppermute | solution.py:62
  18.1 1.4 %collective-permute-done.4.zlo_ref = f32[48,128]{1,0:T(8,128)S(1)} collective-permute-done((f32[48,128]{1,0:T(8,128)S(1)}, f32[48,128]{1,0:T(8,128)S(1)}, u32[]{:S(2)}, u32[]{:S(2)}) %collective-permute-start.4) | collective-permute-done | bytes 24608 | tf_op jit(solution)/shard_map/ppermute | solution.py:62
  19.5 2.8 %collective-permute-done.5.zhi_ref = f32[48,128]{1,0:T(8,128)S(1)} collective-permute-done((f32[48,128]{1,0:T(8,128)S(1)}, f32[48,128]{1,0:T(8,128)S(1)}, u32[]{:S(2)}, u32[]{:S(2)}) %collective-permute-start.5) | collective-permute-done | bytes 24608 | tf_op jit(solution)/shard_map/ppermute | solution.py:62
  22.4 1.3 %pack.1 = bf16[512,128]{1,0:T(8,128)(2,1)} custom-call(f32[96,256]{1,0:T(8,128)S(1)} %get-tuple-element.69.own_ref, f32[48,128]{1,0:T(8,128)S(1)} %collective-permute-done.4.zlo_ref, f32[48,128]{1,0:T(8,128)S(1)} %collective-permute-done.5.zhi_ref, s32[2,256]{1,0:T(2,128)S(1)} %pad_add_fusion.info_ref, bf16[128,768]{1,0:T(8,128)(2,1)S(1)} %get-tuple-element.70.rows_ref, ...), custom_call_target="tpu_custom_call" | custom-call | flops 560000000 | bytes 1000000 | tf_op jit(solution)/shard_map/pack/pallas_call | solution.py:406
  23.7 7.4 %all-to-all-start = ((bf16[32,16,128]{2,1,0:T(8,128)(2,1)}), bf16[32,16,128]{2,1,0:T(8,128)(2,1)S(1)}, u32[]{:S(2)}, u32[]{:S(2)}) async-start(bf16[32,16,128]{2,1,0:T(8,128)(2,1)} %bitcast.2), calls=%async_computation | async-start | bytes 262144 | tf_op jit(solution)/shard_map/all_to_all | solution.py:757
  32.8 1.4 %advance.1 = (f32[3,8,32,128]{3,2,1,0:T(8,128)}, f32[8,128]{1,0:T(8,128)S(1)}) custom-call(f32[3,8,32,128]{3,2,1,0:T(8,128)S(1)} %copy-done.1, f32[3,32,128]{2,1,0:T(8,128)S(1)} %collective-permute-done.xlo_ref, f32[3,32,128]{2,1,0:T(8,128)S(1)} %collective-permute-done.1.xhi_ref, f32[3,16,128]{2,1,0:T(8,128)S(1)} %collective-permute-done.2.ylo_ref, ...), custom_call_target="tpu_custom_call" | custom-call | flops 1200000000 | bytes 1000000 | tf_op jit(solution)/shard_map/advance/pallas_call | solution.py:476
  34.2 7.6 %all-to-all-done = bf16[32,16,128]{2,1,0:T(8,128)(2,1)S(1)} async-done(((bf16[32,16,128]{2,1,0:T(8,128)(2,1)}), bf16[32,16,128]{2,1,0:T(8,128)(2,1)S(1)}, u32[]{:S(2)}, u32[]{:S(2)}) %all-to-all-start) | async-done | bytes 131104 | tf_op jit(solution)/shard_map/all_to_all | solution.py:757
  42.0 2.8 %collective-permute-start.7 = (bf16[96,512]{1,0:T(8,128)(2,1)S(1)}, bf16[96,512]{1,0:T(8,128)(2,1)S(1)}, u32[]{:S(2)}, u32[]{:S(2)}) collective-permute-start(bf16[96,512]{1,0:T(8,128)(2,1)S(1)} %turn.1.refs_0_), channel_id=1, source_target_pairs={{0,4},{1,5},{2,6},{3,7},{4,0},{5,1},{6,2},{7,3},{8,12},{9,13},{10,... | collective-permute-start | bytes 294920 | tf_op jit(solution)/shard_map/ppermute | solution.py:778
  45.1 1.9 %train.3 = (f32[512,96]{1,0:T(8,128)S(1)}, f32[64,512]{1,0:T(8,128)S(1)}, f32[16,512]{1,0:T(8,128)S(1)}, f32[512,128]{1,0:T(8,128)S(1)}, f32[512,128]{1,0:T(8,12...) custom-call(bf16[96,512]{1,0:T(8,128)(2,1)S(1)} %turn.1.refs_0_, ...), custom_call_target="tpu_custom_call" | custom-call | flops 1280000000 | bytes 1000000 | tf_op jit(solution)/shard_map/train/pallas_call | solution.py:694
  47.0 1.6 %collective-permute-done.7.refs_1_ = bf16[96,512]{1,0:T(8,128)(2,1)S(1)} collective-permute-done((bf16[96,512]{1,0:T(8,128)(2,1)S(1)}, bf16[96,512]{1,0:T(8,128)(2,1)S(1)}, u32[]{:S(2)}, u32[]{:S(2)}) %collective-permute-start.7) | collective-permute-done | bytes 98336 | tf_op jit(solution)/shard_map/ppermute | solution.py:778
  48.5 0.9 %collective-permute-done.6.refs_0_ = bf16[96,512]{1,0:T(8,128)(2,1)S(1)} collective-permute-done((bf16[96,512]{1,0:T(8,128)(2,1)S(1)}, bf16[96,512]{1,0:T(8,128)(2,1)S(1)}, u32[]{:S(2)}, u32[]{:S(2)}) %collective-permute-start.6) | collective-permute-done | bytes 98336 | tf_op jit(solution)/shard_map/ppermute | solution.py:777
  49.5 2.0 %collective-permute-start.9 = (bf16[2,96,512]{2,1,0:T(8,128)(2,1)S(1)}, bf16[2,96,512]{2,1,0:T(8,128)(2,1)S(1)}, u32[]{:S(2)}, u32[]{:S(2)}) collective-permute-start(bf16[2,96,512]{2,1,0:T(8,128)(2,1)S(1)} %pad_maximum_fusion), channel_id=1, source_target_pairs={{0,6},{1,7},{2,4},{3,5},{4,2},{5,3},{6,0},{7,1},{8,14},{9,15},{10,... | collective-permute-start | bytes 589832 | tf_op jit(solution)/shard_map/ppermute | solution.py:784
  51.7 2.9 %train.4 = (f32[512,96]{1,0:T(8,128)S(1)}, f32[64,512]{1,0:T(8,128)S(1)}, f32[16,512]{1,0:T(8,128)S(1)}, f32[512,128]{1,0:T(8,128)S(1)}, f32[512,128]{1,0:T(8,128)S(1)}, /*index=5*/f32[8,128]{1,0:T(8,128)S(1)}) custom-call(bf16[96,512]{1,0:T(8,128)(2,1)S(1)} %collective-permute-done.6.refs_0_, bf16[96,512]{1,0:T(8,128)(2,1)S(1)} %collective-permute-done.7.refs_1_, ...), custom_call_target="tpu_custom_call" | custom-call | flops 2560000000 | bytes 1000000 | tf_op jit(solution)/shard_map/train/pallas_call | solution.py:694
  54.6 1.5 %collective-permute-done.10.refs_2_ = bf16[96,512]{1,0:T(8,128)(2,1)S(1)} collective-permute-done((bf16[96,512]{1,0:T(8,128)(2,1)S(1)}, bf16[96,512]{1,0:T(8,128)(2,1)S(1)}, u32[]{:S(2)}, u32[]{:S(2)}) %collective-permute-start.10) | collective-permute-done | bytes 98336 | tf_op jit(solution)/shard_map/ppermute | solution.py:786
  56.7 0.7 %collective-permute-done.8.refs_0_ = bf16[2,96,512]{2,1,0:T(8,128)(2,1)S(1)} collective-permute-done((bf16[2,96,512]{2,1,0:T(8,128)(2,1)S(1)}, bf16[2,96,512]{2,1,0:T(8,128)(2,1)S(1)}, u32[]{:S(2)}, u32[]{:S(2)}) %collective-permute-start.8) | collective-permute-done | bytes 196640 | tf_op jit(solution)/shard_map/ppermute | solution.py:783
  57.4 8.0 %train.5 = (f32[81,1,512]{2,1,0:T(1,128)}, f32[6,1,512]{2,1,0:T(1,128)}, f32[1,1030]{1,0:T(1,128)}, f32[256,128]{1,0:T(8,128)}, f32[256,128]{1,0:T(8,128)}) custom-call(bf16[2,96,512]{2,1,0:T(8,128)(2,1)S(1)} %collective-permute-done.8.refs_0_, bf16[2,96,512]{2,1,0:T(8,128)(2,1)S(1)} %collective-permute-done.9.refs_1_, ...), custom_call_target="tpu_custom_call" | custom-call | flops 6400000000 | bytes 1000000 | tf_op jit(solution)/shard_map/train/pallas_call | solution.py:694
  (41 shorter events, 4.5 us)
Async XLA Ops:
  0.6 1.0 %copy-start = (f32[3,8,32,128]{3,2,1,0:T(8,128)S(1)}, f32[3,8,32,128]{3,2,1,0:T(8,128)}, u32[]{:S(2)}) copy-start(f32[3,8,32,128]{3,2,1,0:T(8,128)} %v_ref.5) | copy-start | bytes 1179652
  1.6 5.1 %collective-permute-start = (f32[3,32,128]{2,1,0:T(8,128)S(1)}, f32[3,32,128]{2,1,0:T(8,128)S(1)}, u32[]{:S(2)}, u32[]{:S(2)}) collective-permute-start(f32[3,32,128]{2,1,0:T(8,128)S(1)} %get-tuple-element.56), channel_id=1, source_target_pairs={{0,32},{32,64},{64,96},{96,128},{128,160},{160,192},{192,224},{224... | collective-permute-start | bytes 147464 | tf_op jit(solution)/shard_map/ppermute | solution.py:62
  1.7 3.1 %copy-start.8 = (bf16[6,256]{1,0:T(8,128)(2,1)S(1)}, bf16[6,256]{1,0:T(8,128)(2,1)}, u32[]{:S(2)}) copy-start(bf16[6,256]{1,0:T(8,128)(2,1)} %param.13) | copy-start | bytes 9220
  1.7 5.0 %collective-permute-start.1 = (f32[3,32,128]{2,1,0:T(8,128)S(1)}, f32[3,32,128]{2,1,0:T(8,128)S(1)}, u32[]{:S(2)}, u32[]{:S(2)}) collective-permute-start(f32[3,32,128]{2,1,0:T(8,128)S(1)} %get-tuple-element.57), channel_id=1, source_target_pairs={{32,0},{64,32},{96,64},{128,96},{160,128},{192,160},{224,192},{0,2... | collective-permute-start | bytes 147464 | tf_op jit(solution)/shard_map/ppermute | solution.py:62
  4.8 0.7 %copy-start.10 = (s32[256]{0:T(256)S(1)}, s32[256]{0:T(256)}, u32[]{:S(2)}) copy-start(s32[256]{0:T(256)} %param.11) | copy-start | bytes 3076
  4.8 0.7 %copy-start.9 = (s32[256,1]{0,1:T(1,128)S(1)}, s32[256,1]{0,1:T(1,128)}, u32[]{:S(2)}) copy-start(s32[256,1]{0,1:T(1,128)} %param.12) | copy-start | bytes 3076
  6.8 7.4 %collective-permute-start.2 = (f32[3,16,128]{2,1,0:T(8,128)S(1)}, f32[3,16,128]{2,1,0:T(8,128)S(1)}, u32[]{:S(2)}, u32[]{:S(2)}) collective-permute-start(f32[3,16,128]{2,1,0:T(8,128)S(1)} %get-tuple-element.59), channel_id=1, source_target_pairs={{0,8},{8,16},{16,24},{24,0},{1,9},{9,17},{17,25},{25,1},{2,10},{10... | collective-permute-start | bytes 73736 | tf_op jit(solution)/shard_map/ppermute | solution.py:62
  10.1 5.4 %collective-permute-start.3 = (f32[3,16,128]{2,1,0:T(8,128)S(1)}, f32[3,16,128]{2,1,0:T(8,128)S(1)}, u32[]{:S(2)}, u32[]{:S(2)}) collective-permute-start(f32[3,16,128]{2,1,0:T(8,128)S(1)} %get-tuple-element.60), channel_id=1, source_target_pairs={{8,0},{16,8},{24,16},{0,24},{9,1},{17,9},{25,17},{1,25},{10,2},{18... | collective-permute-start | bytes 73736 | tf_op jit(solution)/shard_map/ppermute | solution.py:62
  15.6 3.9 %collective-permute-start.4 = (f32[48,128]{1,0:T(8,128)S(1)}, f32[48,128]{1,0:T(8,128)S(1)}, u32[]{:S(2)}, u32[]{:S(2)}) collective-permute-start(f32[48,128]{1,0:T(8,128)S(1)} %get-tuple-element.65), channel_id=1, source_target_pairs={{0,1},{1,2},{2,3},{3,4},{4,5},{5,6},{6,7},{7,0},{8,9},{9,10},{10,1... | collective-permute-start | bytes 73736 | tf_op jit(solution)/shard_map/ppermute | solution.py:62
  17.6 4.7 %collective-permute-start.5 = (f32[48,128]{1,0:T(8,128)S(1)}, f32[48,128]{1,0:T(8,128)S(1)}, u32[]{:S(2)}, u32[]{:S(2)}) collective-permute-start(f32[48,128]{1,0:T(8,128)S(1)} %get-tuple-element.66.after_ref), channel_id=1, source_target_pairs={{1,0},{2,1},{3,2},{4,3},{5,4},{6,5},{7,6},{0,7},{9,8},{10,9},{11,1... | collective-permute-start | bytes 73736 | tf_op jit(solution)/shard_map/ppermute | solution.py:62
  22.3 8.8 %copy-start.2 = (bf16[1,512,512]{2,1,0:T(8,128)(2,1)S(1)}, bf16[1,512,512]{2,1,0:T(8,128)(2,1)}, u32[]{:S(2)}) copy-start(bf16[1,512,512]{2,1,0:T(8,128)(2,1)} %param.15) | copy-start | bytes 1572868
  23.7 7.5 %copy-start.5 = (bf16[1,512,81]{1,2,0:T(8,128)(2,1)S(1)}, bf16[1,512,81]{1,2,0:T(8,128)(2,1)}, u32[]{:S(2)}) copy-start(bf16[1,512,81]{1,2,0:T(8,128)(2,1)} %param.14) | copy-start | bytes 248836
  23.7 7.5 %copy-start.6 = (bf16[1,6,512]{2,1,0:T(8,128)(2,1)S(1)}, bf16[1,6,512]{2,1,0:T(8,128)(2,1)}, u32[]{:S(2)}) copy-start(bf16[1,6,512]{2,1,0:T(8,128)(2,1)} %param.16) | copy-start | bytes 18436
  23.7 18.2 %all-to-all-start = ((bf16[32,16,128]{2,1,0:T(8,128)(2,1)}), bf16[32,16,128]{2,1,0:T(8,128)(2,1)S(1)}, u32[]{:S(2)}, u32[]{:S(2)}) async-start(bf16[32,16,128]{2,1,0:T(8,128)(2,1)} %bitcast.2), calls=%async_computation | async-start | bytes 262144 | tf_op jit(solution)/shard_map/all_to_all | solution.py:757
  31.1 0.7 %copy-start.7 = (f32[1,1030]{1,0:T(1,128)S(1)}, f32[1,1030]{1,0:T(1,128)}, u32[]{:S(2)}) copy-start(f32[1,1030]{1,0:T(1,128)} %biases_ref.1) | copy-start | bytes 12364
  31.8 1.0 %copy-start.1 = (f32[3,8,32,128]{3,2,1,0:T(8,128)S(1)}, f32[3,8,32,128]{3,2,1,0:T(8,128)}, u32[]{:S(2)}) copy-start(f32[3,8,32,128]{3,2,1,0:T(8,128)} %v_ref.5) | copy-start | bytes 1179652
  42.0 6.5 %collective-permute-start.7 = (bf16[96,512]{1,0:T(8,128)(2,1)S(1)}, bf16[96,512]{1,0:T(8,128)(2,1)S(1)}, u32[]{:S(2)}, u32[]{:S(2)}) collective-permute-start(bf16[96,512]{1,0:T(8,128)(2,1)S(1)} %turn.1.refs_0_), channel_id=1, source_target_pairs={{0,4},{1,5},{2,6},{3,7},{4,0},{5,1},{6,2},{7,3},{8,12},{9,13},{10,... | collective-permute-start | bytes 294920 | tf_op jit(solution)/shard_map/ppermute | solution.py:778
  44.8 4.7 %collective-permute-start.6 = (bf16[96,512]{1,0:T(8,128)(2,1)S(1)}, bf16[96,512]{1,0:T(8,128)(2,1)S(1)}, u32[]{:S(2)}, u32[]{:S(2)}) collective-permute-start(bf16[96,512]{1,0:T(8,128)(2,1)S(1)} %turn.1.refs_0_), channel_id=1, source_target_pairs={{0,1},{1,0},{2,3},{3,2},{4,5},{5,4},{6,7},{7,6},{8,9},{9,8},{10,11... | collective-permute-start | bytes 294920 | tf_op jit(solution)/shard_map/ppermute | solution.py:777
  49.5 7.9 %copy-start.3 = (f32[1,32768]{1,0:T(1,128)S(1)}, f32[1,32768]{1,0:T(1,128)}, u32[]{:S(2)}) copy-start(f32[1,32768]{1,0:T(1,128)} %param.19) | copy-start | bytes 393220
  49.5 7.9 %copy-start.4 = (f32[1,32768]{1,0:T(1,128)S(1)}, f32[1,32768]{1,0:T(1,128)}, u32[]{:S(2)}) copy-start(f32[1,32768]{1,0:T(1,128)} %param.18) | copy-start | bytes 393220
  49.5 7.2 %collective-permute-start.9 = (bf16[2,96,512]{2,1,0:T(8,128)(2,1)S(1)}, bf16[2,96,512]{2,1,0:T(8,128)(2,1)S(1)}, u32[]{:S(2)}, u32[]{:S(2)}) collective-permute-start(bf16[2,96,512]{2,1,0:T(8,128)(2,1)S(1)} %pad_maximum_fusion), channel_id=1, source_target_pairs={{0,6},{1,7},{2,4},{3,5},{4,2},{5,3},{6,0},{7,1},{8,14},{9,15},{10,... | collective-permute-start | bytes 589832 | tf_op jit(solution)/shard_map/ppermute | solution.py:784
  51.5 5.9 %collective-permute-start.8 = (bf16[2,96,512]{2,1,0:T(8,128)(2,1)S(1)}, bf16[2,96,512]{2,1,0:T(8,128)(2,1)S(1)}, u32[]{:S(2)}, u32[]{:S(2)}) collective-permute-start(bf16[2,96,512]{2,1,0:T(8,128)(2,1)S(1)} %pad_maximum_fusion), channel_id=1, source_target_pairs={{0,2},{1,3},{2,0},{3,1},{4,6},{5,7},{6,4},{7,5},{8,10},{9,11},{10,... | collective-permute-start | bytes 589832 | tf_op jit(solution)/shard_map/ppermute | solution.py:783
  51.5 4.6 %collective-permute-start.10 = (bf16[96,512]{1,0:T(8,128)(2,1)S(1)}, bf16[96,512]{1,0:T(8,128)(2,1)S(1)}, u32[]{:S(2)}, u32[]{:S(2)}) collective-permute-start(bf16[96,512]{1,0:T(8,128)(2,1)S(1)} %collective-permute-done.7.refs_1_), channel_id=1, source_target_pairs={{0,1},{1,0},{2,3},{3,2},{4,5},{5,4},{6,7},{7,6},{8,9},{9,8},{10,11... | collective-permute-start | bytes 294920 | tf_op jit(solution)/shard_map/ppermute | solution.py:786
